TPU v7x, 512 devices: a whole 4x4x16 slice. The times are simulated.
512 devices in a mesh: grp: 16 (over x, y), pb: 4 (over z_hi), ka: 8 (over z_lo, core).
Axes of the slice: x: 4, y: 4, z: 16 (z_hi: 4, z_lo: 4; z = z_hi * 4 + z_lo), core: 2. Of those that a mesh axis runs over, the one named last changes fastest.
Arguments:
- lengths: int32 [16], P('grp'), may hold values from 64 to 256, as said below
- single: bfloat16 [16, 8, 256, 768], P('grp', None, ('pb', 'ka')), may hold values from -6 to 6
- attn_gain: float32 [768], replicated, may hold values from 0.25 to 1.75
- w_query: bfloat16 [768, 768], P(('grp', 'pb')), may hold values from -0.21875 to 0.21875
- w_key: bfloat16 [768, 768], P(('grp', 'pb')), may hold values from -0.21875 to 0.21875
- w_value: bfloat16 [768, 768], P(('grp', 'pb')), may hold values from -0.21875 to 0.21875
- w_gate: bfloat16 [768, 768], P(('grp', 'pb')), may hold values from -0.21875 to 0.21875
- w_out: bfloat16 [768, 768], P(('grp', 'pb'), 'ka'), may hold values from -0.21875 to 0.21875
- pair_rep: bfloat16 [16, 256, 4, 64, 128], P('grp', 'pb', None, 'ka'), may hold values from -16 to 16
- pair_gain: float32 [128], replicated, may hold values from 0.25 to 1.75
- pair_proj: float32 [128, 16], replicated, may hold values from -3 to 3
- trans_gain: float32 [768], replicated, may hold values from 0.25 to 1.75
- w_swish: bfloat16 [768, 1536], P(('grp', 'pb'), 'ka'), may hold values from -0.21875 to 0.21875
- w_up: bfloat16 [768, 1536], P(('grp', 'pb'), 'ka'), may hold values from -0.21875 to 0.21875
- w_down: bfloat16 [1536, 768], P('ka', ('grp', 'pb')), may hold values from -0.15625 to 0.15625
Outputs:
- updated: bfloat16 [16, 8, 256, 768], P('grp', None, ('pb', 'ka'))
Inputs may be any that keep to these rules, and one draw needn't show every extreme that they name: `lengths`: tokens of a complex; positions from it on are padding; some complex has exactly 256 tokens.
All inputs are finite; a program needn't handle non-finite values.
Results may differ from a plain program's by a relative error of at most 0.014.
Values may be sent and summed in bfloat16 or wider, within the bound.
No kernel may reach another device: no remote copies, remote signals or barrier semaphores. Data moves between devices by JAX's collectives and lax.ppermute only.
A program may use at most 192 MiB of HBM per device.

v0:
```python
import math

import jax
import jax.numpy as jnp
from jax import lax
from jax.sharding import PartitionSpec as P

HEADS = 16


epsilon = 1e-05
very_negative = -1e30


def layer_norm(inputs, scale_gain):
    mean_val = jnp.mean(inputs, axis=-1, keepdims=True)
    centred = inputs - mean_val
    spread = jnp.mean(centred * centred, axis=-1, keepdims=True)
    return centred * lax.rsqrt(spread + epsilon) * scale_gain


def project(inputs, weight):
    return jnp.dot(inputs, weight, preferred_element_type=jnp.float32)


def on_device(
    lengths,
    single,
    attn_gain,
    w_query,
    w_key,
    w_value,
    w_gate,
    w_out,
    pair_rep,
    pair_gain,
    pair_proj,
    trans_gain,
    w_swish,
    w_up,
    w_down,
):
    w_query, w_key, w_value, w_gate, w_out, w_swish, w_up, w_down = (
        lax.all_gather(w_query, ("grp", "pb"), axis=0, tiled=True),
        lax.all_gather(w_key, ("grp", "pb"), axis=0, tiled=True),
        lax.all_gather(w_value, ("grp", "pb"), axis=0, tiled=True),
        lax.all_gather(w_gate, ("grp", "pb"), axis=0, tiled=True),
        lax.all_gather(w_out, ("grp", "pb"), axis=0, tiled=True),
        lax.all_gather(w_swish, ("grp", "pb"), axis=0, tiled=True),
        lax.all_gather(w_up, ("grp", "pb"), axis=0, tiled=True),
        lax.all_gather(w_down, ("grp", "pb"), axis=1, tiled=True),
    )
    own_rows = single[0]
    samples, row_count, model_width = own_rows.shape
    head_dim = model_width // HEADS
    pb_count = lax.axis_size("pb")
    ka_count = lax.axis_size("ka")
    block_rows = row_count * ka_count
    key_count = row_count * pb_count
    ka_index = lax.axis_index("ka")
    normed = (
        layer_norm(own_rows.astype(jnp.float32), attn_gain)
        .astype(jnp.bfloat16)
        .reshape(samples * row_count, model_width)
    )
    key_proj = project(normed, w_key).astype(jnp.bfloat16).reshape(samples, row_count, model_width)
    value_proj = (
        project(normed, w_value).astype(jnp.bfloat16).reshape(samples, row_count, model_width)
    )
    key_proj, value_proj = (
        lax.all_gather(key_proj, "pb", axis=1, tiled=True),
        lax.all_gather(value_proj, "pb", axis=1, tiled=True),
    )
    block_single = lax.all_gather(own_rows, "ka", axis=1, tiled=True)
    block_normed = (
        layer_norm(block_single.astype(jnp.float32), attn_gain)
        .astype(jnp.bfloat16)
        .reshape(samples * block_rows, model_width)
    )
    queries = (
        project(block_normed, w_query)
        .astype(jnp.bfloat16)
        .reshape(samples, block_rows, model_width)
    )
    gate_vals = (
        jax.nn.sigmoid(project(block_normed, w_gate))
        .astype(jnp.bfloat16)
        .reshape(samples, block_rows, model_width)
    )
    pair_tile = pair_rep[0].astype(jnp.float32)
    pair_bias = jnp.einsum(
        "qbrc,ch->qhbr",
        layer_norm(pair_tile, pair_gain),
        pair_proj,
        precision=lax.Precision.HIGHEST,
    ).reshape(block_rows, HEADS, key_count)
    key_pos = (
        lax.broadcasted_iota(jnp.int32, (pb_count, row_count), 0) * block_rows
        + ka_index * row_count
        + lax.broadcasted_iota(jnp.int32, (pb_count, row_count), 1)
    ).reshape(key_count)
    key_live = key_pos < lengths[0]
    query_heads = queries.reshape(samples, block_rows, HEADS, head_dim)
    key_heads = key_proj.reshape(samples, key_count, HEADS, head_dim)
    scores = jnp.einsum(
        "sqhd,skhd->qshk", query_heads, key_heads, preferred_element_type=jnp.float32
    ) / math.sqrt(head_dim)
    scores = jnp.where(key_live, scores + pair_bias[:, None], very_negative)
    peaks = jnp.max(scores, axis=-1)
    soft_weights = jnp.exp(scores - peaks[..., None])
    totals = jnp.sum(soft_weights, axis=-1)
    value_heads = value_proj.reshape(samples, key_count, HEADS, head_dim).astype(jnp.float32)
    weighted = jnp.einsum(
        "qshk,skhd->qshd", soft_weights, value_heads, precision=lax.Precision.HIGHEST
    )
    peaks, totals, weighted = (
        lax.all_to_all(peaks[None], "ka", split_axis=1, concat_axis=0, tiled=True),
        lax.all_to_all(totals[None], "ka", split_axis=1, concat_axis=0, tiled=True),
        lax.all_to_all(weighted[None], "ka", split_axis=1, concat_axis=0, tiled=True),
    )
    top_peak = jnp.max(peaks, axis=0)
    rescale = jnp.exp(peaks - top_peak)
    attended = (
        jnp.sum(weighted * rescale[..., None], axis=0)
        / jnp.sum(totals * rescale, axis=0)[..., None]
    )
    attended = attended.reshape(row_count, samples, model_width)
    own_gates = (
        lax.dynamic_slice_in_dim(gate_vals, ka_index * row_count, row_count, 1)
        .transpose(1, 0, 2)
        .astype(jnp.float32)
    )
    own_gated = (attended * own_gates).astype(jnp.bfloat16)
    gated_out = lax.all_gather(own_gated, "ka", axis=0, tiled=True)
    col_count = w_out.shape[1]
    residual = lax.dynamic_slice_in_dim(block_single, ka_index * col_count, col_count, 2).transpose(
        1, 0, 2
    )
    mixed_cols = (
        residual.astype(jnp.float32)
        + project(gated_out.reshape(block_rows * samples, model_width), w_out).reshape(
            block_rows, samples, col_count
        )
    ).astype(jnp.bfloat16)
    mixed_rows = lax.all_gather(mixed_cols, "ka", axis=2, tiled=True)
    normed_t = layer_norm(mixed_rows.astype(jnp.float32), trans_gain).astype(jnp.bfloat16)
    count = lax.axis_size("ka") * row_count
    row_part = normed_t.reshape(count * samples, model_width)
    hidden = (jax.nn.silu(project(row_part, w_swish)) * project(row_part, w_up)).astype(
        jnp.bfloat16
    )
    update = lax.psum_scatter(
        project(hidden, w_down).reshape(count, samples, model_width).astype(jnp.bfloat16),
        "ka",
        scatter_dimension=0,
        tiled=True,
    ).astype(jnp.float32)
    own_mixed = lax.dynamic_slice_in_dim(mixed_rows, ka_index * row_count, row_count, 0)
    result = (own_mixed.astype(jnp.float32) + update).astype(jnp.bfloat16)
    return result.transpose(1, 0, 2)[None]


def solution(mesh):
    return jax.shard_map(
        on_device,
        mesh=mesh,
        in_specs=(
            P("grp"),
            P("grp", None, ("pb", "ka"), None),
            P(),
            P(("grp", "pb"), None),
            P(("grp", "pb"), None),
            P(("grp", "pb"), None),
            P(("grp", "pb"), None),
            P(("grp", "pb"), "ka"),
            P("grp", "pb", None, "ka", None),
            P(),
            P(),
            P(),
            P(("grp", "pb"), "ka"),
            P(("grp", "pb"), "ka"),
            P("ka", ("grp", "pb")),
        ),
        out_specs=P("grp", None, ("pb", "ka"), None),
        check_vma=False,
    )
```

profile of v0, /device:TPU:1, one launch (start us, length us, event | category | flops | bytes accessed | tf_op | source)
XLA Modules:
  0.0 1403.0 jit_solution(1153973695589729702)
XLA Ops:
  10.7 22.5 %all-gather = bf16[1,8,64,768]{3,1,0,2:T(8,128)(2,1)S(1)} all-gather(bf16[1,8,8,768]{3,1,0,2:T(8,128)(2,1)S(1)} %copy.85), channel_id=2, replica_groups=mesh['grp'=16,'pb'=4,'ka'=8] {'ka'}, dimensions={2}, use_global_device_ids=true | all-gather | bytes 884736 | tf_op jit(solution)/shard_map/all_gather | solution.py:74
  41.1 83.3 %all-gather.18.cloned.1.call-done = bf16[64,12,768]{2,1,0:T(8,128)(2,1)} async-done(((bf16[1,12,768]{2,1,0:T(8,128)(2,1)}), bf16[64,12,768]{2,1,0:T(8,128)(2,1)}) %all-gather.18.cloned.1.call-update) | async-done | bytes 1179664 | tf_op jit(solution)/shard_map/all_gather | solution.py:44
  124.5 2.2 reshape.151
  127.5 3.5 reshape.164
  131.1 99.5 %all-gather.16.cloned.1.call-done = bf16[64,12,768]{2,1,0:T(8,128)(2,1)} async-done(((bf16[1,12,768]{2,1,0:T(8,128)(2,1)}), bf16[64,12,768]{2,1,0:T(8,128)(2,1)}) %all-gather.16.cloned.1.call-update) | async-done | bytes 1179664 | tf_op jit(solution)/shard_map/all_gather | solution.py:45
  230.5 2.2 reshape.149
  233.2 18.8 %all_gather.43 = bf16[8,32,768]{2,1,0:T(8,128)(2,1)S(1)} all-gather(bf16[8,8,768]{2,1,0:T(8,128)(2,1)S(1)} %fusion.21), channel_id=1, replica_groups=mesh['grp'=16,'pb'=4,'ka'=8] {'pb'}, dimensions={1}, use_global_device_ids=true | all-gather | bytes 491520 | tf_op jit(solution)/shard_map/all_gather | solution.py:71
  252.0 2.2 reshape.136
  254.2 3.1 fusion.59
  258.9 6.7 all-to-all-start.2
  266.5 70.1 %all-gather.14.cloned.1.call-done = bf16[64,12,768]{2,1,0:T(8,128)(2,1)} async-done(((bf16[1,12,768]{2,1,0:T(8,128)(2,1)}), bf16[64,12,768]{2,1,0:T(8,128)(2,1)}) %all-gather.14.cloned.1.call-update) | async-done | bytes 1179664 | tf_op jit(solution)/shard_map/all_gather | solution.py:46
  336.7 3.1 reshape.147
  341.4 19.0 %all_gather.41 = bf16[8,32,768]{2,1,0:T(8,128)(2,1)S(1)} all-gather(bf16[8,8,768]{2,1,0:T(8,128)(2,1)S(1)} %fusion.20), channel_id=1, replica_groups=mesh['grp'=16,'pb'=4,'ka'=8] {'pb'}, dimensions={1}, use_global_device_ids=true | all-gather | bytes 491520 | tf_op jit(solution)/shard_map/all_gather | solution.py:72
  360.4 2.2 reshape.134
  362.6 6.7 all-to-all-start.1
  369.3 4.9 convolution_bitcast_fusion
  374.2 5.2 copy.93
  379.4 7.8 reshape.165
  387.8 5.1 all-to-all-start
  393.6 216.3 %all-gather.5 = bf16[64,12,96]{2,1,0:T(8,128)(2,1)S(1)} all-gather(bf16[1,12,96]{2,1,0:T(8,128)(2,1)S(1)} %bitcast.151), channel_id=1, replica_groups=mesh['grp'=16,'pb'=4,'ka'=8] {'grp','pb'}, dimensions={0}, use_global_device_ids=true | all-gather | bytes 149760 | tf_op jit(solution)/shard_map/all_gather | solution.py:48
  610.6 188.7 %all-gather.6 = bf16[64,12,192]{2,1,0:T(8,128)(2,1)S(1)} all-gather(bf16[1,12,192]{2,1,0:T(8,128)(2,1)S(1)} %bitcast.148), channel_id=1, replica_groups=mesh['grp'=16,'pb'=4,'ka'=8] {'grp','pb'}, dimensions={0}, use_global_device_ids=true | all-gather | bytes 299520 | tf_op jit(solution)/shard_map/all_gather | solution.py:49
  800.3 193.2 %all-gather.7 = bf16[64,12,192]{2,1,0:T(8,128)(2,1)S(1)} all-gather(bf16[1,12,192]{2,1,0:T(8,128)(2,1)S(1)} %bitcast.149), channel_id=1, replica_groups=mesh['grp'=16,'pb'=4,'ka'=8] {'grp','pb'}, dimensions={0}, use_global_device_ids=true | all-gather | bytes 299520 | tf_op jit(solution)/shard_map/all_gather | solution.py:50
  994.5 187.7 %all-gather.8 = bf16[64,12,192]{2,1,0:T(8,128)(2,1)S(1)} all-gather(bf16[1,12,192]{2,1,0:T(8,128)(2,1)S(1)} %bitcast.150), channel_id=1, replica_groups=mesh['grp'=16,'pb'=4,'ka'=8] {'grp','pb'}, dimensions={0}, use_global_device_ids=true | all-gather | bytes 299520 | tf_op jit(solution)/shard_map/all_gather | solution.py:51
  1183.1 2.2 reshape.153
  1185.4 2.1 divide_convert_fusion
  1191.5 6.3 reduce.3
  1197.8 5.0 reshape.166
  1202.8 2.9 multiply_reduce_fusion
  1206.3 134.6 %all_gather.46 = bf16[64,8,768]{2,1,0:T(8,128)(2,1)S(1)} all-gather(bf16[8,8,768]{2,1,0:T(8,128)(2,1)S(1)} %fusion.52), channel_id=1, replica_groups=mesh['grp'=16,'pb'=4,'ka'=8] {'ka'}, dimensions={0}, use_global_device_ids=true | all-gather | bytes 884736 | tf_op jit(solution)/shard_map/all_gather | solution.py:134
  1341.4 20.6 %all_gather.48 = bf16[64,8,768]{0,1,2:T(8,128)(2,1)S(1)} all-gather(bf16[64,8,96]{0,1,2:T(8,128)(2,1)S(1)} %copy.98), channel_id=1, replica_groups=mesh['grp'=16,'pb'=4,'ka'=8] {'ka'}, dimensions={2}, use_global_device_ids=true | all-gather | bytes 884736 | tf_op jit(solution)/shard_map/all_gather | solution.py:145
  1364.5 1.9 fusion.17
  1366.5 28.4 %reduce-scatter.2.cloned.1.call-done = bf16[8,8,768]{2,1,0:T(8,128)(2,1)} async-done(((bf16[64,8,768]{2,1,0:T(8,128)(2,1)}), bf16[8,8,768]{2,1,0:T(8,128)(2,1)}) %reduce-scatter.2.cloned.1.call-update) | async-done | bytes 98320 | tf_op jit(solution)/shard_map/reduce_scatter | solution.py:152
  (108 shorter events, 30.4 us)
Async XLA Ops:
  6.5 29.7 %copy-start = (f32[128,16]{0,1:T(8,128)S(1)}, f32[128,16]{0,1:T(8,128)}, u32[]{:S(2)}) copy-start(f32[128,16]{0,1:T(8,128)} %param.25) | copy-start | bytes 24580
  6.5 28.4 %copy-start.2 = (bf16[1,64,4,8,128]{4,3,2,1,0:T(8,128)(2,1)S(1)}, bf16[1,64,4,8,128]{4,3,2,1,0:T(8,128)(2,1)}, u32[]{:S(2)}) copy-start(bf16[1,64,4,8,128]{4,3,2,1,0:T(8,128)(2,1)} %param.23) | copy-start | bytes 1572868
  6.5 117.9 %all-gather.18.cloned.1.call-start = ((), (), s32[]{:S(2)}) async-start(), calls=%async_computation.7 | async-start | bytes 1597440 | tf_op jit(solution)/shard_map/all_gather | solution.py:44
  7.3 223.3 %all-gather.16.cloned.1.call-start = ((), (), s32[]{:S(2)}) async-start(), calls=%async_computation.6 | async-start | bytes 1597440 | tf_op jit(solution)/shard_map/all_gather | solution.py:45
  8.0 328.6 %all-gather.14.cloned.1.call-start = ((), (), s32[]{:S(2)}) async-start(), calls=%async_computation.5 | async-start | bytes 1597440 | tf_op jit(solution)/shard_map/all_gather | solution.py:46
  9.7 26.6 %copy-start.18 = (f32[128]{0:T(128)S(1)}, f32[128]{0:T(128)}, u32[]{:S(2)}) copy-start(f32[128]{0:T(128)} %param.24) | copy-start | bytes 1540
  37.5 3.3 copy-start.11
  41.1 86.4 %copy-start.4 = (bf16[8,64,768]{2,1,0:T(8,128)(2,1)}, bf16[8,64,768]{2,1,0:T(8,128)(2,1)S(1)}, u32[]{:S(2)}) copy-start(bf16[8,64,768]{2,1,0:T(8,128)(2,1)S(1)} %fusion.16) | copy-start | bytes 2359300
  131.1 101.8 %copy-start.1 = (bf16[1,8,8,768]{3,2,1,0:T(8,128)(2,1)S(1)}, bf16[1,8,8,768]{3,2,1,0:T(8,128)(2,1)}, u32[]{:S(2)}) copy-start(bf16[1,8,8,768]{3,2,1,0:T(8,128)(2,1)} %param.16) | copy-start | bytes 294916
  131.1 101.8 %copy-start.15 = (f32[64]{0:T(128)S(1)}, f32[64]{0:T(128)}, u32[]{:S(2)}) copy-start(f32[64]{0:T(128)} %rsqrt.36) | copy-start | bytes 772
  232.8 21.4 %copy-start.8 = (f32[64,16,32]{0,2,1:T(8,128)S(1)}, f32[64,16,32]{0,2,1:T(8,128)}, u32[]{:S(2)}) copy-start(f32[64,16,32]{0,2,1:T(8,128)} %copy.91) | copy-start | bytes 393220
  232.8 21.4 %copy-start.19 = (pred[32]{0:T(512)(128)(4,1)S(1)}, pred[32]{0:T(512)(128)(4,1)}, u32[]{:S(2)}) copy-start(pred[32]{0:T(512)(128)(4,1)} %lt.19) | copy-start | bytes 100
  258.9 103.7 %all-to-all-start.2 = ((f32[8,1,1024]{2,1,0:T(1,128)}), f32[8,1,1024]{2,1,0:T(1,128)S(1)}, u32[]{:S(2)}, u32[]{:S(2)}) async-start(f32[8,1,1024]{2,1,0:T(1,128)} %reshape.169), calls=%async_computation.2 | async-start | bytes 65536 | tf_op jit(solution)/shard_map/all_to_all | solution.py:118
  362.6 11.6 copy-start.9
  362.6 24.6 %all-to-all-start.1 = ((f32[8,1,1024]{2,1,0:T(1,128)}), f32[8,1,1024]{2,1,0:T(1,128)S(1)}, u32[]{:S(2)}, u32[]{:S(2)}) async-start(f32[8,1,1024]{2,1,0:T(1,128)} %reshape.167), calls=%async_computation.1 | async-start | bytes 65536 | tf_op jit(solution)/shard_map/all_to_all | solution.py:117
  387.2 6.4 copy-start.16
  387.2 223.4 %copy-start.12 = (bf16[12,192]{1,0:T(8,128)(2,1)S(1)}, bf16[12,192]{1,0:T(8,128)(2,1)}, u32[]{:S(2)}) copy-start(bf16[12,192]{1,0:T(8,128)(2,1)} %param.27) | copy-start | bytes 13828
  387.2 0.6 copy-start.10
  387.8 803.6 %all-to-all-start = ((f32[8,1,49152]{2,1,0:T(1,128)}), f32[8,1,49152]{2,1,0:T(1,128)S(1)}, u32[]{:S(2)}, u32[]{:S(2)}) async-start(f32[8,1,49152]{2,1,0:T(1,128)} %reshape.165), calls=%async_computation | async-start | bytes 3145728 | tf_op jit(solution)/shard_map/all_to_all | solution.py:119
  393.0 407.3 %copy-start.13 = (bf16[12,192]{1,0:T(8,128)(2,1)S(1)}, bf16[12,192]{1,0:T(8,128)(2,1)}, u32[]{:S(2)}) copy-start(bf16[12,192]{1,0:T(8,128)(2,1)} %param.28) | copy-start | bytes 13828
  393.0 790.2 %all-gather.20.cloned.1.call-start = ((), (), s32[]{:S(2)}) async-start(), calls=%async_computation.8 | async-start | bytes 1597440 | tf_op jit(solution)/shard_map/all_gather | solution.py:47
  393.5 1001.4 %reduce-scatter.2.cloned.1.call-start = ((), (), s32[]{:S(2)}) async-start(), calls=%async_computation.4 | async-start | bytes 884736 | tf_op jit(solution)/shard_map/reduce_scatter | solution.py:152
  609.8 384.6 %copy-start.14 = (bf16[192,12]{0,1:T(8,128)(2,1)S(1)}, bf16[192,12]{0,1:T(8,128)(2,1)}, u32[]{:S(2)}) copy-start(bf16[192,12]{0,1:T(8,128)(2,1)} %param.29) | copy-start | bytes 13828
  1205.8 135.0 %copy-start.3 = (bf16[768,96]{1,0:T(8,128)(2,1)S(1)}, bf16[768,96]{1,0:T(8,128)(2,1)}, u32[]{:S(2)}) copy-start(bf16[768,96]{1,0:T(8,128)(2,1)} %reshape.155) | copy-start | bytes 442372
  1362.0 1.8 copy-start.5
  1362.0 1.8 copy-start.17
  1363.4 1.0 copy-start.6
  1363.4 1.1 copy-start.7
Sparse Core Ops, SparseCore 0:
  11.5 112.8 all-gather.17
  128.6 101.9 all-gather.15
  234.7 101.9 all-gather.13
  397.6 109.8 all-gather.19
  1366.6 28.2 reduce-scatter.1
where the time goes:
time: 1410 us; the launch traced here: 1400 us
  blocking collectives  1000 us (71%)
  waiting for transfers between devices  284 us (20%)
  local copies, waits for them, and re-layouts  48.8 us (3%)
  other arithmetic  19 us (1%)
  starting transfers between devices  18.7 us (1%)
  matrix products  17 us (1%)
  between operations  14.2 us (1%)
    all_gather x1, blocking collectives, on_device(): lax.all_gather(w_out, ('grp', 'pb'), axis=0, tiled=True)  216 us
    all_gather x1, blocking collectives, on_device(): lax.all_gather(w_up, ('grp', 'pb'), axis=0, tiled=True)  193 us
    all_gather x1, blocking collectives, on_device(): lax.all_gather(w_swish, ('grp', 'pb'), axis=0, tiled=True)  189 us
    all_gather x1, blocking collectives, on_device(): lax.all_gather(w_down, ('grp', 'pb'), axis=1, tiled=True)  188 us
    all_gather x1, blocking collectives, on_device(): gated_out = lax.all_gather(own_gated, 'ka', axis=0, tiled=True)  135 us
    all_gather x1, waiting for transfers between devices, on_device(): lax.all_gather(w_key, ('grp', 'pb'), axis=0, tiled=True)  99.5 us
    all_gather x1, waiting for transfers between devices, on_device(): lax.all_gather(w_query, ('grp', 'pb'), axis=0, tiled=True)  83.3 us
    all_gather x1, waiting for transfers between devices, on_device(): lax.all_gather(w_value, ('grp', 'pb'), axis=0, tiled=True)  70.1 us
  transfers between devices with their start and end apart: 8, of which 4 were waited for; matrix products, arithmetic and copies ran while one was open for 4% of the time, Pallas kernels for 0%

commit v1 on v0

v1 whole, which is shorter than its diff:
```python
import functools
import math

import jax
import jax.numpy as jnp
from jax import lax
from jax.experimental import pallas as pl
from jax.experimental.pallas import tpu as pltpu
from jax.sharding import PartitionSpec as P

HEADS = 16
TP = 4

epsilon = 1e-05
very_negative = -1e30
f32 = jnp.float32
bf16 = jnp.bfloat16
VMEM_LIMIT = 48 * 1024 * 1024


def layer_norm(inputs, scale_gain):
    mean_val = jnp.mean(inputs, axis=-1, keepdims=True)
    centred = inputs - mean_val
    spread = jnp.mean(centred * centred, axis=-1, keepdims=True)
    return centred * lax.rsqrt(spread + epsilon) * scale_gain


def dot_last(a, b, precision=None):
    return lax.dot_general(
        a, b, (((1,), (1,)), ((), ())), preferred_element_type=f32, precision=precision
    )


def exchange(blocks, axes, groups=None):
    return lax.all_to_all(
        blocks, axes, split_axis=0, concat_axis=0, tiled=True, axis_index_groups=groups
    )


def spread(block, count, axes):
    return exchange(jnp.broadcast_to(block[None], (count,) + block.shape), axes)


def gather(block, axes):
    return lax.all_gather(block, axes, axis=0, tiled=False)


def swap(block, axis, flip):
    count = lax.axis_size(axis)
    return lax.ppermute(block, axis, [(i, i ^ flip) for i in range(count)])


def bias_kernel(info_ref, x_ref, gain_ref, proj_ref, *refs):
    out_refs, rows, held = refs[:-2], refs[-2], refs[-1]
    queries, keys, channels = x_ref.shape
    pairs = len(out_refs)
    normed = layer_norm(
        x_ref[...].reshape(queries * keys, channels).astype(f32), gain_ref[...]
    )
    rows[...] = normed
    together = 256 // queries
    for start in range(0, keys, together):
        block = jnp.concatenate(
            [rows[pl.ds(start + j, queries, stride=keys), :] for j in range(together)], axis=0
        )
        bias = dot_last(proj_ref[...], block, lax.Precision.HIGHEST)
        for j in range(together):
            cols = slice(j * queries, (j + 1) * queries)
            tile = jnp.concatenate([bias[:pairs, cols], bias[pairs:, cols]], axis=1)
            held[:, start + j, :] = tile
    for flip, out_ref in enumerate(out_refs):
        out_ref[...] = held[info_ref[1] ^ flip]


def attention_kernel(feats, info_ref, x_ref, other_ref, gain_ref, w_ref, *refs):
    count = len(refs) - 5
    bias_refs = refs[:count]
    out_ref, held_normed, held_bias, held_query, held_gate = refs[count:]
    places, own_rows, width = x_ref.shape
    chips = count // 2
    blocks = places // chips
    keys_held, lanes = bias_refs[0].shape
    q_rows = lanes // 2
    each = q_rows // count
    samples = own_rows // each
    key_count = blocks * q_rows
    head_dim = feats // 2
    length, at, block_at = info_ref[0], info_ref[1], info_ref[2]
    core = at % 2
    weights = w_ref[...].reshape(width, 4 * feats)
    w_kv, w_qg = weights[:, : 2 * feats], weights[:, 2 * feats :]
    key_value = []
    for side, ref in enumerate((x_ref, other_ref)):
        x = ref[...].reshape(places * own_rows, width).astype(f32)
        normed = layer_norm(x, gain_ref[...]).astype(bf16)
        held_normed[side] = normed.reshape(places, own_rows, width)
        proj = jnp.dot(normed, w_kv, preferred_element_type=f32)
        key_value.append(proj.reshape(places, samples, each, 2 * feats))
    for side in range(2):
        rows = held_normed[side, pl.ds(block_at * chips, chips)].reshape(chips * own_rows, width)
        proj = jnp.dot(rows, w_qg, preferred_element_type=f32)
        for z in range(chips):
            k = 2 * z + (core ^ side)
            part = proj[z * own_rows : (z + 1) * own_rows]
            held_query[k] = part[:, :feats]
            held_gate[k] = part[:, feats:]
    for flip in range(count):
        held_bias[at ^ flip] = bias_refs[flip][...]
    bias = jnp.concatenate(
        [
            held_bias[2 * z + (core ^ side), b * each : (b + 1) * each, :]
            for side in range(2)
            for b in range(blocks)
            for z in range(chips)
        ],
        axis=0,
    )
    index = lax.broadcasted_iota(jnp.int32, (key_count, lanes), 0)
    span = places * each
    side = index // span
    position = ((index % span) // each) * (2 * each) + (side ^ core) * each + index % each
    live = position < length
    first = lax.broadcasted_iota(jnp.int32, (q_rows, feats), 1) < head_dim
    done = []
    for s in range(samples):
        both_sides = jnp.concatenate(
            [part[:, s].reshape(span, 2 * feats) for part in key_value], axis=0
        )
        keys = both_sides[:, :feats].astype(bf16)
        values = both_sides[:, feats:].astype(bf16)
        rows = slice(s * each, (s + 1) * each)
        query = held_query[:, rows, :].reshape(q_rows, feats)
        both = jnp.concatenate(
            [jnp.where(first, query, 0.0), jnp.where(first, 0.0, query)], axis=0
        ).astype(bf16)
        scores = dot_last(keys, both) * (1.0 / math.sqrt(head_dim)) + bias
        scores = jnp.where(live, scores, very_negative)
        peak = jnp.max(scores, axis=0, keepdims=True)
        soft = jnp.exp(scores - peak)
        total = jnp.sum(soft, axis=0, keepdims=True)
        weighted = lax.dot_general(
            values, soft.astype(bf16), (((0,), (0,)), ((), ())), preferred_element_type=f32
        )
        attended = (weighted / total).T
        attended = jnp.where(first, attended[:q_rows], attended[q_rows:])
        gate = jax.nn.sigmoid(held_gate[:, rows, :].reshape(q_rows, feats))
        gate = gate.astype(bf16).astype(f32)
        done.append((attended * gate).reshape(count, each, feats))
        if s % 2:
            size = 2 * each
            start = s // 2 * size
            out_ref[:, start : start + size, :] = jnp.concatenate(done, axis=1).astype(bf16)
            done = []


def mix_kernel(
    info_ref, gated_ref, w_ref, other_ref, single_ref, gain_ref, mixed_ref, normed_ref, held
):
    ka_count, rows, feats = gated_ref.shape
    width = single_ref.shape[1]
    chips = ka_count // 2
    at = info_ref[1]
    gated = jnp.concatenate([gated_ref[k] for k in range(ka_count)], axis=1)
    for side, ref in enumerate((w_ref, other_ref)):
        weights = ref[:, :, ref.shape[2] - chips * feats :].reshape(width, chips * feats)
        added = jnp.dot(gated, weights, preferred_element_type=f32)
        for flip in range(chips):
            held[at ^ (2 * flip + side)] = added[:, flip * feats : (flip + 1) * feats]
    added = jnp.concatenate([held[k] for k in range(ka_count)], axis=1)
    mixed = (single_ref[...].astype(f32) + added).astype(bf16)
    mixed_ref[...] = mixed
    normed = layer_norm(mixed.astype(f32), gain_ref[...]).astype(bf16)
    for i in range(normed_ref.shape[0]):
        normed_ref[i] = normed


def transition_kernel(hidden_count, x_ref, w_ref, out_ref):
    groups, rows, width = x_ref.shape
    part = hidden_count
    x = x_ref[...].reshape(groups * rows, width)
    down, swish, up = (
        w_ref[:, :, i * part : (i + 1) * part].reshape(width, part) for i in range(3)
    )
    a = jnp.dot(x, swish, preferred_element_type=f32)
    b = jnp.dot(x, up, preferred_element_type=f32)
    hidden = ((a / (1.0 + jnp.exp(-a))) * b).astype(bf16)
    out_ref[...] = dot_last(hidden, down).astype(bf16).reshape(groups, rows, width)


def finish_kernel(mixed_ref, part_ref, out_ref):
    total = mixed_ref[...].astype(f32)
    for i in range(part_ref.shape[0]):
        total = total + part_ref[i].astype(f32)
    out_ref[...] = total.astype(bf16)


def call(kernel, out_shape, scratch=(), scalars=0, flops=0, moved=0):
    def run(*operands):
        return pl.pallas_call(
            kernel,
            out_shape=out_shape,
            in_specs=[
                pl.BlockSpec(memory_space=pltpu.SMEM if i < scalars else pltpu.VMEM)
                for i in range(len(operands))
            ],
            scratch_shapes=list(scratch),
            compiler_params=pltpu.CompilerParams(vmem_limit_bytes=VMEM_LIMIT),
            cost_estimate=pl.CostEstimate(flops=flops, bytes_accessed=moved, transcendentals=0),
        )(*operands)

    return run


def on_device(
    lengths,
    single,
    attn_gain,
    w_query,
    w_key,
    w_value,
    w_gate,
    w_out,
    pair_rep,
    pair_gain,
    pair_proj,
    trans_gain,
    w_swish,
    w_up,
    w_down,
):
    grp_count = lax.axis_size("grp")
    pb_count = lax.axis_size("pb")
    ka_count = lax.axis_size("ka")
    ka_index = lax.axis_index("ka")
    samples, row_count, width = single.shape[1:]
    w_rows = w_query.shape[0]
    feats = width // ka_count
    hid = w_swish.shape[1]
    own_rows = samples * row_count
    chips = ka_count // 2
    held = ka_count // TP
    info = jnp.stack([lengths[0], ka_index, lax.axis_index("pb")]).astype(jnp.int32)
    own = single.reshape(own_rows, width)

    line = [[i * 2 + c for i in range(pb_count * chips)] for c in range(2)]
    x = lax.all_gather(own, ("pb", "ka"), axis=0, tiled=False, axis_index_groups=line)
    other = swap(x, "ka", 1)

    early = [
        lax.dynamic_slice_in_dim(w, ka_index * feats, feats, 1)
        for w in (w_key, w_value, w_query, w_gate)
    ]
    early = jnp.concatenate(early + [w_down.T, w_swish, w_up, w_out], axis=1)
    early, pair_rep = lax.optimization_barrier((early, pair_rep))
    early = spread(early, pb_count, "pb").reshape(pb_count * w_rows, early.shape[1])

    attn_w = spread(early[:, : 4 * feats], grp_count, "grp")

    out_w = early[:, 4 * feats + 3 * hid :]
    out_w = [out_w] + [swap(out_w, "ka", 2)]
    late = jnp.concatenate([early[:, 4 * feats : 4 * feats + 3 * hid]] + out_w, axis=1)
    late = [late] + [swap(late, "ka", TP)]
    late = jnp.concatenate(
        [w[:, i * hid : (i + 1) * hid] for i in range(3) for w in late]
        + [w[:, 3 * hid :] for w in late],
        axis=1,
    )

    _, queries, key_blocks, key_rows, channels = pair_rep.shape
    keys_held = key_blocks * key_rows
    lanes = 2 * queries
    proj = pair_proj.reshape(channels, HEADS // 2, 2).transpose(2, 1, 0).reshape(HEADS, channels)
    bias = call(
        bias_kernel,
        (jax.ShapeDtypeStruct((keys_held, lanes), f32),) * ka_count,
        scratch=[
            pltpu.VMEM((queries * keys_held, channels), f32),
            pltpu.VMEM((ka_count, keys_held, lanes), f32),
        ],
        scalars=1,
        flops=2 * 6 * queries * keys_held * channels * HEADS,
        moved=queries * keys_held * channels * 2 + 4 * ka_count * keys_held * lanes,
    )(info, pair_rep.reshape(queries, keys_held, channels), pair_gain.reshape(1, channels), proj)
    late, attn_w, bias = lax.optimization_barrier((late, attn_w, list(bias)))
    late = spread(late, grp_count, "grp")
    bias = [bias[0]] + [swap(bias[i], "ka", i) for i in range(1, ka_count)]

    gated = call(
        functools.partial(attention_kernel, feats),
        jax.ShapeDtypeStruct((ka_count, own_rows, feats), bf16),
        scratch=[
            pltpu.VMEM((2,) + x.shape, bf16),
            pltpu.VMEM((ka_count, keys_held, lanes), f32),
            pltpu.VMEM((ka_count, own_rows, feats), f32),
            pltpu.VMEM((ka_count, own_rows, feats), f32),
        ],
        scalars=1,
        flops=4 * x.size * 2 * feats,
        moved=x.size * 4 + attn_w.size * 2,
    )(info, x, other, attn_gain.reshape(1, width), attn_w, *bias)
    gated = exchange(gated, "ka")
    out_w = swap(late[:, :, held * 3 * hid :], "ka", 1)

    rows = jax.ShapeDtypeStruct((own_rows, width), bf16)
    shared = jax.ShapeDtypeStruct((TP, own_rows, width), bf16)
    mixed, normed_t = call(
        mix_kernel,
        (rows, shared),
        scratch=[pltpu.VMEM((ka_count, own_rows, feats), f32)],
        scalars=1,
        flops=2 * own_rows * width * width,
        moved=width * width * 2,
    )(info, gated, late, out_w, own, trans_gain.reshape(1, width))

    groups = [list(range(i, i + TP)) for i in range(0, ka_count, TP)]
    normed_t = exchange(normed_t, "ka", groups)
    part = call(
        functools.partial(transition_kernel, held * hid),
        shared,
        flops=2 * own_rows * width * hid * ka_count * 3,
        moved=3 * width * hid * ka_count // TP * 2,
    )(normed_t, late)
    part = exchange(part, "ka", groups)
    result = call(finish_kernel, rows)(mixed, part)
    return result.reshape(1, samples, row_count, width)


def solution(mesh):
    return jax.shard_map(
        on_device,
        mesh=mesh,
        in_specs=(
            P("grp"),
            P("grp", None, ("pb", "ka"), None),
            P(),
            P(("grp", "pb"), None),
            P(("grp", "pb"), None),
            P(("grp", "pb"), None),
            P(("grp", "pb"), None),
            P(("grp", "pb"), "ka"),
            P("grp", "pb", None, "ka", None),
            P(),
            P(),
            P(),
            P(("grp", "pb"), "ka"),
            P(("grp", "pb"), "ka"),
            P("ka", ("grp", "pb")),
        ),
        out_specs=P("grp", None, ("pb", "ka"), None),
        check_vma=False,
    )
```

time: 1410 us -> 179 us (0.13)
  blocking collectives: 1000 us -> 19.6 us
  waiting for transfers between devices: 284 us -> 33.7 us
  starting transfers between devices: 18.7 us -> 79.3 us
  local copies, waits for them, and re-layouts: 48.8 us -> 19.6 us
  other arithmetic: 19 us -> 0.24 us
  matrix products: 17 us -> 0 us
    all_gather x9 -> x0, blocking collectives: 1000 us -> none  [the longest x1 216 us: on_device(): lax.all_gather(w_out, ('grp', 'pb'), axis=0, tiled=True)]
    all_gather x4 -> x1, waiting for transfers between devices: 253 us -> 12.9 us  [on_device(): lax.all_gather(own, ('pb', 'ka'), axis=0, tiled=False, axis_index_groups=...]
    ppermute x0 -> x11, starting transfers between devices: none -> 48.1 us  [swap(): return lax.ppermute(block, axis, [(i, i ^ flip) for i in range(count)])]
    reduce_scatter x1 -> x0, waiting for transfers between devices: 28.4 us -> none  [on_device(): lax.psum_scatter(project(hidden, w_down).reshape(count, samples, model_wi...]
    all_to_all x0 -> x2, blocking collectives: none -> 19.6 us  [exchange(): lax.all_to_all(blocks, axes, split_axis=0, concat_axis=0, tiled=True, axi...]
    unnamed x55 -> x30, local copies, waits for them, and re-layouts: 29.8 us -> 10.6 us
    dot_general x10 -> x0, matrix products: 17 us -> none  [the longest x7 7.77 us: project(): return jnp.dot(inputs, weight, preferred_element_type=jnp.float32)]
    all_to_all x3 -> x4, starting transfers between devices: 18.6 us -> 31.2 us  [exchange(): lax.all_to_all(blocks, axes, split_axis=0, concat_axis=0, tiled=True, axi...]
  transfers between devices with their start and end apart: 8 -> 16, of which waited for: 4 -> 7; matrix products, arithmetic and copies ran while one was open for 4% -> 5% of each run, Pallas kernels for 0% -> 4%
where the time goes in v1:
time: 179 us; the launch traced here: 177 us
  starting transfers between devices  79.3 us (44%)
  waiting for transfers between devices  33.7 us (19%)
  local copies, waits for them, and re-layouts  19.6 us (11%)
  blocking collectives  19.6 us (11%)
  between operations  14.3 us (8%)
  Pallas kernels  10.6 us (6%)
    ppermute x11, starting transfers between devices, swap(): return lax.ppermute(block, axis, [(i, i ^ flip) for i in range(count)])  48.1 us
    all_to_all x4, starting transfers between devices, exchange(): lax.all_to_all(blocks, axes, split_axis=0, concat_axis=0, tiled=True, axi...  31.2 us
    all_to_all x2, blocking collectives, exchange(): lax.all_to_all(blocks, axes, split_axis=0, concat_axis=0, tiled=True, axi...  19.6 us
    all_to_all x4, waiting for transfers between devices, exchange(): lax.all_to_all(blocks, axes, split_axis=0, concat_axis=0, tiled=True, axi...  13.5 us
    all_gather x1, waiting for transfers between devices, on_device(): lax.all_gather(own, ('pb', 'ka'), axis=0, tiled=False, axis_index_groups=...  12.9 us
    unnamed x30, local copies, waits for them, and re-layouts  10.6 us
    pallas_call x5, Pallas kernels, run(): pl.pallas_call(kernel, out_shape=out_shape, in_specs=[pl.BlockSpec(memory...  10.6 us
    ppermute x11, waiting for transfers between devices, swap(): return lax.ppermute(block, axis, [(i, i ^ flip) for i in range(count)])  6.63 us
  transfers between devices with their start and end apart: 16, of which 7 were waited for; matrix products, arithmetic and copies ran while one was open for 5% of the time, Pallas kernels for 4%

profile of v1, /device:TPU:1, one launch (start us, length us, event | category | flops | bytes accessed | tf_op | source)
XLA Modules:
  0.0 177.4 jit_solution(5730594751208359471)
XLA Ops:
  10.3 15.6 %all-to-all-start = ((bf16[4,12,1056]{2,1,0:T(8,128)(2,1)}), bf16[4,12,1056]{2,1,0:T(8,128)(2,1)S(1)}, u32[]{:S(2)}, u32[]{:S(2)}) async-start(bf16[4,12,1056]{2,1,0:T(8,128)(2,1)} %broadcast_in_dim.6), calls=%async_computation | async-start | bytes 294912 | tf_op jit(solution)/shard_map/all_to_all | solution.py:35
  27.9 1.0 copy-done.2
  29.6 2.3 %shard_map.145 = (f32[32,128]{1,0:T(8,128)S(1)}, f32[32,128]{1,0:T(8,128)S(1)}, f32[32,128]{1,0:T(8,128)S(1)}, f32[32,128]{1,0:T(8,128)S(1)}, f32[32,128]{1,0:T(...) custom-call(s32[3]{0:T(128)S(1)} %pad_add_fusion.info_ref, ...), custom_call_target="tpu_custom_call" | custom-call | flops 50331648 | bytes 655360 | tf_op jit(solution)/shard_map/pallas_call | solution.py:199
  36.1 2.6 %all-to-all-done = bf16[4,12,1056]{2,1,0:T(8,128)(2,1)S(1)} async-done(((bf16[4,12,1056]{2,1,0:T(8,128)(2,1)}), bf16[4,12,1056]{2,1,0:T(8,128)(2,1)S(1)}, u32[]{:S(2)}, u32[]{:S(2)}) %all-to-all-start) | async-done | bytes 101408 | tf_op jit(solution)/shard_map/all_to_all | solution.py:35
  38.9 4.6 %collective-permute-start.1 = (bf16[48,96]{1,0:T(8,128)(2,1)S(1)}, bf16[48,96]{1,0:T(8,128)(2,1)S(1)}, u32[]{:S(2)}, u32[]{:S(2)}) collective-permute-start(bf16[48,96]{1,0:T(8,128)(2,1)S(1)} %slice.54), channel_id=1, source_target_pairs={{0,2},{1,3},{2,0},{3,1},{4,6},{5,7},{6,4},{7,5},{8,10},{9,11},{10,... | collective-permute-start | bytes 27656 | tf_op jit(solution)/shard_map/ppermute | solution.py:50
  44.3 6.7 %all-to-all-start.1 = ((bf16[16,48,384]{2,1,0:T(8,128)(2,1)}), bf16[16,48,384]{2,1,0:T(8,128)(2,1)S(1)}, u32[]{:S(2)}, u32[]{:S(2)}) async-start(bf16[16,48,384]{2,1,0:T(8,128)(2,1)} %broadcast_in_dim.7), calls=%async_computation.1 | async-start | bytes 1179648 | tf_op jit(solution)/shard_map/all_to_all | solution.py:35
  51.2 2.4 %collective-permute-start.2 = (bf16[48,768]{1,0:T(8,128)(2,1)S(1)}, bf16[48,768]{1,0:T(8,128)(2,1)S(1)}, u32[]{:S(2)}, u32[]{:S(2)}) collective-permute-start(bf16[48,768]{1,0:T(8,128)(2,1)S(1)} %pad_maximum_fusion), channel_id=1, source_target_pairs={{0,4},{1,5},{2,6},{3,7},{4,0},{5,1},{6,2},{7,3},{8,12},{9,13},{10,... | collective-permute-start | bytes 221192 | tf_op jit(solution)/shard_map/ppermute | solution.py:50
  53.7 4.3 %collective-permute-done.2 = bf16[48,768]{1,0:T(8,128)(2,1)S(1)} collective-permute-done((bf16[48,768]{1,0:T(8,128)(2,1)S(1)}, bf16[48,768]{1,0:T(8,128)(2,1)S(1)}, u32[]{:S(2)}, u32[]{:S(2)}) %collective-permute-start.2) | collective-permute-done | bytes 73760 | tf_op jit(solution)/shard_map/ppermute | solution.py:50
  58.2 2.2 %all-to-all-done.1.w_ref = bf16[16,48,384]{2,1,0:T(8,128)(2,1)S(1)} async-done(((bf16[16,48,384]{2,1,0:T(8,128)(2,1)}), bf16[16,48,384]{2,1,0:T(8,128)(2,1)S(1)}, u32[]{:S(2)}, u32[]{:S(2)}) %all-to-all-start.1) | async-done | bytes 589856 | tf_op jit(solution)/shard_map/all_to_all | solution.py:35
  60.4 1.6 broadcast_in_dim.8
  62.1 4.9 %all-to-all-start.3 = ((bf16[16,48,1536]{2,1,0:T(8,128)(2,1)}), bf16[16,48,1536]{2,1,0:T(8,128)(2,1)S(1)}, u32[]{:S(2)}, u32[]{:S(2)}) async-start(bf16[16,48,1536]{2,1,0:T(8,128)(2,1)} %broadcast_in_dim.8), calls=%async_computation.3 | async-start | bytes 4718592 | tf_op jit(solution)/shard_map/all_to_all | solution.py:35
  67.0 12.9 %all-gather.2.cloned.1.call-done.x_ref = bf16[16,64,768]{2,1,0:T(8,128)(2,1)} async-done(((bf16[1,64,768]{2,1,0:T(8,128)(2,1)}), bf16[16,64,768]{2,1,0:T(8,128)(2,1)}) %all-gather.2.cloned.1.call-update) | async-done | bytes 1572880 | tf_op jit(solution)/shard_map/all_gather | solution.py:246
  79.9 11.0 %collective-permute-start = (bf16[16,64,768]{2,1,0:T(8,128)(2,1)}, bf16[16,64,768]{2,1,0:T(8,128)(2,1)}, u32[]{:S(2)}, u32[]{:S(2)}) collective-permute-start(bf16[16,64,768]{2,1,0:T(8,128)(2,1)} %all-gather.2.cloned.1.call-done.x_ref), channel_id=1, source_target_pairs={{0,1},{1,0},{2,3},{3,2},{4,5},{5,4},{6,7},{7,6},{8,9},{9,8},{10,11... | collective-permute-start | bytes 4718600 | tf_op jit(solution)/shard_map/ppermute | solution.py:50
  90.9 3.6 %all-to-all-done.3.w_ref = bf16[16,48,1536]{2,1,0:T(8,128)(2,1)S(1)} async-done(((bf16[16,48,1536]{2,1,0:T(8,128)(2,1)}), bf16[16,48,1536]{2,1,0:T(8,128)(2,1)S(1)}, u32[]{:S(2)}, u32[]{:S(2)}) %all-to-all-start.3) | async-done | bytes 2359328 | tf_op jit(solution)/shard_map/all_to_all | solution.py:35
  94.5 0.9 slice.64
  95.4 8.5 %collective-permute-start.10 = (bf16[16,48,384]{2,1,0:T(8,128)(2,1)}, bf16[16,48,384]{2,1,0:T(8,128)(2,1)S(1)}, u32[]{:S(2)}, u32[]{:S(2)}) collective-permute-start(bf16[16,48,384]{2,1,0:T(8,128)(2,1)} %slice.64), channel_id=1, source_target_pairs={{0,1},{1,0},{2,3},{3,2},{4,5},{5,4},{6,7},{7,6},{8,9},{9,8},{10,11... | collective-permute-start | bytes 1769480 | tf_op jit(solution)/shard_map/ppermute | solution.py:50
  103.9 1.9 %collective-permute-start.3 = (f32[32,128]{1,0:T(8,128)}, f32[32,128]{1,0:T(8,128)S(1)}, u32[]{:S(2)}, u32[]{:S(2)}) collective-permute-start(f32[32,128]{1,0:T(8,128)} %copy-done.14), channel_id=1, source_target_pairs={{0,1},{1,0},{2,3},{3,2},{4,5},{5,4},{6,7},{7,6},{8,9},{9,8},{10,11... | collective-permute-start | bytes 49160 | tf_op jit(solution)/shard_map/ppermute | solution.py:50
  105.8 2.0 %collective-permute-start.4 = (f32[32,128]{1,0:T(8,128)}, f32[32,128]{1,0:T(8,128)S(1)}, u32[]{:S(2)}, u32[]{:S(2)}) collective-permute-start(f32[32,128]{1,0:T(8,128)} %copy-done.13), channel_id=1, source_target_pairs={{0,2},{1,3},{2,0},{3,1},{4,6},{5,7},{6,4},{7,5},{8,10},{9,11},{10,... | collective-permute-start | bytes 49160 | tf_op jit(solution)/shard_map/ppermute | solution.py:50
  107.8 4.0 %collective-permute-start.5 = (f32[32,128]{1,0:T(8,128)}, f32[32,128]{1,0:T(8,128)S(1)}, u32[]{:S(2)}, u32[]{:S(2)}) collective-permute-start(f32[32,128]{1,0:T(8,128)} %copy-done.12), channel_id=1, source_target_pairs={{0,3},{1,2},{2,1},{3,0},{4,7},{5,6},{6,5},{7,4},{8,11},{9,10},{10,... | collective-permute-start | bytes 49160 | tf_op jit(solution)/shard_map/ppermute | solution.py:50
  111.8 1.9 %collective-permute-start.6 = (f32[32,128]{1,0:T(8,128)}, f32[32,128]{1,0:T(8,128)S(1)}, u32[]{:S(2)}, u32[]{:S(2)}) collective-permute-start(f32[32,128]{1,0:T(8,128)} %copy-done.11), channel_id=1, source_target_pairs={{0,4},{1,5},{2,6},{3,7},{4,0},{5,1},{6,2},{7,3},{8,12},{9,13},{10,... | collective-permute-start | bytes 49160 | tf_op jit(solution)/shard_map/ppermute | solution.py:50
  113.7 4.2 %collective-permute-start.7 = (f32[32,128]{1,0:T(8,128)}, f32[32,128]{1,0:T(8,128)S(1)}, u32[]{:S(2)}, u32[]{:S(2)}) collective-permute-start(f32[32,128]{1,0:T(8,128)} %copy-done.10), channel_id=1, source_target_pairs={{0,5},{1,4},{2,7},{3,6},{4,1},{5,0},{6,3},{7,2},{8,13},{9,12},{10,... | collective-permute-start | bytes 49160 | tf_op jit(solution)/shard_map/ppermute | solution.py:50
  117.9 3.3 %collective-permute-start.8 = (f32[32,128]{1,0:T(8,128)}, f32[32,128]{1,0:T(8,128)S(1)}, u32[]{:S(2)}, u32[]{:S(2)}) collective-permute-start(f32[32,128]{1,0:T(8,128)} %copy-done.9), channel_id=1, source_target_pairs={{0,6},{1,7},{2,4},{3,5},{4,2},{5,3},{6,0},{7,1},{8,14},{9,15},{10,... | collective-permute-start | bytes 49160 | tf_op jit(solution)/shard_map/ppermute | solution.py:50
  121.2 4.4 %collective-permute-start.9 = (f32[32,128]{1,0:T(8,128)}, f32[32,128]{1,0:T(8,128)S(1)}, u32[]{:S(2)}, u32[]{:S(2)}) collective-permute-start(f32[32,128]{1,0:T(8,128)} %copy-done.8), channel_id=1, source_target_pairs={{0,7},{1,6},{2,5},{3,4},{4,3},{5,2},{6,1},{7,0},{8,15},{9,14},{10,... | collective-permute-start | bytes 49160 | tf_op jit(solution)/shard_map/ppermute | solution.py:50
  126.4 2.3 %collective-permute-done.9.refs_7_ = f32[32,128]{1,0:T(8,128)S(1)} collective-permute-done((f32[32,128]{1,0:T(8,128)}, f32[32,128]{1,0:T(8,128)S(1)}, u32[]{:S(2)}, u32[]{:S(2)}) %collective-permute-start.9) | collective-permute-done | bytes 16416 | tf_op jit(solution)/shard_map/ppermute | solution.py:50
  128.7 1.4 copy-done
  130.7 5.5 %shard_map.146 = bf16[8,64,96]{2,1,0:T(8,128)(2,1)S(1)} custom-call(s32[3]{0:T(128)S(1)} %copy-done.5, bf16[16,64,768]{2,1,0:T(8,128)(2,1)S(1)} %copy-done, bf16[16,64,768]{2,1,0:T(8,128)(2,1)} %collective-permute-done.other_ref, f32[1,768]{1,0:T(1,128)S(1)} %reshape.30.gain_ref, bf16[16,48,384]{2,1,0:T(8,128)(2,1)S(1)} %all-to-all-done.1.w_ref, ...), custom_call_target="tpu_custom_call" | custom-call | flops 603979776 | bytes 3735552 | tf_op jit(solution)/shard_map/pallas_call | solution.py:199
  136.9 3.9 %all-to-all-start.2 = ((bf16[8,64,96]{2,1,0:T(8,128)(2,1)}), bf16[8,64,96]{2,1,0:T(8,128)(2,1)S(1)}, u32[]{:S(2)}, u32[]{:S(2)}) async-start(bf16[8,64,96]{2,1,0:T(8,128)(2,1)} %copy-done.1), calls=%async_computation.2 | async-start | bytes 262144 | tf_op jit(solution)/shard_map/all_to_all | solution.py:35
  141.4 5.1 %all-to-all-done.2.gated_ref = bf16[8,64,96]{2,1,0:T(8,128)(2,1)S(1)} async-done(((bf16[8,64,96]{2,1,0:T(8,128)(2,1)}), bf16[8,64,96]{2,1,0:T(8,128)(2,1)S(1)}, u32[]{:S(2)}, u32[]{:S(2)}) %all-to-all-start.2) | async-done | bytes 98336 | tf_op jit(solution)/shard_map/all_to_all | solution.py:35
  146.6 0.9 copy-done.3
  148.1 1.3 shard_map.147
  149.4 9.8 %all_to_all.30.x_ref = bf16[4,64,768]{2,1,0:T(8,128)(2,1)S(1)} all-to-all(bf16[4,64,768]{2,1,0:T(8,128)(2,1)S(1)} %get-tuple-element.48), channel_id=1, replica_groups={{0,1,2,3},{4,5,6,7},{8,9,10,11},{12,13,14,15},{16,17,18,19},{20,21,22,2..., dimensions={0} | all-to-all | bytes 786432 | tf_op jit(solution)/shard_map/all_to_all | solution.py:35
  160.0 9.8 %all_to_all.31.part_ref = bf16[4,64,768]{2,1,0:T(8,128)(2,1)S(1)} all-to-all(bf16[4,64,768]{2,1,0:T(8,128)(2,1)S(1)} %shard_map.148), channel_id=1, replica_groups={{0,1,2,3},{4,5,6,7},{8,9,10,11},{12,13,14,15},{16,17,18,19},{20,21,22,2..., dimensions={0} | all-to-all | bytes 786432 | tf_op jit(solution)/shard_map/all_to_all | solution.py:35
  (58 shorter events, 16.3 us)
Async XLA Ops:
  6.5 73.4 %all-gather.2.cloned.1.call-start = ((), (), s32[]{:S(2)}) async-start(), calls=%async_computation.6 | async-start | bytes 1671168 | tf_op jit(solution)/shard_map/all_gather | solution.py:246
  10.3 28.4 %all-to-all-start = ((bf16[4,12,1056]{2,1,0:T(8,128)(2,1)}), bf16[4,12,1056]{2,1,0:T(8,128)(2,1)S(1)}, u32[]{:S(2)}, u32[]{:S(2)}) async-start(bf16[4,12,1056]{2,1,0:T(8,128)(2,1)} %broadcast_in_dim.6), calls=%async_computation | async-start | bytes 294912 | tf_op jit(solution)/shard_map/all_to_all | solution.py:35
  27.4 0.5 copy-start.4
  27.9 1.0 copy-start.2
  29.0 0.7 copy-start.7
  31.9 0.6 copy-start.8
  32.5 0.6 copy-start.9
  33.1 0.6 copy-start.10
  33.7 0.6 copy-start.11
  34.3 0.6 copy-start.12
  34.9 0.6 copy-start.13
  35.5 0.6 copy-start.14
  38.9 12.3 %collective-permute-start.1 = (bf16[48,96]{1,0:T(8,128)(2,1)S(1)}, bf16[48,96]{1,0:T(8,128)(2,1)S(1)}, u32[]{:S(2)}, u32[]{:S(2)}) collective-permute-start(bf16[48,96]{1,0:T(8,128)(2,1)S(1)} %slice.54), channel_id=1, source_target_pairs={{0,2},{1,3},{2,0},{3,1},{4,6},{5,7},{6,4},{7,5},{8,10},{9,11},{10,... | collective-permute-start | bytes 27656 | tf_op jit(solution)/shard_map/ppermute | solution.py:50
  44.3 16.1 %all-to-all-start.1 = ((bf16[16,48,384]{2,1,0:T(8,128)(2,1)}), bf16[16,48,384]{2,1,0:T(8,128)(2,1)S(1)}, u32[]{:S(2)}, u32[]{:S(2)}) async-start(bf16[16,48,384]{2,1,0:T(8,128)(2,1)} %broadcast_in_dim.7), calls=%async_computation.1 | async-start | bytes 1179648 | tf_op jit(solution)/shard_map/all_to_all | solution.py:35
  51.2 6.7 %collective-permute-start.2 = (bf16[48,768]{1,0:T(8,128)(2,1)S(1)}, bf16[48,768]{1,0:T(8,128)(2,1)S(1)}, u32[]{:S(2)}, u32[]{:S(2)}) collective-permute-start(bf16[48,768]{1,0:T(8,128)(2,1)S(1)} %pad_maximum_fusion), channel_id=1, source_target_pairs={{0,4},{1,5},{2,6},{3,7},{4,0},{5,1},{6,2},{7,3},{8,12},{9,13},{10,... | collective-permute-start | bytes 221192 | tf_op jit(solution)/shard_map/ppermute | solution.py:50
  62.1 32.4 %all-to-all-start.3 = ((bf16[16,48,1536]{2,1,0:T(8,128)(2,1)}), bf16[16,48,1536]{2,1,0:T(8,128)(2,1)S(1)}, u32[]{:S(2)}, u32[]{:S(2)}) async-start(bf16[16,48,1536]{2,1,0:T(8,128)(2,1)} %broadcast_in_dim.8), calls=%async_computation.3 | async-start | bytes 4718592 | tf_op jit(solution)/shard_map/all_to_all | solution.py:35
  79.9 48.8 %collective-permute-start = (bf16[16,64,768]{2,1,0:T(8,128)(2,1)}, bf16[16,64,768]{2,1,0:T(8,128)(2,1)}, u32[]{:S(2)}, u32[]{:S(2)}) collective-permute-start(bf16[16,64,768]{2,1,0:T(8,128)(2,1)} %all-gather.2.cloned.1.call-done.x_ref), channel_id=1, source_target_pairs={{0,1},{1,0},{2,3},{3,2},{4,5},{5,4},{6,7},{7,6},{8,9},{9,8},{10,11... | collective-permute-start | bytes 4718600 | tf_op jit(solution)/shard_map/ppermute | solution.py:50
  95.4 46.1 %collective-permute-start.10 = (bf16[16,48,384]{2,1,0:T(8,128)(2,1)}, bf16[16,48,384]{2,1,0:T(8,128)(2,1)S(1)}, u32[]{:S(2)}, u32[]{:S(2)}) collective-permute-start(bf16[16,48,384]{2,1,0:T(8,128)(2,1)} %slice.64), channel_id=1, source_target_pairs={{0,1},{1,0},{2,3},{3,2},{4,5},{5,4},{6,7},{7,6},{8,9},{9,8},{10,11... | collective-permute-start | bytes 1769480 | tf_op jit(solution)/shard_map/ppermute | solution.py:50
  103.9 7.9 %collective-permute-start.3 = (f32[32,128]{1,0:T(8,128)}, f32[32,128]{1,0:T(8,128)S(1)}, u32[]{:S(2)}, u32[]{:S(2)}) collective-permute-start(f32[32,128]{1,0:T(8,128)} %copy-done.14), channel_id=1, source_target_pairs={{0,1},{1,0},{2,3},{3,2},{4,5},{5,4},{6,7},{7,6},{8,9},{9,8},{10,11... | collective-permute-start | bytes 49160 | tf_op jit(solution)/shard_map/ppermute | solution.py:50
  105.8 7.9 %collective-permute-start.4 = (f32[32,128]{1,0:T(8,128)}, f32[32,128]{1,0:T(8,128)S(1)}, u32[]{:S(2)}, u32[]{:S(2)}) collective-permute-start(f32[32,128]{1,0:T(8,128)} %copy-done.13), channel_id=1, source_target_pairs={{0,2},{1,3},{2,0},{3,1},{4,6},{5,7},{6,4},{7,5},{8,10},{9,11},{10,... | collective-permute-start | bytes 49160 | tf_op jit(solution)/shard_map/ppermute | solution.py:50
  107.8 10.1 %collective-permute-start.5 = (f32[32,128]{1,0:T(8,128)}, f32[32,128]{1,0:T(8,128)S(1)}, u32[]{:S(2)}, u32[]{:S(2)}) collective-permute-start(f32[32,128]{1,0:T(8,128)} %copy-done.12), channel_id=1, source_target_pairs={{0,3},{1,2},{2,1},{3,0},{4,7},{5,6},{6,5},{7,4},{8,11},{9,10},{10,... | collective-permute-start | bytes 49160 | tf_op jit(solution)/shard_map/ppermute | solution.py:50
  111.8 9.5 %collective-permute-start.6 = (f32[32,128]{1,0:T(8,128)}, f32[32,128]{1,0:T(8,128)S(1)}, u32[]{:S(2)}, u32[]{:S(2)}) collective-permute-start(f32[32,128]{1,0:T(8,128)} %copy-done.11), channel_id=1, source_target_pairs={{0,4},{1,5},{2,6},{3,7},{4,0},{5,1},{6,2},{7,3},{8,12},{9,13},{10,... | collective-permute-start | bytes 49160 | tf_op jit(solution)/shard_map/ppermute | solution.py:50
  113.7 12.6 %collective-permute-start.7 = (f32[32,128]{1,0:T(8,128)}, f32[32,128]{1,0:T(8,128)S(1)}, u32[]{:S(2)}, u32[]{:S(2)}) collective-permute-start(f32[32,128]{1,0:T(8,128)} %copy-done.10), channel_id=1, source_target_pairs={{0,5},{1,4},{2,7},{3,6},{4,1},{5,0},{6,3},{7,2},{8,13},{9,12},{10,... | collective-permute-start | bytes 49160 | tf_op jit(solution)/shard_map/ppermute | solution.py:50
  117.9 8.5 %collective-permute-start.8 = (f32[32,128]{1,0:T(8,128)}, f32[32,128]{1,0:T(8,128)S(1)}, u32[]{:S(2)}, u32[]{:S(2)}) collective-permute-start(f32[32,128]{1,0:T(8,128)} %copy-done.9), channel_id=1, source_target_pairs={{0,6},{1,7},{2,4},{3,5},{4,2},{5,3},{6,0},{7,1},{8,14},{9,15},{10,... | collective-permute-start | bytes 49160 | tf_op jit(solution)/shard_map/ppermute | solution.py:50
  121.2 7.4 %collective-permute-start.9 = (f32[32,128]{1,0:T(8,128)}, f32[32,128]{1,0:T(8,128)S(1)}, u32[]{:S(2)}, u32[]{:S(2)}) collective-permute-start(f32[32,128]{1,0:T(8,128)} %copy-done.8), channel_id=1, source_target_pairs={{0,7},{1,6},{2,5},{3,4},{4,3},{5,2},{6,1},{7,0},{8,15},{9,14},{10,... | collective-permute-start | bytes 49160 | tf_op jit(solution)/shard_map/ppermute | solution.py:50
  128.7 1.4 copy-start
  130.1 0.6 copy-start.5
  136.2 0.7 copy-start.1
  136.9 9.7 %all-to-all-start.2 = ((bf16[8,64,96]{2,1,0:T(8,128)(2,1)}), bf16[8,64,96]{2,1,0:T(8,128)(2,1)S(1)}, u32[]{:S(2)}, u32[]{:S(2)}) async-start(bf16[8,64,96]{2,1,0:T(8,128)(2,1)} %copy-done.1), calls=%async_computation.2 | async-start | bytes 262144 | tf_op jit(solution)/shard_map/all_to_all | solution.py:35
  146.6 0.9 copy-start.3
  147.4 0.6 copy-start.6
Sparse Core Ops, SparseCore 0:
  9.4 70.4 all-gather.1

commit v2 on v1

--- a/solution.py
+++ b/solution.py
@@ -16,6 +16,7 @@
 f32 = jnp.float32
 bf16 = jnp.bfloat16
 VMEM_LIMIT = 48 * 1024 * 1024
+MOST_VMEM = 62 * 1024 * 1024
 
 
 def layer_norm(inputs, scale_gain):
@@ -50,12 +51,12 @@
     return lax.ppermute(block, axis, [(i, i ^ flip) for i in range(count)])
 
 
-def bias_kernel(info_ref, x_ref, gain_ref, proj_ref, *refs):
+def bias_kernel(x_ref, gain_ref, proj_ref, *refs):
     out_refs, rows, held = refs[:-2], refs[-2], refs[-1]
     queries, keys, channels = x_ref.shape
     pairs = len(out_refs)
     normed = layer_norm(
-        x_ref[...].reshape(queries * keys, channels).astype(f32), gain_ref[...]
+        x_ref[...].reshape(queries * keys, channels).astype(f32), gain_ref[...].reshape(1, -1)
     )
     rows[...] = normed
     together = 256 // queries
@@ -69,10 +70,10 @@
             tile = jnp.concatenate([bias[:pairs, cols], bias[pairs:, cols]], axis=1)
             held[:, start + j, :] = tile
     for flip, out_ref in enumerate(out_refs):
-        out_ref[...] = held[info_ref[1] ^ flip]
-
-
-def attention_kernel(feats, info_ref, x_ref, other_ref, gain_ref, w_ref, *refs):
+        out_ref[...] = held[lax.axis_index("ka") ^ flip]
+
+
+def attention_kernel(feats, length_ref, x_ref, other_ref, gain_ref, w_ref, *refs):
     count = len(refs) - 5
     bias_refs = refs[:count]
     out_ref, held_normed, held_bias, held_query, held_gate = refs[count:]
@@ -85,14 +86,14 @@
     samples = own_rows // each
     key_count = blocks * q_rows
     head_dim = feats // 2
-    length, at, block_at = info_ref[0], info_ref[1], info_ref[2]
+    length, at, block_at = length_ref[0], lax.axis_index("ka"), lax.axis_index("pb")
     core = at % 2
     weights = w_ref[...].reshape(width, 4 * feats)
     w_kv, w_qg = weights[:, : 2 * feats], weights[:, 2 * feats :]
     key_value = []
     for side, ref in enumerate((x_ref, other_ref)):
         x = ref[...].reshape(places * own_rows, width).astype(f32)
-        normed = layer_norm(x, gain_ref[...]).astype(bf16)
+        normed = layer_norm(x, gain_ref[...].reshape(1, -1)).astype(bf16)
         held_normed[side] = normed.reshape(places, own_rows, width)
         proj = jnp.dot(normed, w_kv, preferred_element_type=f32)
         key_value.append(proj.reshape(places, samples, each, 2 * feats))
@@ -154,12 +155,12 @@
 
 
 def mix_kernel(
-    info_ref, gated_ref, w_ref, other_ref, single_ref, gain_ref, mixed_ref, normed_ref, held
+    gated_ref, w_ref, other_ref, single_ref, gain_ref, mixed_ref, normed_ref, held
 ):
     ka_count, rows, feats = gated_ref.shape
     width = single_ref.shape[1]
     chips = ka_count // 2
-    at = info_ref[1]
+    at = lax.axis_index("ka")
     gated = jnp.concatenate([gated_ref[k] for k in range(ka_count)], axis=1)
     for side, ref in enumerate((w_ref, other_ref)):
         weights = ref[:, :, ref.shape[2] - chips * feats :].reshape(width, chips * feats)
@@ -169,7 +170,7 @@
     added = jnp.concatenate([held[k] for k in range(ka_count)], axis=1)
     mixed = (single_ref[...].astype(f32) + added).astype(bf16)
     mixed_ref[...] = mixed
-    normed = layer_norm(mixed.astype(f32), gain_ref[...]).astype(bf16)
+    normed = layer_norm(mixed.astype(f32), gain_ref[...].reshape(1, -1)).astype(bf16)
     for i in range(normed_ref.shape[0]):
         normed_ref[i] = normed
 
@@ -194,7 +195,7 @@
     out_ref[...] = total.astype(bf16)
 
 
-def call(kernel, out_shape, scratch=(), scalars=0, flops=0, moved=0):
+def call(kernel, out_shape, scratch=(), scalars=0, flops=0, moved=0, limit=VMEM_LIMIT):
     def run(*operands):
         return pl.pallas_call(
             kernel,
@@ -204,7 +205,7 @@
                 for i in range(len(operands))
             ],
             scratch_shapes=list(scratch),
-            compiler_params=pltpu.CompilerParams(vmem_limit_bytes=VMEM_LIMIT),
+            compiler_params=pltpu.CompilerParams(vmem_limit_bytes=limit),
             cost_estimate=pl.CostEstimate(flops=flops, bytes_accessed=moved, transcendentals=0),
         )(*operands)
 
@@ -239,12 +240,10 @@
     own_rows = samples * row_count
     chips = ka_count // 2
     held = ka_count // TP
-    info = jnp.stack([lengths[0], ka_index, lax.axis_index("pb")]).astype(jnp.int32)
     own = single.reshape(own_rows, width)
 
     line = [[i * 2 + c for i in range(pb_count * chips)] for c in range(2)]
     x = lax.all_gather(own, ("pb", "ka"), axis=0, tiled=False, axis_index_groups=line)
-    other = swap(x, "ka", 1)
 
     early = [
         lax.dynamic_slice_in_dim(w, ka_index * feats, feats, 1)
@@ -252,19 +251,7 @@
     ]
     early = jnp.concatenate(early + [w_down.T, w_swish, w_up, w_out], axis=1)
     early, pair_rep = lax.optimization_barrier((early, pair_rep))
-    early = spread(early, pb_count, "pb").reshape(pb_count * w_rows, early.shape[1])
-
-    attn_w = spread(early[:, : 4 * feats], grp_count, "grp")
-
-    out_w = early[:, 4 * feats + 3 * hid :]
-    out_w = [out_w] + [swap(out_w, "ka", 2)]
-    late = jnp.concatenate([early[:, 4 * feats : 4 * feats + 3 * hid]] + out_w, axis=1)
-    late = [late] + [swap(late, "ka", TP)]
-    late = jnp.concatenate(
-        [w[:, i * hid : (i + 1) * hid] for i in range(3) for w in late]
-        + [w[:, 3 * hid :] for w in late],
-        axis=1,
-    )
+    early = spread(early, pb_count, "pb")
 
     _, queries, key_blocks, key_rows, channels = pair_rep.shape
     keys_held = key_blocks * key_rows
@@ -277,13 +264,31 @@
             pltpu.VMEM((queries * keys_held, channels), f32),
             pltpu.VMEM((ka_count, keys_held, lanes), f32),
         ],
-        scalars=1,
         flops=2 * 6 * queries * keys_held * channels * HEADS,
         moved=queries * keys_held * channels * 2 + 4 * ka_count * keys_held * lanes,
-    )(info, pair_rep.reshape(queries, keys_held, channels), pair_gain.reshape(1, channels), proj)
-    late, attn_w, bias = lax.optimization_barrier((late, attn_w, list(bias)))
+    )(pair_rep.reshape(queries, keys_held, channels), pair_gain, proj)
+    near = [swap(bias[i], "ka", i) for i in (1, 2)]
+    early, near = lax.optimization_barrier((early, near))
+    early = early.reshape(pb_count * w_rows, early.shape[2])
+
+    attn_w = spread(early[:, : 4 * feats], grp_count, "grp")
+
+    out_w = early[:, 4 * feats + 3 * hid :]
+    out_w = [out_w] + [swap(out_w, "ka", 2)]
+    late = jnp.concatenate([early[:, 4 * feats : 4 * feats + 3 * hid]] + out_w, axis=1)
+    late = [late] + [swap(late, "ka", TP)]
+    late = jnp.concatenate(
+        [w[:, i * hid : (i + 1) * hid] for i in range(3) for w in late]
+        + [w[:, 3 * hid :] for w in late],
+        axis=1,
+    )
+
+    late, attn_w, far = lax.optimization_barrier((late, attn_w, list(bias[3:])))
     late = spread(late, grp_count, "grp")
-    bias = [bias[0]] + [swap(bias[i], "ka", i) for i in range(1, ka_count)]
+    far = [swap(block, "ka", i + 3) for i, block in enumerate(far)]
+    x, far = lax.optimization_barrier((x, far))
+    other = swap(x, "ka", 1)
+    bias = [bias[0]] + near + far
 
     gated = call(
         functools.partial(attention_kernel, feats),
@@ -297,7 +302,9 @@
         scalars=1,
         flops=4 * x.size * 2 * feats,
         moved=x.size * 4 + attn_w.size * 2,
-    )(info, x, other, attn_gain.reshape(1, width), attn_w, *bias)
+        limit=MOST_VMEM,
+    )(lengths, x, other, attn_gain, attn_w, *bias)
+    gated, late = lax.optimization_barrier((gated, late))
     gated = exchange(gated, "ka")
     out_w = swap(late[:, :, held * 3 * hid :], "ka", 1)
 
@@ -307,10 +314,9 @@
         mix_kernel,
         (rows, shared),
         scratch=[pltpu.VMEM((ka_count, own_rows, feats), f32)],
-        scalars=1,
         flops=2 * own_rows * width * width,
         moved=width * width * 2,
-    )(info, gated, late, out_w, own, trans_gain.reshape(1, width))
+    )(gated, late, out_w, own, trans_gain)
 
     groups = [list(range(i, i + TP)) for i in range(0, ka_count, TP)]
     normed_t = exchange(normed_t, "ka", groups)

time: 179 us -> 150 us (0.84)
  waiting for transfers between devices: 33.7 us -> 16.4 us
  starting transfers between devices: 79.3 us -> 63.5 us
  blocking collectives: 19.6 us -> 29.1 us
  local copies, waits for them, and re-layouts: 19.6 us -> 11.3 us
  Pallas kernels: 10.6 us -> 14.3 us
    all_gather x1, waiting for transfers between devices: 12.9 us -> 0.01 us  [on_device(): lax.all_gather(own, ('pb', 'ka'), axis=0, tiled=False, axis_index_groups=...]
    ppermute x11, starting transfers between devices: 48.1 us -> 36.2 us  [swap(): return lax.ppermute(block, axis, [(i, i ^ flip) for i in range(count)])]
    all_to_all x4 -> x3, waiting for transfers between devices: 13.5 us -> 2.57 us  [exchange(): lax.all_to_all(blocks, axes, split_axis=0, concat_axis=0, tiled=True, axi...]
    all_to_all x2 -> x3, blocking collectives: 19.6 us -> 29.1 us  [exchange(): lax.all_to_all(blocks, axes, split_axis=0, concat_axis=0, tiled=True, axi...]
    unnamed x30 -> x28, local copies, waits for them, and re-layouts: 10.6 us -> 3.47 us
    ppermute x11, waiting for transfers between devices: 6.63 us -> 13.2 us  [swap(): return lax.ppermute(block, axis, [(i, i ^ flip) for i in range(count)])]
    all_to_all x4 -> x3, starting transfers between devices: 31.2 us -> 27.3 us  [exchange(): lax.all_to_all(blocks, axes, split_axis=0, concat_axis=0, tiled=True, axi...]
    pallas_call x5, Pallas kernels: 10.6 us -> 14.3 us  [run(): pl.pallas_call(kernel, out_shape=out_shape, in_specs=[pl.BlockSpec(memory...]
  transfers between devices with their start and end apart: 16 -> 15, of which waited for: 7 -> 6; matrix products, arithmetic and copies ran while one was open for 5% -> 5% of each run, Pallas kernels for 4% -> 6%
where the time goes in v2:
time: 150 us; the launch traced here: 149 us
  starting transfers between devices  63.5 us (42%)
  blocking collectives  29.1 us (19%)
  waiting for transfers between devices  16.4 us (11%)
  Pallas kernels  14.3 us (10%)
  between operations  14.3 us (10%)
  local copies, waits for them, and re-layouts  11.3 us (8%)
    ppermute x11, starting transfers between devices, swap(): return lax.ppermute(block, axis, [(i, i ^ flip) for i in range(count)])  36.2 us
    all_to_all x3, blocking collectives, exchange(): lax.all_to_all(blocks, axes, split_axis=0, concat_axis=0, tiled=True, axi...  29.1 us
    all_to_all x3, starting transfers between devices, exchange(): lax.all_to_all(blocks, axes, split_axis=0, concat_axis=0, tiled=True, axi...  27.3 us
    pallas_call x5, Pallas kernels, run(): pl.pallas_call(kernel, out_shape=out_shape, in_specs=[pl.BlockSpec(memory...  14.3 us
    ppermute x11, waiting for transfers between devices, swap(): return lax.ppermute(block, axis, [(i, i ^ flip) for i in range(count)])  13.2 us
    unnamed x28, local copies, waits for them, and re-layouts  3.47 us
    broadcast_in_dim x3, local copies, waits for them, and re-layouts, spread(): return exchange(jnp.broadcast_to(block[None], (count,) + block.shape), axes)  3.2 us
  transfers between devices with their start and end apart: 15, of which 6 were waited for; matrix products, arithmetic and copies ran while one was open for 5% of the time, Pallas kernels for 6%

profile of v2, /device:TPU:1, one launch (start us, length us, event | category | flops | bytes accessed | tf_op | source)
XLA Modules:
  0.0 149.1 jit_solution(3913834528744463337)
XLA Ops:
  8.8 0.8 concatenate.10
  10.4 15.6 %all-to-all-start = ((bf16[4,12,1056]{2,1,0:T(8,128)(2,1)}), bf16[4,12,1056]{2,1,0:T(8,128)(2,1)S(1)}, u32[]{:S(2)}, u32[]{:S(2)}) async-start(bf16[4,12,1056]{2,1,0:T(8,128)(2,1)} %broadcast_in_dim.6), calls=%async_computation | async-start | bytes 294912 | tf_op jit(solution)/shard_map/all_to_all | solution.py:36
  26.7 1.0 copy-done
  28.4 1.8 %shard_map.145 = (f32[32,128]{1,0:T(8,128)S(1)}, f32[32,128]{1,0:T(8,128)S(1)}, f32[32,128]{1,0:T(8,128)S(1)}, f32[32,128]{1,0:T(8,128)S(1)}, f32[32,128]{1,0:T(...) custom-call(bf16[64,32,128]{2,1,0:T(8,128)(2,1)S(1)} %bitcast.11, ...), custom_call_target="tpu_custom_call" | custom-call | flops 50331648 | bytes 655360 | tf_op jit(solution)/shard_map/pallas_call | solution.py:200
  30.7 2.9 %collective-permute-start = (f32[32,128]{1,0:T(8,128)S(1)}, f32[32,128]{1,0:T(8,128)S(1)}, u32[]{:S(2)}, u32[]{:S(2)}) collective-permute-start(f32[32,128]{1,0:T(8,128)S(1)} %get-tuple-element.37), channel_id=1, source_target_pairs={{0,1},{1,0},{2,3},{3,2},{4,5},{5,4},{6,7},{7,6},{8,9},{9,8},{10,11... | collective-permute-start | bytes 49160 | tf_op jit(solution)/shard_map/ppermute | solution.py:51
  33.6 2.6 %collective-permute-start.1 = (f32[32,128]{1,0:T(8,128)S(1)}, f32[32,128]{1,0:T(8,128)S(1)}, u32[]{:S(2)}, u32[]{:S(2)}) collective-permute-start(f32[32,128]{1,0:T(8,128)S(1)} %get-tuple-element.38), channel_id=1, source_target_pairs={{0,2},{1,3},{2,0},{3,1},{4,6},{5,7},{6,4},{7,5},{8,10},{9,11},{10,... | collective-permute-start | bytes 49160 | tf_op jit(solution)/shard_map/ppermute | solution.py:51
  36.3 2.2 %collective-permute-done.1.refs_2_ = f32[32,128]{1,0:T(8,128)S(1)} collective-permute-done((f32[32,128]{1,0:T(8,128)S(1)}, f32[32,128]{1,0:T(8,128)S(1)}, u32[]{:S(2)}, u32[]{:S(2)}) %collective-permute-start.1) | collective-permute-done | bytes 16416 | tf_op jit(solution)/shard_map/ppermute | solution.py:51
  38.9 4.6 %collective-permute-start.2 = (bf16[48,96]{1,0:T(8,128)(2,1)S(1)}, bf16[48,96]{1,0:T(8,128)(2,1)S(1)}, u32[]{:S(2)}, u32[]{:S(2)}) collective-permute-start(bf16[48,96]{1,0:T(8,128)(2,1)S(1)} %slice.54), channel_id=1, source_target_pairs={{0,2},{1,3},{2,0},{3,1},{4,6},{5,7},{6,4},{7,5},{8,10},{9,11},{10,... | collective-permute-start | bytes 27656 | tf_op jit(solution)/shard_map/ppermute | solution.py:51
  43.4 0.9 broadcast_in_dim.7
  44.3 6.7 %all-to-all-start.1 = ((bf16[16,48,384]{2,1,0:T(8,128)(2,1)}), bf16[16,48,384]{2,1,0:T(8,128)(2,1)S(1)}, u32[]{:S(2)}, u32[]{:S(2)}) async-start(bf16[16,48,384]{2,1,0:T(8,128)(2,1)} %broadcast_in_dim.7), calls=%async_computation.1 | async-start | bytes 1179648 | tf_op jit(solution)/shard_map/all_to_all | solution.py:36
  51.2 2.4 %collective-permute-start.3 = (bf16[48,768]{1,0:T(8,128)(2,1)S(1)}, bf16[48,768]{1,0:T(8,128)(2,1)S(1)}, u32[]{:S(2)}, u32[]{:S(2)}) collective-permute-start(bf16[48,768]{1,0:T(8,128)(2,1)S(1)} %pad_maximum_fusion), channel_id=1, source_target_pairs={{0,4},{1,5},{2,6},{3,7},{4,0},{5,1},{6,2},{7,3},{8,12},{9,13},{10,... | collective-permute-start | bytes 221192 | tf_op jit(solution)/shard_map/ppermute | solution.py:51
  53.7 4.2 %collective-permute-done.3 = bf16[48,768]{1,0:T(8,128)(2,1)S(1)} collective-permute-done((bf16[48,768]{1,0:T(8,128)(2,1)S(1)}, bf16[48,768]{1,0:T(8,128)(2,1)S(1)}, u32[]{:S(2)}, u32[]{:S(2)}) %collective-permute-start.3) | collective-permute-done | bytes 73760 | tf_op jit(solution)/shard_map/ppermute | solution.py:51
  58.1 2.3 %all-to-all-done.1.w_ref = bf16[16,48,384]{2,1,0:T(8,128)(2,1)S(1)} async-done(((bf16[16,48,384]{2,1,0:T(8,128)(2,1)}), bf16[16,48,384]{2,1,0:T(8,128)(2,1)S(1)}, u32[]{:S(2)}, u32[]{:S(2)}) %all-to-all-start.1) | async-done | bytes 589856 | tf_op jit(solution)/shard_map/all_to_all | solution.py:36
  60.5 1.7 %broadcast_in_dim.8 = bf16[16,48,1536]{2,1,0:T(8,128)(2,1)} broadcast(bf16[48,1536]{1,0:T(8,128)(2,1)S(1)} %concatenate.12), dimensions={1,2} | broadcast | bytes 2506752 | tf_op jit(solution)/shard_map/broadcast_in_dim | solution.py:42
  62.1 4.9 %all-to-all-start.2 = ((bf16[16,48,1536]{2,1,0:T(8,128)(2,1)}), bf16[16,48,1536]{2,1,0:T(8,128)(2,1)}, u32[]{:S(2)}, u32[]{:S(2)}) async-start(bf16[16,48,1536]{2,1,0:T(8,128)(2,1)} %broadcast_in_dim.8), calls=%async_computation.2 | async-start | bytes 4718592 | tf_op jit(solution)/shard_map/all_to_all | solution.py:36
  67.1 5.8 %collective-permute-start.4 = (f32[32,128]{1,0:T(8,128)S(1)}, f32[32,128]{1,0:T(8,128)S(1)}, u32[]{:S(2)}, u32[]{:S(2)}) collective-permute-start(f32[32,128]{1,0:T(8,128)S(1)} %get-tuple-element.45), channel_id=1, source_target_pairs={{0,3},{1,2},{2,1},{3,0},{4,7},{5,6},{6,5},{7,4},{8,11},{9,10},{10,... | collective-permute-start | bytes 49160 | tf_op jit(solution)/shard_map/ppermute | solution.py:51
  72.8 4.5 %collective-permute-start.5 = (f32[32,128]{1,0:T(8,128)S(1)}, f32[32,128]{1,0:T(8,128)S(1)}, u32[]{:S(2)}, u32[]{:S(2)}) collective-permute-start(f32[32,128]{1,0:T(8,128)S(1)} %get-tuple-element.46), channel_id=1, source_target_pairs={{0,4},{1,5},{2,6},{3,7},{4,0},{5,1},{6,2},{7,3},{8,12},{9,13},{10,... | collective-permute-start | bytes 49160 | tf_op jit(solution)/shard_map/ppermute | solution.py:51
  77.3 2.7 %collective-permute-start.6 = (f32[32,128]{1,0:T(8,128)S(1)}, f32[32,128]{1,0:T(8,128)S(1)}, u32[]{:S(2)}, u32[]{:S(2)}) collective-permute-start(f32[32,128]{1,0:T(8,128)S(1)} %get-tuple-element.47), channel_id=1, source_target_pairs={{0,5},{1,4},{2,7},{3,6},{4,1},{5,0},{6,3},{7,2},{8,13},{9,12},{10,... | collective-permute-start | bytes 49160 | tf_op jit(solution)/shard_map/ppermute | solution.py:51
  80.0 3.5 %collective-permute-start.7 = (f32[32,128]{1,0:T(8,128)S(1)}, f32[32,128]{1,0:T(8,128)S(1)}, u32[]{:S(2)}, u32[]{:S(2)}) collective-permute-start(f32[32,128]{1,0:T(8,128)S(1)} %get-tuple-element.48), channel_id=1, source_target_pairs={{0,6},{1,7},{2,4},{3,5},{4,2},{5,3},{6,0},{7,1},{8,14},{9,15},{10,... | collective-permute-start | bytes 49160 | tf_op jit(solution)/shard_map/ppermute | solution.py:51
  83.5 3.4 %collective-permute-start.8 = (f32[32,128]{1,0:T(8,128)S(1)}, f32[32,128]{1,0:T(8,128)S(1)}, u32[]{:S(2)}, u32[]{:S(2)}) collective-permute-start(f32[32,128]{1,0:T(8,128)S(1)} %get-tuple-element.49), channel_id=1, source_target_pairs={{0,7},{1,6},{2,5},{3,4},{4,3},{5,2},{6,1},{7,0},{8,15},{9,14},{10,... | collective-permute-start | bytes 49160 | tf_op jit(solution)/shard_map/ppermute | solution.py:51
  87.0 3.8 %collective-permute-done.8.refs_7_ = f32[32,128]{1,0:T(8,128)S(1)} collective-permute-done((f32[32,128]{1,0:T(8,128)S(1)}, f32[32,128]{1,0:T(8,128)S(1)}, u32[]{:S(2)}, u32[]{:S(2)}) %collective-permute-start.8) | collective-permute-done | bytes 16416 | tf_op jit(solution)/shard_map/ppermute | solution.py:51
  90.8 1.9 %collective-permute-start.9 = (bf16[16,64,768]{2,1,0:T(8,128)(2,1)}, bf16[16,64,768]{2,1,0:T(8,128)(2,1)S(1)}, u32[]{:S(2)}, u32[]{:S(2)}) collective-permute-start(bf16[16,64,768]{2,1,0:T(8,128)(2,1)} %all-gather.2.cloned.1.call-done.x_ref), channel_id=1, source_target_pairs={{0,1},{1,0},{2,3},{3,2},{4,5},{5,4},{6,7},{7,6},{8,9},{9,8},{10,11... | collective-permute-start | bytes 4718600 | tf_op jit(solution)/shard_map/ppermute | solution.py:51
  93.3 2.9 %collective-permute-done.9.other_ref = bf16[16,64,768]{2,1,0:T(8,128)(2,1)S(1)} collective-permute-done((bf16[16,64,768]{2,1,0:T(8,128)(2,1)}, bf16[16,64,768]{2,1,0:T(8,128)(2,1)S(1)}, u32[]{:S(2)}, u32[]{:S(2)}) %collective-permute-start.9) | collective-permute-done | bytes 1572896 | tf_op jit(solution)/shard_map/ppermute | solution.py:51
  96.3 1.1 copy-done.6
  97.5 6.9 %shard_map.146 = bf16[8,64,96]{2,1,0:T(8,128)(2,1)} custom-call(s32[1]{0:T(128)S(6)} %copy.21.length_ref, bf16[16,64,768]{2,1,0:T(8,128)(2,1)} %all-gather.2.cloned.1.call-done.x_ref, bf16[16,64,768]{2,1,0:T(8,128)(2,1)} %copy-done.6, f32[768]{0:T(1024)} %gain_ref.4, bf16[16,48,384]{2,1,0:T(8,128)(2,1)} %copy-done.5, f32[32,128]{1,0:T(8,128)} %copy-done.2, ...), custom_call_target="tpu_custom_call" | custom-call | flops 603979776 | bytes 3735552 | tf_op jit(solution)/shard_map/pallas_call | solution.py:200
  104.3 1.1 slice.51
  105.5 2.1 %collective-permute-start.10 = (bf16[16,48,384]{2,1,0:T(8,128)(2,1)S(1)}, bf16[16,48,384]{2,1,0:T(8,128)(2,1)S(1)}, u32[]{:S(2)}, u32[]{:S(2)}) collective-permute-start(bf16[16,48,384]{2,1,0:T(8,128)(2,1)S(1)} %slice.51), channel_id=1, source_target_pairs={{0,1},{1,0},{2,3},{3,2},{4,5},{5,4},{6,7},{7,6},{8,9},{9,8},{10,11... | collective-permute-start | bytes 1769480 | tf_op jit(solution)/shard_map/ppermute | solution.py:51
  107.5 9.5 %all_to_all.30.gated_ref = bf16[8,64,96]{2,1,0:T(8,128)(2,1)S(1)} all-to-all(bf16[8,64,96]{2,1,0:T(8,128)(2,1)} %shard_map.146), channel_id=1, replica_groups=mesh['grp'=16,'pb'=4,'ka'=8] {'ka'}, dimensions={0} | all-to-all | bytes 196608 | tf_op jit(solution)/shard_map/all_to_all | solution.py:36
  117.0 2.4 %shard_map.147 = (bf16[64,768]{1,0:T(8,128)(2,1)S(1)}, bf16[4,64,768]{2,1,0:T(8,128)(2,1)S(1)}) custom-call(bf16[8,64,96]{2,1,0:T(8,128)(2,1)S(1)} %all_to_all.30.gated_ref, bf16[16,48,1536]{2,1,0:T(8,128)(2,1)} %all-to-all-done.2.w_ref, bf16[16,48,384]{2,1,0:T(8,128)(2,1)S(1)} %collective-permute-done.10.other_ref, bf16[64,768]{1,0:T(8,128)(2,1)S(1)} %bitcast.13, ...), custom_call_target="tpu_custom_call" | custom-call | flops 75497472 | bytes 1179648 | tf_op jit(solution)/shard_map/pallas_call | solution.py:200
  119.4 9.8 %all_to_all.31.x_ref = bf16[4,64,768]{2,1,0:T(8,128)(2,1)S(1)} all-to-all(bf16[4,64,768]{2,1,0:T(8,128)(2,1)S(1)} %get-tuple-element.64), channel_id=1, replica_groups={{0,1,2,3},{4,5,6,7},{8,9,10,11},{12,13,14,15},{16,17,18,19},{20,21,22,2..., dimensions={0} | all-to-all | bytes 786432 | tf_op jit(solution)/shard_map/all_to_all | solution.py:36
  129.2 2.5 %shard_map.148 = bf16[4,64,768]{2,1,0:T(8,128)(2,1)S(1)} custom-call(bf16[4,64,768]{2,1,0:T(8,128)(2,1)S(1)} %all_to_all.31.x_ref, bf16[16,48,1536]{2,1,0:T(8,128)(2,1)} %all-to-all-done.2.w_ref), custom_call_target="tpu_custom_call" | custom-call | flops 452984832 | bytes 1769472 | tf_op jit(solution)/shard_map/pallas_call | solution.py:200
  131.7 9.8 %all_to_all.32.part_ref = bf16[4,64,768]{2,1,0:T(8,128)(2,1)S(1)} all-to-all(bf16[4,64,768]{2,1,0:T(8,128)(2,1)S(1)} %shard_map.148), channel_id=1, replica_groups={{0,1,2,3},{4,5,6,7},{8,9,10,11},{12,13,14,15},{16,17,18,19},{20,21,22,2..., dimensions={0} | all-to-all | bytes 786432 | tf_op jit(solution)/shard_map/all_to_all | solution.py:36
  (52 shorter events, 6.5 us)
Async XLA Ops:
  6.5 84.2 %all-gather.2.cloned.1.call-start = ((), (), s32[]{:S(2)}) async-start(), calls=%async_computation.6 | async-start | bytes 1671168 | tf_op jit(solution)/shard_map/all_gather | solution.py:246
  10.4 28.4 %all-to-all-start = ((bf16[4,12,1056]{2,1,0:T(8,128)(2,1)}), bf16[4,12,1056]{2,1,0:T(8,128)(2,1)S(1)}, u32[]{:S(2)}, u32[]{:S(2)}) async-start(bf16[4,12,1056]{2,1,0:T(8,128)(2,1)} %broadcast_in_dim.6), calls=%async_computation | async-start | bytes 294912 | tf_op jit(solution)/shard_map/all_to_all | solution.py:36
  26.7 1.0 copy-start
  27.7 0.7 copy-start.4
  30.1 0.6 copy-start.2
  30.7 5.5 %collective-permute-start = (f32[32,128]{1,0:T(8,128)S(1)}, f32[32,128]{1,0:T(8,128)S(1)}, u32[]{:S(2)}, u32[]{:S(2)}) collective-permute-start(f32[32,128]{1,0:T(8,128)S(1)} %get-tuple-element.37), channel_id=1, source_target_pairs={{0,1},{1,0},{2,3},{3,2},{4,5},{5,4},{6,7},{7,6},{8,9},{9,8},{10,11... | collective-permute-start | bytes 49160 | tf_op jit(solution)/shard_map/ppermute | solution.py:51
  33.6 4.9 %collective-permute-start.1 = (f32[32,128]{1,0:T(8,128)S(1)}, f32[32,128]{1,0:T(8,128)S(1)}, u32[]{:S(2)}, u32[]{:S(2)}) collective-permute-start(f32[32,128]{1,0:T(8,128)S(1)} %get-tuple-element.38), channel_id=1, source_target_pairs={{0,2},{1,3},{2,0},{3,1},{4,6},{5,7},{6,4},{7,5},{8,10},{9,11},{10,... | collective-permute-start | bytes 49160 | tf_op jit(solution)/shard_map/ppermute | solution.py:51
  36.3 25.8 %copy-start.7 = (f32[32,128]{1,0:T(8,128)}, f32[32,128]{1,0:T(8,128)S(1)}, u32[]{:S(2)}) copy-start(f32[32,128]{1,0:T(8,128)S(1)} %collective-permute-done.refs_1_) | copy-start | bytes 49156
  38.5 23.6 %copy-start.8 = (f32[32,128]{1,0:T(8,128)}, f32[32,128]{1,0:T(8,128)S(1)}, u32[]{:S(2)}) copy-start(f32[32,128]{1,0:T(8,128)S(1)} %collective-permute-done.1.refs_2_) | copy-start | bytes 49156
  38.9 12.3 %collective-permute-start.2 = (bf16[48,96]{1,0:T(8,128)(2,1)S(1)}, bf16[48,96]{1,0:T(8,128)(2,1)S(1)}, u32[]{:S(2)}, u32[]{:S(2)}) collective-permute-start(bf16[48,96]{1,0:T(8,128)(2,1)S(1)} %slice.54), channel_id=1, source_target_pairs={{0,2},{1,3},{2,0},{3,1},{4,6},{5,7},{6,4},{7,5},{8,10},{9,11},{10,... | collective-permute-start | bytes 27656 | tf_op jit(solution)/shard_map/ppermute | solution.py:51
  44.3 16.1 %all-to-all-start.1 = ((bf16[16,48,384]{2,1,0:T(8,128)(2,1)}), bf16[16,48,384]{2,1,0:T(8,128)(2,1)S(1)}, u32[]{:S(2)}, u32[]{:S(2)}) async-start(bf16[16,48,384]{2,1,0:T(8,128)(2,1)} %broadcast_in_dim.7), calls=%async_computation.1 | async-start | bytes 1179648 | tf_op jit(solution)/shard_map/all_to_all | solution.py:36
  51.2 6.7 %collective-permute-start.3 = (bf16[48,768]{1,0:T(8,128)(2,1)S(1)}, bf16[48,768]{1,0:T(8,128)(2,1)S(1)}, u32[]{:S(2)}, u32[]{:S(2)}) collective-permute-start(bf16[48,768]{1,0:T(8,128)(2,1)S(1)} %pad_maximum_fusion), channel_id=1, source_target_pairs={{0,4},{1,5},{2,6},{3,7},{4,0},{5,1},{6,2},{7,3},{8,12},{9,13},{10,... | collective-permute-start | bytes 221192 | tf_op jit(solution)/shard_map/ppermute | solution.py:51
  60.5 1.7 %copy-start.5 = (bf16[16,48,384]{2,1,0:T(8,128)(2,1)}, bf16[16,48,384]{2,1,0:T(8,128)(2,1)S(1)}, u32[]{:S(2)}) copy-start(bf16[16,48,384]{2,1,0:T(8,128)(2,1)S(1)} %all-to-all-done.1.w_ref) | copy-start | bytes 1769476
  62.1 42.2 %all-to-all-start.2 = ((bf16[16,48,1536]{2,1,0:T(8,128)(2,1)}), bf16[16,48,1536]{2,1,0:T(8,128)(2,1)}, u32[]{:S(2)}, u32[]{:S(2)}) async-start(bf16[16,48,1536]{2,1,0:T(8,128)(2,1)} %broadcast_in_dim.8), calls=%async_computation.2 | async-start | bytes 4718592 | tf_op jit(solution)/shard_map/all_to_all | solution.py:36
  67.1 19.8 %collective-permute-start.4 = (f32[32,128]{1,0:T(8,128)S(1)}, f32[32,128]{1,0:T(8,128)S(1)}, u32[]{:S(2)}, u32[]{:S(2)}) collective-permute-start(f32[32,128]{1,0:T(8,128)S(1)} %get-tuple-element.45), channel_id=1, source_target_pairs={{0,3},{1,2},{2,1},{3,0},{4,7},{5,6},{6,5},{7,4},{8,11},{9,10},{10,... | collective-permute-start | bytes 49160 | tf_op jit(solution)/shard_map/ppermute | solution.py:51
  72.8 14.1 %collective-permute-start.5 = (f32[32,128]{1,0:T(8,128)S(1)}, f32[32,128]{1,0:T(8,128)S(1)}, u32[]{:S(2)}, u32[]{:S(2)}) collective-permute-start(f32[32,128]{1,0:T(8,128)S(1)} %get-tuple-element.46), channel_id=1, source_target_pairs={{0,4},{1,5},{2,6},{3,7},{4,0},{5,1},{6,2},{7,3},{8,12},{9,13},{10,... | collective-permute-start | bytes 49160 | tf_op jit(solution)/shard_map/ppermute | solution.py:51
  77.3 9.6 %collective-permute-start.6 = (f32[32,128]{1,0:T(8,128)S(1)}, f32[32,128]{1,0:T(8,128)S(1)}, u32[]{:S(2)}, u32[]{:S(2)}) collective-permute-start(f32[32,128]{1,0:T(8,128)S(1)} %get-tuple-element.47), channel_id=1, source_target_pairs={{0,5},{1,4},{2,7},{3,6},{4,1},{5,0},{6,3},{7,2},{8,13},{9,12},{10,... | collective-permute-start | bytes 49160 | tf_op jit(solution)/shard_map/ppermute | solution.py:51
  80.0 7.0 %collective-permute-start.7 = (f32[32,128]{1,0:T(8,128)S(1)}, f32[32,128]{1,0:T(8,128)S(1)}, u32[]{:S(2)}, u32[]{:S(2)}) collective-permute-start(f32[32,128]{1,0:T(8,128)S(1)} %get-tuple-element.48), channel_id=1, source_target_pairs={{0,6},{1,7},{2,4},{3,5},{4,2},{5,3},{6,0},{7,1},{8,14},{9,15},{10,... | collective-permute-start | bytes 49160 | tf_op jit(solution)/shard_map/ppermute | solution.py:51
  83.5 7.3 %collective-permute-start.8 = (f32[32,128]{1,0:T(8,128)S(1)}, f32[32,128]{1,0:T(8,128)S(1)}, u32[]{:S(2)}, u32[]{:S(2)}) collective-permute-start(f32[32,128]{1,0:T(8,128)S(1)} %get-tuple-element.49), channel_id=1, source_target_pairs={{0,7},{1,6},{2,5},{3,4},{4,3},{5,2},{6,1},{7,0},{8,15},{9,14},{10,... | collective-permute-start | bytes 49160 | tf_op jit(solution)/shard_map/ppermute | solution.py:51
  86.9 9.4 %copy-start.9 = (f32[32,128]{1,0:T(8,128)}, f32[32,128]{1,0:T(8,128)S(1)}, u32[]{:S(2)}) copy-start(f32[32,128]{1,0:T(8,128)S(1)} %collective-permute-done.4.refs_3_) | copy-start | bytes 49156
  86.9 9.4 %copy-start.10 = (f32[32,128]{1,0:T(8,128)}, f32[32,128]{1,0:T(8,128)S(1)}, u32[]{:S(2)}) copy-start(f32[32,128]{1,0:T(8,128)S(1)} %collective-permute-done.5.refs_4_) | copy-start | bytes 49156
  87.0 9.3 %copy-start.11 = (f32[32,128]{1,0:T(8,128)}, f32[32,128]{1,0:T(8,128)S(1)}, u32[]{:S(2)}) copy-start(f32[32,128]{1,0:T(8,128)S(1)} %collective-permute-done.6.refs_5_) | copy-start | bytes 49156
  87.0 9.3 %copy-start.12 = (f32[32,128]{1,0:T(8,128)}, f32[32,128]{1,0:T(8,128)S(1)}, u32[]{:S(2)}) copy-start(f32[32,128]{1,0:T(8,128)S(1)} %collective-permute-done.7.refs_6_) | copy-start | bytes 49156
  90.8 5.5 %copy-start.13 = (f32[32,128]{1,0:T(8,128)}, f32[32,128]{1,0:T(8,128)S(1)}, u32[]{:S(2)}) copy-start(f32[32,128]{1,0:T(8,128)S(1)} %collective-permute-done.8.refs_7_) | copy-start | bytes 49156
  90.8 5.5 %collective-permute-start.9 = (bf16[16,64,768]{2,1,0:T(8,128)(2,1)}, bf16[16,64,768]{2,1,0:T(8,128)(2,1)S(1)}, u32[]{:S(2)}, u32[]{:S(2)}) collective-permute-start(bf16[16,64,768]{2,1,0:T(8,128)(2,1)} %all-gather.2.cloned.1.call-done.x_ref), channel_id=1, source_target_pairs={{0,1},{1,0},{2,3},{3,2},{4,5},{5,4},{6,7},{7,6},{8,9},{9,8},{10,11... | collective-permute-start | bytes 4718600 | tf_op jit(solution)/shard_map/ppermute | solution.py:51
  96.3 1.2 copy-start.6
  97.5 19.5 %copy-start.1 = (bf16[1,8,8,768]{3,2,1,0:T(8,128)(2,1)S(1)}, bf16[1,8,8,768]{3,2,1,0:T(8,128)(2,1)}, u32[]{:S(2)}) copy-start(bf16[1,8,8,768]{3,2,1,0:T(8,128)(2,1)} %param.16) | copy-start | bytes 294916
  97.5 19.5 %copy-start.3 = (f32[768]{0:T(1024)S(1)}, f32[768]{0:T(1024)}, u32[]{:S(2)}) copy-start(f32[768]{0:T(1024)} %gain_ref.5) | copy-start | bytes 9220
  105.5 11.5 %collective-permute-start.10 = (bf16[16,48,384]{2,1,0:T(8,128)(2,1)S(1)}, bf16[16,48,384]{2,1,0:T(8,128)(2,1)S(1)}, u32[]{:S(2)}, u32[]{:S(2)}) collective-permute-start(bf16[16,48,384]{2,1,0:T(8,128)(2,1)S(1)} %slice.51), channel_id=1, source_target_pairs={{0,1},{1,0},{2,3},{3,2},{4,5},{5,4},{6,7},{7,6},{8,9},{9,8},{10,11... | collective-permute-start | bytes 1769480 | tf_op jit(solution)/shard_map/ppermute | solution.py:51
Sparse Core Ops, SparseCore 0:
  9.4 70.3 all-gather.1

commit v3 on v2

--- a/solution.py
+++ b/solution.py
@@ -16,7 +16,7 @@
 f32 = jnp.float32
 bf16 = jnp.bfloat16
 VMEM_LIMIT = 48 * 1024 * 1024
-MOST_VMEM = 62 * 1024 * 1024
+MOST_VMEM = 63 * 1024 * 1024
 
 
 def layer_norm(inputs, scale_gain):
@@ -73,33 +73,46 @@
         out_ref[...] = held[lax.axis_index("ka") ^ flip]
 
 
-def attention_kernel(feats, length_ref, x_ref, other_ref, gain_ref, w_ref, *refs):
-    count = len(refs) - 5
+def project_side(samples, x_ref, gain_ref, w_ref, held_ref, kv_ref):
+    places, own_rows, width = x_ref.shape
+    feats = kv_ref.shape[2] // 2
+    each = own_rows // samples
+    chips = places // lax.axis_size("pb")
+    weights = w_ref[...].reshape(width, 4 * feats)
+    x = x_ref[...].reshape(places * own_rows, width).astype(f32)
+    normed = layer_norm(x, gain_ref[...].reshape(1, -1)).astype(bf16)
+    held_ref[...] = normed.reshape(places, own_rows, width)
+    proj = jnp.dot(normed, weights[:, : 2 * feats], preferred_element_type=f32)
+    proj = proj.reshape(places, samples, each, 2 * feats)
+    for s in range(samples):
+        kv_ref[s] = proj[:, s].reshape(places * each, 2 * feats).astype(bf16)
+    rows = held_ref[pl.ds(lax.axis_index("pb") * chips, chips)].reshape(chips * own_rows, width)
+    return jnp.dot(rows, weights[:, 2 * feats :], preferred_element_type=f32)
+
+
+def project_kernel(x_ref, gain_ref, w_ref, kv_ref, query_ref, held_ref):
+    samples = kv_ref.shape[0]
+    query_ref[...] = project_side(samples, x_ref, gain_ref, w_ref, held_ref, kv_ref)
+
+
+def attention_kernel(length_ref, x_ref, gain_ref, w_ref, kv_ref, near_ref, *refs):
+    count = len(refs) - 6
     bias_refs = refs[:count]
-    out_ref, held_normed, held_bias, held_query, held_gate = refs[count:]
+    out_ref, held_normed, held_kv, held_bias, held_query, held_gate = refs[count:]
     places, own_rows, width = x_ref.shape
+    samples, span, feats = kv_ref.shape
+    feats = feats // 2
     chips = count // 2
     blocks = places // chips
     keys_held, lanes = bias_refs[0].shape
     q_rows = lanes // 2
     each = q_rows // count
-    samples = own_rows // each
     key_count = blocks * q_rows
     head_dim = feats // 2
-    length, at, block_at = length_ref[0], lax.axis_index("ka"), lax.axis_index("pb")
+    length, at = length_ref[0], lax.axis_index("ka")
     core = at % 2
-    weights = w_ref[...].reshape(width, 4 * feats)
-    w_kv, w_qg = weights[:, : 2 * feats], weights[:, 2 * feats :]
-    key_value = []
-    for side, ref in enumerate((x_ref, other_ref)):
-        x = ref[...].reshape(places * own_rows, width).astype(f32)
-        normed = layer_norm(x, gain_ref[...].reshape(1, -1)).astype(bf16)
-        held_normed[side] = normed.reshape(places, own_rows, width)
-        proj = jnp.dot(normed, w_kv, preferred_element_type=f32)
-        key_value.append(proj.reshape(places, samples, each, 2 * feats))
-    for side in range(2):
-        rows = held_normed[side, pl.ds(block_at * chips, chips)].reshape(chips * own_rows, width)
-        proj = jnp.dot(rows, w_qg, preferred_element_type=f32)
+    far = project_side(samples, x_ref, gain_ref, w_ref, held_normed, held_kv)
+    for side, proj in enumerate((near_ref[...], far)):
         for z in range(chips):
             k = 2 * z + (core ^ side)
             part = proj[z * own_rows : (z + 1) * own_rows]
@@ -117,18 +130,14 @@
         axis=0,
     )
     index = lax.broadcasted_iota(jnp.int32, (key_count, lanes), 0)
-    span = places * each
     side = index // span
     position = ((index % span) // each) * (2 * each) + (side ^ core) * each + index % each
     live = position < length
     first = lax.broadcasted_iota(jnp.int32, (q_rows, feats), 1) < head_dim
     done = []
     for s in range(samples):
-        both_sides = jnp.concatenate(
-            [part[:, s].reshape(span, 2 * feats) for part in key_value], axis=0
-        )
-        keys = both_sides[:, :feats].astype(bf16)
-        values = both_sides[:, feats:].astype(bf16)
+        both_sides = jnp.concatenate([kv_ref[s], held_kv[s]], axis=0)
+        keys, values = both_sides[:, :feats], both_sides[:, feats:]
         rows = slice(s * each, (s + 1) * each)
         query = held_query[:, rows, :].reshape(q_rows, feats)
         both = jnp.concatenate(
@@ -163,7 +172,7 @@
     at = lax.axis_index("ka")
     gated = jnp.concatenate([gated_ref[k] for k in range(ka_count)], axis=1)
     for side, ref in enumerate((w_ref, other_ref)):
-        weights = ref[:, :, ref.shape[2] - chips * feats :].reshape(width, chips * feats)
+        weights = ref[...].reshape(width, chips * feats)
         added = jnp.dot(gated, weights, preferred_element_type=f32)
         for flip in range(chips):
             held[at ^ (2 * flip + side)] = added[:, flip * feats : (flip + 1) * feats]
@@ -175,17 +184,26 @@
         normed_ref[i] = normed
 
 
-def transition_kernel(hidden_count, x_ref, w_ref, out_ref):
+def transition_kernel(x_ref, w_ref, out_ref, swish, up, down, sems):
     groups, rows, width = x_ref.shape
-    part = hidden_count
+    hidden_count = down.shape[2]
+    copies = [
+        pltpu.make_async_copy(
+            w_ref.at[:, :, pl.ds(i * hidden_count, hidden_count)], part, sems.at[i]
+        )
+        for i, part in ((1, swish), (2, up), (0, down))
+    ]
+    for copy in copies:
+        copy.start()
     x = x_ref[...].reshape(groups * rows, width)
-    down, swish, up = (
-        w_ref[:, :, i * part : (i + 1) * part].reshape(width, part) for i in range(3)
-    )
-    a = jnp.dot(x, swish, preferred_element_type=f32)
-    b = jnp.dot(x, up, preferred_element_type=f32)
+    copies[0].wait()
+    a = jnp.dot(x, swish[...].reshape(width, hidden_count), preferred_element_type=f32)
+    copies[1].wait()
+    b = jnp.dot(x, up[...].reshape(width, hidden_count), preferred_element_type=f32)
     hidden = ((a / (1.0 + jnp.exp(-a))) * b).astype(bf16)
-    out_ref[...] = dot_last(hidden, down).astype(bf16).reshape(groups, rows, width)
+    copies[2].wait()
+    out = dot_last(hidden, down[...].reshape(width, hidden_count))
+    out_ref[...] = out.astype(bf16).reshape(groups, rows, width)
 
 
 def finish_kernel(mixed_ref, part_ref, out_ref):
@@ -195,13 +213,15 @@
     out_ref[...] = total.astype(bf16)
 
 
-def call(kernel, out_shape, scratch=(), scalars=0, flops=0, moved=0, limit=VMEM_LIMIT):
+def call(kernel, out_shape, scratch=(), scalars=0, flops=0, moved=0, limit=VMEM_LIMIT, left=()):
     def run(*operands):
         return pl.pallas_call(
             kernel,
             out_shape=out_shape,
             in_specs=[
-                pl.BlockSpec(memory_space=pltpu.SMEM if i < scalars else pltpu.VMEM)
+                pl.BlockSpec(
+                    memory_space=pltpu.SMEM if i < scalars else pl.ANY if i in left else pltpu.VMEM
+                )
                 for i in range(len(operands))
             ],
             scratch_shapes=list(scratch),
@@ -267,7 +287,7 @@
         flops=2 * 6 * queries * keys_held * channels * HEADS,
         moved=queries * keys_held * channels * 2 + 4 * ka_count * keys_held * lanes,
     )(pair_rep.reshape(queries, keys_held, channels), pair_gain, proj)
-    near = [swap(bias[i], "ka", i) for i in (1, 2)]
+    near = [swap(bias[i], "ka", i) for i in (1, 2, 3)]
     early, near = lax.optimization_barrier((early, near))
     early = early.reshape(pb_count * w_rows, early.shape[2])
 
@@ -283,30 +303,42 @@
         axis=1,
     )
 
-    late, attn_w, far = lax.optimization_barrier((late, attn_w, list(bias[3:])))
+    late, attn_w, far = lax.optimization_barrier((late, attn_w, list(bias[4:])))
     late = spread(late, grp_count, "grp")
-    far = [swap(block, "ka", i + 3) for i, block in enumerate(far)]
+    far = [swap(block, "ka", i + 4) for i, block in enumerate(far)]
     x, far = lax.optimization_barrier((x, far))
     other = swap(x, "ka", 1)
     bias = [bias[0]] + near + far
 
+    line_rows = pb_count * chips * row_count
+    kv_shape = (samples, line_rows, 2 * feats)
+    query_shape = (chips * own_rows, 2 * feats)
+    costs = dict(
+        flops=2 * x.size * 3 * feats, moved=x.size * 2 + attn_w.size * 2, limit=MOST_VMEM
+    )
+    near_kv, near_query = call(
+        project_kernel,
+        (jax.ShapeDtypeStruct(kv_shape, bf16), jax.ShapeDtypeStruct(query_shape, f32)),
+        scratch=[pltpu.VMEM(x.shape, bf16)],
+        **costs,
+    )(x, attn_gain, attn_w)
     gated = call(
-        functools.partial(attention_kernel, feats),
+        attention_kernel,
         jax.ShapeDtypeStruct((ka_count, own_rows, feats), bf16),
         scratch=[
-            pltpu.VMEM((2,) + x.shape, bf16),
+            pltpu.VMEM(x.shape, bf16),
+            pltpu.VMEM(kv_shape, bf16),
             pltpu.VMEM((ka_count, keys_held, lanes), f32),
             pltpu.VMEM((ka_count, own_rows, feats), f32),
             pltpu.VMEM((ka_count, own_rows, feats), f32),
         ],
         scalars=1,
-        flops=4 * x.size * 2 * feats,
-        moved=x.size * 4 + attn_w.size * 2,
-        limit=MOST_VMEM,
-    )(lengths, x, other, attn_gain, attn_w, *bias)
+        **costs,
+    )(lengths, other, attn_gain, attn_w, near_kv, near_query, *bias)
     gated, late = lax.optimization_barrier((gated, late))
     gated = exchange(gated, "ka")
-    out_w = swap(late[:, :, held * 3 * hid :], "ka", 1)
+    out_w = late[:, :, held * 3 * hid :]
+    other_w = swap(out_w, "ka", 1)
 
     rows = jax.ShapeDtypeStruct((own_rows, width), bf16)
     shared = jax.ShapeDtypeStruct((TP, own_rows, width), bf16)
@@ -316,13 +348,16 @@
         scratch=[pltpu.VMEM((ka_count, own_rows, feats), f32)],
         flops=2 * own_rows * width * width,
         moved=width * width * 2,
-    )(gated, late, out_w, own, trans_gain)
+    )(gated, out_w, other_w, own, trans_gain)
 
     groups = [list(range(i, i + TP)) for i in range(0, ka_count, TP)]
     normed_t = exchange(normed_t, "ka", groups)
     part = call(
-        functools.partial(transition_kernel, held * hid),
+        transition_kernel,
         shared,
+        scratch=[pltpu.VMEM((grp_count, pb_count * w_rows, held * hid), bf16)] * 3
+        + [pltpu.SemaphoreType.DMA((3,))],
+        left=(1,),
         flops=2 * own_rows * width * hid * ka_count * 3,
         moved=3 * width * hid * ka_count // TP * 2,
     )(normed_t, late)

time: 150 us -> 147 us (0.980)
  starting transfers between devices: 63.5 us -> 61.4 us
  waiting for transfers between devices: 16.4 us -> 14.7 us
    ppermute x11, starting transfers between devices: 36.2 us -> 33.5 us  [swap(): return lax.ppermute(block, axis, [(i, i ^ flip) for i in range(count)])]
    all_to_all x3, waiting for transfers between devices: 2.57 us -> 0.06 us  [exchange(): lax.all_to_all(blocks, axes, split_axis=0, concat_axis=0, tiled=True, axi...]
    pallas_call x5 -> x6, Pallas kernels: 14.3 us -> 15.4 us  [run(): pl.pallas_call(kernel, out_shape=out_shape, in_specs=[pl.BlockSpec(memory...]
    unnamed x28 -> x26, local copies, waits for them, and re-layouts: 3.47 us -> 2.33 us
  transfers between devices with their start and end apart: 15 -> 15, of which waited for: 6 -> 5; matrix products, arithmetic and copies ran while one was open for 5% -> 5% of each run, Pallas kernels for 6% -> 8%
where the time goes in v3:
time: 147 us; the launch traced here: 145 us
  starting transfers between devices  61.4 us (42%)
  blocking collectives  29.1 us (20%)
  Pallas kernels  15.4 us (10%)
  waiting for transfers between devices  14.7 us (10%)
  between operations  14.3 us (10%)
  local copies, waits for them, and re-layouts  10.2 us (7%)
    ppermute x11, starting transfers between devices, swap(): return lax.ppermute(block, axis, [(i, i ^ flip) for i in range(count)])  33.5 us
    all_to_all x3, blocking collectives, exchange(): lax.all_to_all(blocks, axes, split_axis=0, concat_axis=0, tiled=True, axi...  29.1 us
    all_to_all x3, starting transfers between devices, exchange(): lax.all_to_all(blocks, axes, split_axis=0, concat_axis=0, tiled=True, axi...  27.9 us
    pallas_call x6, Pallas kernels, run(): pl.pallas_call(kernel, out_shape=out_shape, in_specs=[pl.BlockSpec(memory...  15.4 us
    ppermute x11, waiting for transfers between devices, swap(): return lax.ppermute(block, axis, [(i, i ^ flip) for i in range(count)])  13.9 us
    broadcast_in_dim x3, local copies, waits for them, and re-layouts, spread(): return exchange(jnp.broadcast_to(block[None], (count,) + block.shape), axes)  3.2 us
  transfers between devices with their start and end apart: 15, of which 5 were waited for; matrix products, arithmetic and copies ran while one was open for 5% of the time, Pallas kernels for 8%

profile of v3, /device:TPU:1, one launch (start us, length us, event | category | flops | bytes accessed | tf_op | source)
XLA Modules:
  0.0 145.2 jit_solution(4945182473075206431)
XLA Ops:
  7.3 0.8 constant_dynamic-slice_fusion
  8.1 0.8 constant_dynamic-slice_fusion.2
  8.8 0.8 concatenate.10
  10.4 15.6 %all-to-all-start = ((bf16[4,12,1056]{2,1,0:T(8,128)(2,1)}), bf16[4,12,1056]{2,1,0:T(8,128)(2,1)S(1)}, u32[]{:S(2)}, u32[]{:S(2)}) async-start(bf16[4,12,1056]{2,1,0:T(8,128)(2,1)} %broadcast_in_dim.6), calls=%async_computation | async-start | bytes 294912 | tf_op jit(solution)/shard_map/all_to_all | solution.py:36
  26.7 1.0 copy-done
  28.4 1.8 %shard_map.145 = (f32[32,128]{1,0:T(8,128)S(1)}, f32[32,128]{1,0:T(8,128)S(1)}, f32[32,128]{1,0:T(8,128)S(1)}, f32[32,128]{1,0:T(8,128)S(1)}, f32[32,128]{1,0:T(...) custom-call(bf16[64,32,128]{2,1,0:T(8,128)(2,1)S(1)} %bitcast.11, ...), custom_call_target="tpu_custom_call" | custom-call | flops 50331648 | bytes 655360 | tf_op jit(solution)/shard_map/pallas_call | solution.py:218
  30.7 2.9 %collective-permute-start = (f32[32,128]{1,0:T(8,128)S(1)}, f32[32,128]{1,0:T(8,128)S(1)}, u32[]{:S(2)}, u32[]{:S(2)}) collective-permute-start(f32[32,128]{1,0:T(8,128)S(1)} %get-tuple-element.38), channel_id=1, source_target_pairs={{0,1},{1,0},{2,3},{3,2},{4,5},{5,4},{6,7},{7,6},{8,9},{9,8},{10,11... | collective-permute-start | bytes 49160 | tf_op jit(solution)/shard_map/ppermute | solution.py:51
  33.6 2.6 %collective-permute-start.1 = (f32[32,128]{1,0:T(8,128)S(1)}, f32[32,128]{1,0:T(8,128)S(1)}, u32[]{:S(2)}, u32[]{:S(2)}) collective-permute-start(f32[32,128]{1,0:T(8,128)S(1)} %get-tuple-element.39), channel_id=1, source_target_pairs={{0,2},{1,3},{2,0},{3,1},{4,6},{5,7},{6,4},{7,5},{8,10},{9,11},{10,... | collective-permute-start | bytes 49160 | tf_op jit(solution)/shard_map/ppermute | solution.py:51
  36.3 2.8 %collective-permute-start.2 = (f32[32,128]{1,0:T(8,128)S(1)}, f32[32,128]{1,0:T(8,128)S(1)}, u32[]{:S(2)}, u32[]{:S(2)}) collective-permute-start(f32[32,128]{1,0:T(8,128)S(1)} %get-tuple-element.40), channel_id=1, source_target_pairs={{0,3},{1,2},{2,1},{3,0},{4,7},{5,6},{6,5},{7,4},{8,11},{9,10},{10,... | collective-permute-start | bytes 49160 | tf_op jit(solution)/shard_map/ppermute | solution.py:51
  39.1 2.3 %collective-permute-done.2.refs_3_ = f32[32,128]{1,0:T(8,128)S(1)} collective-permute-done((f32[32,128]{1,0:T(8,128)S(1)}, f32[32,128]{1,0:T(8,128)S(1)}, u32[]{:S(2)}, u32[]{:S(2)}) %collective-permute-start.2) | collective-permute-done | bytes 16416 | tf_op jit(solution)/shard_map/ppermute | solution.py:51
  41.6 2.9 %collective-permute-start.3 = (bf16[48,96]{1,0:T(8,128)(2,1)S(1)}, bf16[48,96]{1,0:T(8,128)(2,1)S(1)}, u32[]{:S(2)}, u32[]{:S(2)}) collective-permute-start(bf16[48,96]{1,0:T(8,128)(2,1)S(1)} %slice.54), channel_id=1, source_target_pairs={{0,2},{1,3},{2,0},{3,1},{4,6},{5,7},{6,4},{7,5},{8,10},{9,11},{10,... | collective-permute-start | bytes 27656 | tf_op jit(solution)/shard_map/ppermute | solution.py:51
  44.5 0.9 broadcast_in_dim.7
  45.4 6.8 %all-to-all-start.1 = ((bf16[16,48,384]{2,1,0:T(8,128)(2,1)}), bf16[16,48,384]{2,1,0:T(8,128)(2,1)S(1)}, u32[]{:S(2)}, u32[]{:S(2)}) async-start(bf16[16,48,384]{2,1,0:T(8,128)(2,1)} %broadcast_in_dim.7), calls=%async_computation.1 | async-start | bytes 1179648 | tf_op jit(solution)/shard_map/all_to_all | solution.py:36
  52.4 2.7 %collective-permute-start.4 = (bf16[48,768]{1,0:T(8,128)(2,1)S(1)}, bf16[48,768]{1,0:T(8,128)(2,1)S(1)}, u32[]{:S(2)}, u32[]{:S(2)}) collective-permute-start(bf16[48,768]{1,0:T(8,128)(2,1)S(1)} %pad_maximum_fusion), channel_id=1, source_target_pairs={{0,4},{1,5},{2,6},{3,7},{4,0},{5,1},{6,2},{7,3},{8,12},{9,13},{10,... | collective-permute-start | bytes 221192 | tf_op jit(solution)/shard_map/ppermute | solution.py:51
  55.2 6.2 %collective-permute-done.4 = bf16[48,768]{1,0:T(8,128)(2,1)S(1)} collective-permute-done((bf16[48,768]{1,0:T(8,128)(2,1)S(1)}, bf16[48,768]{1,0:T(8,128)(2,1)S(1)}, u32[]{:S(2)}, u32[]{:S(2)}) %collective-permute-start.4) | collective-permute-done | bytes 73760 | tf_op jit(solution)/shard_map/ppermute | solution.py:51
  61.7 1.7 %broadcast_in_dim.8 = bf16[16,48,1536]{2,1,0:T(8,128)(2,1)} broadcast(bf16[48,1536]{1,0:T(8,128)(2,1)S(1)} %concatenate.12), dimensions={1,2} | broadcast | bytes 2506752 | tf_op jit(solution)/shard_map/broadcast_in_dim | solution.py:42
  63.3 5.4 %all-to-all-start.2 = ((bf16[16,48,1536]{2,1,0:T(8,128)(2,1)}), bf16[16,48,1536]{2,1,0:T(8,128)(2,1)}, u32[]{:S(2)}, u32[]{:S(2)}) async-start(bf16[16,48,1536]{2,1,0:T(8,128)(2,1)} %broadcast_in_dim.8), calls=%async_computation.2 | async-start | bytes 4718592 | tf_op jit(solution)/shard_map/all_to_all | solution.py:36
  68.8 2.6 %collective-permute-start.5 = (f32[32,128]{1,0:T(8,128)S(1)}, f32[32,128]{1,0:T(8,128)S(1)}, u32[]{:S(2)}, u32[]{:S(2)}) collective-permute-start(f32[32,128]{1,0:T(8,128)S(1)} %get-tuple-element.46), channel_id=1, source_target_pairs={{0,4},{1,5},{2,6},{3,7},{4,0},{5,1},{6,2},{7,3},{8,12},{9,13},{10,... | collective-permute-start | bytes 49160 | tf_op jit(solution)/shard_map/ppermute | solution.py:51
  71.4 6.6 %collective-permute-start.6 = (f32[32,128]{1,0:T(8,128)S(1)}, f32[32,128]{1,0:T(8,128)S(1)}, u32[]{:S(2)}, u32[]{:S(2)}) collective-permute-start(f32[32,128]{1,0:T(8,128)S(1)} %get-tuple-element.47), channel_id=1, source_target_pairs={{0,5},{1,4},{2,7},{3,6},{4,1},{5,0},{6,3},{7,2},{8,13},{9,12},{10,... | collective-permute-start | bytes 49160 | tf_op jit(solution)/shard_map/ppermute | solution.py:51
  77.9 3.9 %collective-permute-start.7 = (f32[32,128]{1,0:T(8,128)S(1)}, f32[32,128]{1,0:T(8,128)S(1)}, u32[]{:S(2)}, u32[]{:S(2)}) collective-permute-start(f32[32,128]{1,0:T(8,128)S(1)} %get-tuple-element.48), channel_id=1, source_target_pairs={{0,6},{1,7},{2,4},{3,5},{4,2},{5,3},{6,0},{7,1},{8,14},{9,15},{10,... | collective-permute-start | bytes 49160 | tf_op jit(solution)/shard_map/ppermute | solution.py:51
  81.9 1.9 %collective-permute-start.8 = (f32[32,128]{1,0:T(8,128)S(1)}, f32[32,128]{1,0:T(8,128)S(1)}, u32[]{:S(2)}, u32[]{:S(2)}) collective-permute-start(f32[32,128]{1,0:T(8,128)S(1)} %get-tuple-element.49), channel_id=1, source_target_pairs={{0,7},{1,6},{2,5},{3,4},{4,3},{5,2},{6,1},{7,0},{8,15},{9,14},{10,... | collective-permute-start | bytes 49160 | tf_op jit(solution)/shard_map/ppermute | solution.py:51
  83.8 0.8 collective-permute-done.7.refs_6_
  84.7 4.6 %collective-permute-done.8.refs_7_ = f32[32,128]{1,0:T(8,128)S(1)} collective-permute-done((f32[32,128]{1,0:T(8,128)S(1)}, f32[32,128]{1,0:T(8,128)S(1)}, u32[]{:S(2)}, u32[]{:S(2)}) %collective-permute-start.8) | collective-permute-done | bytes 16416 | tf_op jit(solution)/shard_map/ppermute | solution.py:51
  89.3 2.2 %collective-permute-start.9 = (bf16[16,64,768]{2,1,0:T(8,128)(2,1)}, bf16[16,64,768]{2,1,0:T(8,128)(2,1)}, u32[]{:S(2)}, u32[]{:S(2)}) collective-permute-start(bf16[16,64,768]{2,1,0:T(8,128)(2,1)} %all-gather.2.cloned.1.call-done.x_ref), channel_id=1, source_target_pairs={{0,1},{1,0},{2,3},{3,2},{4,5},{5,4},{6,7},{7,6},{8,9},{9,8},{10,11... | collective-permute-start | bytes 4718600 | tf_op jit(solution)/shard_map/ppermute | solution.py:51
  92.1 3.9 %shard_map.146 = (bf16[8,128,192]{2,1,0:T(8,128)(2,1)}, f32[256,192]{1,0:T(8,128)}) custom-call(bf16[16,64,768]{2,1,0:T(8,128)(2,1)} %all-gather.2.cloned.1.call-done.x_ref, f32[768]{0:T(1024)} %gain_ref.6, bf16[16,48,384]{2,1,0:T(8,128)(2,1)} %copy-done.5), custom_call_target="tpu_custom_call" | custom-call | flops 452984832 | bytes 2162688 | tf_op jit(solution)/shard_map/pallas_call | solution.py:218
  96.1 6.1 %shard_map.147 = bf16[8,64,96]{2,1,0:T(8,128)(2,1)} custom-call(s32[1]{0:T(128)S(6)} %copy.21.length_ref, bf16[16,64,768]{2,1,0:T(8,128)(2,1)} %collective-permute-done.9.x_ref, f32[768]{0:T(1024)} %gain_ref.6, bf16[16,48,384]{2,1,0:T(8,128)(2,1)} %copy-done.5, bf16[8,128,192]{2,1,0:T(8,128)(2,1)} %get-tuple-element.52.kv_ref, ...), custom_call_target="tpu_custom_call" | custom-call | flops 452984832 | bytes 2162688 | tf_op jit(solution)/shard_map/pallas_call | solution.py:218
  102.1 1.1 slice.51.w_ref
  103.3 2.3 %collective-permute-start.10 = (bf16[16,48,384]{2,1,0:T(8,128)(2,1)S(1)}, bf16[16,48,384]{2,1,0:T(8,128)(2,1)S(1)}, u32[]{:S(2)}, u32[]{:S(2)}) collective-permute-start(bf16[16,48,384]{2,1,0:T(8,128)(2,1)S(1)} %slice.51.w_ref), channel_id=1, source_target_pairs={{0,1},{1,0},{2,3},{3,2},{4,5},{5,4},{6,7},{7,6},{8,9},{9,8},{10,11... | collective-permute-start | bytes 1769480 | tf_op jit(solution)/shard_map/ppermute | solution.py:51
  105.6 9.5 %all_to_all.30.gated_ref = bf16[8,64,96]{2,1,0:T(8,128)(2,1)S(1)} all-to-all(bf16[8,64,96]{2,1,0:T(8,128)(2,1)} %shard_map.147), channel_id=1, replica_groups=mesh['grp'=16,'pb'=4,'ka'=8] {'ka'}, dimensions={0} | all-to-all | bytes 196608 | tf_op jit(solution)/shard_map/all_to_all | solution.py:36
  115.8 9.8 %all_to_all.31.x_ref = bf16[4,64,768]{2,1,0:T(8,128)(2,1)S(1)} all-to-all(bf16[4,64,768]{2,1,0:T(8,128)(2,1)S(1)} %get-tuple-element.66), channel_id=1, replica_groups={{0,1,2,3},{4,5,6,7},{8,9,10,11},{12,13,14,15},{16,17,18,19},{20,21,22,2..., dimensions={0} | all-to-all | bytes 786432 | tf_op jit(solution)/shard_map/all_to_all | solution.py:36
  125.6 2.2 %shard_map.149 = bf16[4,64,768]{2,1,0:T(8,128)(2,1)S(1)} custom-call(bf16[4,64,768]{2,1,0:T(8,128)(2,1)S(1)} %all_to_all.31.x_ref, bf16[16,48,1536]{2,1,0:T(8,128)(2,1)} %all-to-all-done.2.w_ref), custom_call_target="tpu_custom_call" | custom-call | flops 452984832 | bytes 1769472 | tf_op jit(solution)/shard_map/pallas_call | solution.py:218
  127.8 9.8 %all_to_all.32.part_ref = bf16[4,64,768]{2,1,0:T(8,128)(2,1)S(1)} all-to-all(bf16[4,64,768]{2,1,0:T(8,128)(2,1)S(1)} %shard_map.149), channel_id=1, replica_groups={{0,1,2,3},{4,5,6,7},{8,9,10,11},{12,13,14,15},{16,17,18,19},{20,21,22,2..., dimensions={0} | all-to-all | bytes 786432 | tf_op jit(solution)/shard_map/all_to_all | solution.py:36
  (51 shorter events, 5.5 us)
Async XLA Ops:
  6.5 82.7 %all-gather.2.cloned.1.call-start = ((), (), s32[]{:S(2)}) async-start(), calls=%async_computation.6 | async-start | bytes 1671168 | tf_op jit(solution)/shard_map/all_gather | solution.py:266
  10.4 31.1 %all-to-all-start = ((bf16[4,12,1056]{2,1,0:T(8,128)(2,1)}), bf16[4,12,1056]{2,1,0:T(8,128)(2,1)S(1)}, u32[]{:S(2)}, u32[]{:S(2)}) async-start(bf16[4,12,1056]{2,1,0:T(8,128)(2,1)} %broadcast_in_dim.6), calls=%async_computation | async-start | bytes 294912 | tf_op jit(solution)/shard_map/all_to_all | solution.py:36
  26.7 1.0 copy-start
  27.7 0.7 copy-start.4
  30.1 0.6 copy-start.2
  30.7 8.3 %collective-permute-start = (f32[32,128]{1,0:T(8,128)S(1)}, f32[32,128]{1,0:T(8,128)S(1)}, u32[]{:S(2)}, u32[]{:S(2)}) collective-permute-start(f32[32,128]{1,0:T(8,128)S(1)} %get-tuple-element.38), channel_id=1, source_target_pairs={{0,1},{1,0},{2,3},{3,2},{4,5},{5,4},{6,7},{7,6},{8,9},{9,8},{10,11... | collective-permute-start | bytes 49160 | tf_op jit(solution)/shard_map/ppermute | solution.py:51
  33.6 5.5 %collective-permute-start.1 = (f32[32,128]{1,0:T(8,128)S(1)}, f32[32,128]{1,0:T(8,128)S(1)}, u32[]{:S(2)}, u32[]{:S(2)}) collective-permute-start(f32[32,128]{1,0:T(8,128)S(1)} %get-tuple-element.39), channel_id=1, source_target_pairs={{0,2},{1,3},{2,0},{3,1},{4,6},{5,7},{6,4},{7,5},{8,10},{9,11},{10,... | collective-permute-start | bytes 49160 | tf_op jit(solution)/shard_map/ppermute | solution.py:51
  36.3 5.2 %collective-permute-start.2 = (f32[32,128]{1,0:T(8,128)S(1)}, f32[32,128]{1,0:T(8,128)S(1)}, u32[]{:S(2)}, u32[]{:S(2)}) collective-permute-start(f32[32,128]{1,0:T(8,128)S(1)} %get-tuple-element.40), channel_id=1, source_target_pairs={{0,3},{1,2},{2,1},{3,0},{4,7},{5,6},{6,5},{7,4},{8,11},{9,10},{10,... | collective-permute-start | bytes 49160 | tf_op jit(solution)/shard_map/ppermute | solution.py:51
  39.1 24.2 %copy-start.6 = (f32[32,128]{1,0:T(8,128)}, f32[32,128]{1,0:T(8,128)S(1)}, u32[]{:S(2)}) copy-start(f32[32,128]{1,0:T(8,128)S(1)} %collective-permute-done.refs_1_) | copy-start | bytes 49156
  39.1 24.2 %copy-start.7 = (f32[32,128]{1,0:T(8,128)}, f32[32,128]{1,0:T(8,128)S(1)}, u32[]{:S(2)}) copy-start(f32[32,128]{1,0:T(8,128)S(1)} %collective-permute-done.1.refs_2_) | copy-start | bytes 49156
  41.4 21.9 %copy-start.8 = (f32[32,128]{1,0:T(8,128)}, f32[32,128]{1,0:T(8,128)S(1)}, u32[]{:S(2)}) copy-start(f32[32,128]{1,0:T(8,128)S(1)} %collective-permute-done.2.refs_3_) | copy-start | bytes 49156
  41.6 10.7 %collective-permute-start.3 = (bf16[48,96]{1,0:T(8,128)(2,1)S(1)}, bf16[48,96]{1,0:T(8,128)(2,1)S(1)}, u32[]{:S(2)}, u32[]{:S(2)}) collective-permute-start(bf16[48,96]{1,0:T(8,128)(2,1)S(1)} %slice.54), channel_id=1, source_target_pairs={{0,2},{1,3},{2,0},{3,1},{4,6},{5,7},{6,4},{7,5},{8,10},{9,11},{10,... | collective-permute-start | bytes 27656 | tf_op jit(solution)/shard_map/ppermute | solution.py:51
  45.4 16.3 %all-to-all-start.1 = ((bf16[16,48,384]{2,1,0:T(8,128)(2,1)}), bf16[16,48,384]{2,1,0:T(8,128)(2,1)S(1)}, u32[]{:S(2)}, u32[]{:S(2)}) async-start(bf16[16,48,384]{2,1,0:T(8,128)(2,1)} %broadcast_in_dim.7), calls=%async_computation.1 | async-start | bytes 1179648 | tf_op jit(solution)/shard_map/all_to_all | solution.py:36
  52.4 9.0 %collective-permute-start.4 = (bf16[48,768]{1,0:T(8,128)(2,1)S(1)}, bf16[48,768]{1,0:T(8,128)(2,1)S(1)}, u32[]{:S(2)}, u32[]{:S(2)}) collective-permute-start(bf16[48,768]{1,0:T(8,128)(2,1)S(1)} %pad_maximum_fusion), channel_id=1, source_target_pairs={{0,4},{1,5},{2,6},{3,7},{4,0},{5,1},{6,2},{7,3},{8,12},{9,13},{10,... | collective-permute-start | bytes 221192 | tf_op jit(solution)/shard_map/ppermute | solution.py:51
  61.7 1.7 %copy-start.5 = (bf16[16,48,384]{2,1,0:T(8,128)(2,1)}, bf16[16,48,384]{2,1,0:T(8,128)(2,1)S(1)}, u32[]{:S(2)}) copy-start(bf16[16,48,384]{2,1,0:T(8,128)(2,1)S(1)} %all-to-all-done.1.w_ref) | copy-start | bytes 1769476
  63.3 38.8 %all-to-all-start.2 = ((bf16[16,48,1536]{2,1,0:T(8,128)(2,1)}), bf16[16,48,1536]{2,1,0:T(8,128)(2,1)}, u32[]{:S(2)}, u32[]{:S(2)}) async-start(bf16[16,48,1536]{2,1,0:T(8,128)(2,1)} %broadcast_in_dim.8), calls=%async_computation.2 | async-start | bytes 4718592 | tf_op jit(solution)/shard_map/all_to_all | solution.py:36
  68.8 15.0 %collective-permute-start.5 = (f32[32,128]{1,0:T(8,128)S(1)}, f32[32,128]{1,0:T(8,128)S(1)}, u32[]{:S(2)}, u32[]{:S(2)}) collective-permute-start(f32[32,128]{1,0:T(8,128)S(1)} %get-tuple-element.46), channel_id=1, source_target_pairs={{0,4},{1,5},{2,6},{3,7},{4,0},{5,1},{6,2},{7,3},{8,12},{9,13},{10,... | collective-permute-start | bytes 49160 | tf_op jit(solution)/shard_map/ppermute | solution.py:51
  71.4 12.5 %collective-permute-start.6 = (f32[32,128]{1,0:T(8,128)S(1)}, f32[32,128]{1,0:T(8,128)S(1)}, u32[]{:S(2)}, u32[]{:S(2)}) collective-permute-start(f32[32,128]{1,0:T(8,128)S(1)} %get-tuple-element.47), channel_id=1, source_target_pairs={{0,5},{1,4},{2,7},{3,6},{4,1},{5,0},{6,3},{7,2},{8,13},{9,12},{10,... | collective-permute-start | bytes 49160 | tf_op jit(solution)/shard_map/ppermute | solution.py:51
  77.9 6.7 %collective-permute-start.7 = (f32[32,128]{1,0:T(8,128)S(1)}, f32[32,128]{1,0:T(8,128)S(1)}, u32[]{:S(2)}, u32[]{:S(2)}) collective-permute-start(f32[32,128]{1,0:T(8,128)S(1)} %get-tuple-element.48), channel_id=1, source_target_pairs={{0,6},{1,7},{2,4},{3,5},{4,2},{5,3},{6,0},{7,1},{8,14},{9,15},{10,... | collective-permute-start | bytes 49160 | tf_op jit(solution)/shard_map/ppermute | solution.py:51
  81.9 7.4 %collective-permute-start.8 = (f32[32,128]{1,0:T(8,128)S(1)}, f32[32,128]{1,0:T(8,128)S(1)}, u32[]{:S(2)}, u32[]{:S(2)}) collective-permute-start(f32[32,128]{1,0:T(8,128)S(1)} %get-tuple-element.49), channel_id=1, source_target_pairs={{0,7},{1,6},{2,5},{3,4},{4,3},{5,2},{6,1},{7,0},{8,15},{9,14},{10,... | collective-permute-start | bytes 49160 | tf_op jit(solution)/shard_map/ppermute | solution.py:51
  83.8 12.2 %copy-start.9 = (f32[32,128]{1,0:T(8,128)}, f32[32,128]{1,0:T(8,128)S(1)}, u32[]{:S(2)}) copy-start(f32[32,128]{1,0:T(8,128)S(1)} %collective-permute-done.5.refs_4_) | copy-start | bytes 49156
  83.8 12.2 %copy-start.10 = (f32[32,128]{1,0:T(8,128)}, f32[32,128]{1,0:T(8,128)S(1)}, u32[]{:S(2)}) copy-start(f32[32,128]{1,0:T(8,128)S(1)} %collective-permute-done.6.refs_5_) | copy-start | bytes 49156
  84.7 11.4 %copy-start.11 = (f32[32,128]{1,0:T(8,128)}, f32[32,128]{1,0:T(8,128)S(1)}, u32[]{:S(2)}) copy-start(f32[32,128]{1,0:T(8,128)S(1)} %collective-permute-done.7.refs_6_) | copy-start | bytes 49156
  89.3 6.8 %copy-start.12 = (f32[32,128]{1,0:T(8,128)}, f32[32,128]{1,0:T(8,128)S(1)}, u32[]{:S(2)}) copy-start(f32[32,128]{1,0:T(8,128)S(1)} %collective-permute-done.8.refs_7_) | copy-start | bytes 49156
  89.3 6.7 %collective-permute-start.9 = (bf16[16,64,768]{2,1,0:T(8,128)(2,1)}, bf16[16,64,768]{2,1,0:T(8,128)(2,1)}, u32[]{:S(2)}, u32[]{:S(2)}) collective-permute-start(bf16[16,64,768]{2,1,0:T(8,128)(2,1)} %all-gather.2.cloned.1.call-done.x_ref), channel_id=1, source_target_pairs={{0,1},{1,0},{2,3},{3,2},{4,5},{5,4},{6,7},{7,6},{8,9},{9,8},{10,11... | collective-permute-start | bytes 4718600 | tf_op jit(solution)/shard_map/ppermute | solution.py:51
  96.0 19.0 %copy-start.1 = (bf16[1,8,8,768]{3,2,1,0:T(8,128)(2,1)S(1)}, bf16[1,8,8,768]{3,2,1,0:T(8,128)(2,1)}, u32[]{:S(2)}) copy-start(bf16[1,8,8,768]{3,2,1,0:T(8,128)(2,1)} %param.16) | copy-start | bytes 294916
  96.0 19.0 %copy-start.3 = (f32[768]{0:T(1024)S(1)}, f32[768]{0:T(1024)}, u32[]{:S(2)}) copy-start(f32[768]{0:T(1024)} %gain_ref.7) | copy-start | bytes 9220
  103.3 11.8 %collective-permute-start.10 = (bf16[16,48,384]{2,1,0:T(8,128)(2,1)S(1)}, bf16[16,48,384]{2,1,0:T(8,128)(2,1)S(1)}, u32[]{:S(2)}, u32[]{:S(2)}) collective-permute-start(bf16[16,48,384]{2,1,0:T(8,128)(2,1)S(1)} %slice.51.w_ref), channel_id=1, source_target_pairs={{0,1},{1,0},{2,3},{3,2},{4,5},{5,4},{6,7},{7,6},{8,9},{9,8},{10,11... | collective-permute-start | bytes 1769480 | tf_op jit(solution)/shard_map/ppermute | solution.py:51
Sparse Core Ops, SparseCore 0:
  9.4 70.7 all-gather.1

commit v4 on v3

--- a/solution.py
+++ b/solution.py
@@ -73,32 +73,47 @@
         out_ref[...] = held[lax.axis_index("ka") ^ flip]
 
 
-def project_side(samples, x_ref, gain_ref, w_ref, held_ref, kv_ref):
+def project_side(samples, x_ref, gain_ref, w_ref, raw_ref, held_ref, sems, kv_ref):
     places, own_rows, width = x_ref.shape
     feats = kv_ref.shape[2] // 2
     each = own_rows // samples
-    chips = places // lax.axis_size("pb")
+    blocks = lax.axis_size("pb")
+    chips = places // blocks
+    copies = [
+        pltpu.make_async_copy(
+            x_ref.at[pl.ds(b * chips, chips)], raw_ref.at[pl.ds(b * chips, chips)], sems.at[b]
+        )
+        for b in range(blocks)
+    ]
+    for copy in copies:
+        copy.start()
     weights = w_ref[...].reshape(width, 4 * feats)
-    x = x_ref[...].reshape(places * own_rows, width).astype(f32)
-    normed = layer_norm(x, gain_ref[...].reshape(1, -1)).astype(bf16)
-    held_ref[...] = normed.reshape(places, own_rows, width)
-    proj = jnp.dot(normed, weights[:, : 2 * feats], preferred_element_type=f32)
-    proj = proj.reshape(places, samples, each, 2 * feats)
-    for s in range(samples):
-        kv_ref[s] = proj[:, s].reshape(places * each, 2 * feats).astype(bf16)
+    for b, copy in enumerate(copies):
+        copy.wait()
+        part = slice(b * chips, (b + 1) * chips)
+        x = raw_ref[part].reshape(chips * own_rows, width).astype(f32)
+        normed = layer_norm(x, gain_ref[...].reshape(1, -1)).astype(bf16)
+        held_ref[part] = normed.reshape(chips, own_rows, width)
+        proj = jnp.dot(normed, weights[:, : 2 * feats], preferred_element_type=f32)
+        proj = proj.reshape(chips, samples, each, 2 * feats)
+        rows = slice(b * chips * each, (b + 1) * chips * each)
+        for s in range(samples):
+            kv_ref[s, rows] = proj[:, s].reshape(chips * each, 2 * feats).astype(bf16)
     rows = held_ref[pl.ds(lax.axis_index("pb") * chips, chips)].reshape(chips * own_rows, width)
     return jnp.dot(rows, weights[:, 2 * feats :], preferred_element_type=f32)
 
 
-def project_kernel(x_ref, gain_ref, w_ref, kv_ref, query_ref, held_ref):
+def project_kernel(x_ref, gain_ref, w_ref, kv_ref, query_ref, raw_ref, held_ref, sems):
     samples = kv_ref.shape[0]
-    query_ref[...] = project_side(samples, x_ref, gain_ref, w_ref, held_ref, kv_ref)
+    query_ref[...] = project_side(
+        samples, x_ref, gain_ref, w_ref, raw_ref, held_ref, sems, kv_ref
+    )
 
 
 def attention_kernel(length_ref, x_ref, gain_ref, w_ref, kv_ref, near_ref, *refs):
-    count = len(refs) - 6
+    count = len(refs) - 8
     bias_refs = refs[:count]
-    out_ref, held_normed, held_kv, held_bias, held_query, held_gate = refs[count:]
+    out_ref, raw, held_normed, sems, held_kv, held_bias, held_query, held_gate = refs[count:]
     places, own_rows, width = x_ref.shape
     samples, span, feats = kv_ref.shape
     feats = feats // 2
@@ -111,7 +126,7 @@
     head_dim = feats // 2
     length, at = length_ref[0], lax.axis_index("ka")
     core = at % 2
-    far = project_side(samples, x_ref, gain_ref, w_ref, held_normed, held_kv)
+    far = project_side(samples, x_ref, gain_ref, w_ref, raw, held_normed, sems, held_kv)
     for side, proj in enumerate((near_ref[...], far)):
         for z in range(chips):
             k = 2 * z + (core ^ side)
@@ -180,8 +195,7 @@
     mixed = (single_ref[...].astype(f32) + added).astype(bf16)
     mixed_ref[...] = mixed
     normed = layer_norm(mixed.astype(f32), gain_ref[...].reshape(1, -1)).astype(bf16)
-    for i in range(normed_ref.shape[0]):
-        normed_ref[i] = normed
+    normed_ref[...] = normed
 
 
 def transition_kernel(x_ref, w_ref, out_ref, swish, up, down, sems):
@@ -291,20 +305,20 @@
     early, near = lax.optimization_barrier((early, near))
     early = early.reshape(pb_count * w_rows, early.shape[2])
 
-    attn_w = spread(early[:, : 4 * feats], grp_count, "grp")
-
+    attn_w = jnp.broadcast_to(early[None, :, : 4 * feats], (grp_count, pb_count * w_rows, 4 * feats))
+    late = early[:, 4 * feats :]
     out_w = early[:, 4 * feats + 3 * hid :]
-    out_w = [out_w] + [swap(out_w, "ka", 2)]
-    late = jnp.concatenate([early[:, 4 * feats : 4 * feats + 3 * hid]] + out_w, axis=1)
+    attn_w, late, out_w = lax.optimization_barrier((attn_w, late, out_w))
+    attn_w = exchange(attn_w, "grp")
+
     late = [late] + [swap(late, "ka", TP)]
+    out_w = [late[0][:, 3 * hid :], swap(out_w, "ka", 2), late[1][:, 3 * hid :], swap(out_w, "ka", 6)]
     late = jnp.concatenate(
-        [w[:, i * hid : (i + 1) * hid] for i in range(3) for w in late]
-        + [w[:, 3 * hid :] for w in late],
-        axis=1,
-    )
-
+        [w[:, i * hid : (i + 1) * hid] for i in range(3) for w in late] + out_w, axis=1
+    )
+    late = jnp.broadcast_to(late[None], (grp_count,) + late.shape)
     late, attn_w, far = lax.optimization_barrier((late, attn_w, list(bias[4:])))
-    late = spread(late, grp_count, "grp")
+    late = exchange(late, "grp")
     far = [swap(block, "ka", i + 4) for i, block in enumerate(far)]
     x, far = lax.optimization_barrier((x, far))
     other = swap(x, "ka", 1)
@@ -316,23 +330,26 @@
     costs = dict(
         flops=2 * x.size * 3 * feats, moved=x.size * 2 + attn_w.size * 2, limit=MOST_VMEM
     )
+    rows_held = [pltpu.VMEM(x.shape, bf16)] * 2 + [pltpu.SemaphoreType.DMA((pb_count,))]
     near_kv, near_query = call(
         project_kernel,
         (jax.ShapeDtypeStruct(kv_shape, bf16), jax.ShapeDtypeStruct(query_shape, f32)),
-        scratch=[pltpu.VMEM(x.shape, bf16)],
+        scratch=rows_held,
+        left=(0,),
         **costs,
     )(x, attn_gain, attn_w)
     gated = call(
         attention_kernel,
         jax.ShapeDtypeStruct((ka_count, own_rows, feats), bf16),
-        scratch=[
-            pltpu.VMEM(x.shape, bf16),
+        scratch=rows_held
+        + [
             pltpu.VMEM(kv_shape, bf16),
             pltpu.VMEM((ka_count, keys_held, lanes), f32),
             pltpu.VMEM((ka_count, own_rows, feats), f32),
             pltpu.VMEM((ka_count, own_rows, feats), f32),
         ],
         scalars=1,
+        left=(1,),
         **costs,
     )(lengths, other, attn_gain, attn_w, near_kv, near_query, *bias)
     gated, late = lax.optimization_barrier((gated, late))
@@ -344,14 +361,14 @@
     shared = jax.ShapeDtypeStruct((TP, own_rows, width), bf16)
     mixed, normed_t = call(
         mix_kernel,
-        (rows, shared),
+        (rows, rows),
         scratch=[pltpu.VMEM((ka_count, own_rows, feats), f32)],
         flops=2 * own_rows * width * width,
         moved=width * width * 2,
     )(gated, out_w, other_w, own, trans_gain)
 
     groups = [list(range(i, i + TP)) for i in range(0, ka_count, TP)]
-    normed_t = exchange(normed_t, "ka", groups)
+    normed_t = lax.all_gather(normed_t, "ka", axis=0, tiled=False, axis_index_groups=groups)
     part = call(
         transition_kernel,
         shared,

time: 147 us -> 146 us (level)
  starting transfers between devices: 61.4 us -> 65.9 us
  blocking collectives: 29.1 us -> 25.1 us
  waiting for transfers between devices: 14.7 us -> 11.2 us
  Pallas kernels: 15.4 us -> 18 us
    all_to_all x3 -> x2, blocking collectives: 29.1 us -> 18.2 us  [exchange(): lax.all_to_all(blocks, axes, split_axis=0, concat_axis=0, tiled=True, axi...]
    all_gather x0 -> x1, blocking collectives: none -> 6.96 us  [on_device(): lax.all_gather(normed_t, 'ka', axis=0, tiled=False, axis_index_groups=gro...]
    ppermute x11 -> x12, starting transfers between devices: 33.5 us -> 37 us  [swap(): return lax.ppermute(block, axis, [(i, i ^ flip) for i in range(count)])]
    ppermute x11 -> x12, waiting for transfers between devices: 13.9 us -> 10.4 us  [swap(): return lax.ppermute(block, axis, [(i, i ^ flip) for i in range(count)])]
    broadcast_in_dim x0 -> x2, local copies, waits for them, and re-layouts: none -> 2.54 us  [the longest x1 1.66 us: on_device(): late = jnp.broadcast_to(late[None], (grp_count,) + late.shape)]
    pallas_call x6, Pallas kernels: 15.4 us -> 18 us  [run(): pl.pallas_call(kernel, out_shape=out_shape, in_specs=[pl.BlockSpec(memory...]
    broadcast_in_dim x3 -> x1, local copies, waits for them, and re-layouts: 3.2 us -> 0.67 us  [spread(): return exchange(jnp.broadcast_to(block[None], (count,) + block.shape), axes)]
  transfers between devices with their start and end apart: 15 -> 16, of which waited for: 5 -> 4; matrix products, arithmetic and copies ran while one was open for 5% -> 5% of each run, Pallas kernels for 8% -> 10%
where the time goes in v4:
time: 146 us; the launch traced here: 145 us
  starting transfers between devices  65.9 us (45%)
  blocking collectives  25.1 us (17%)
  Pallas kernels  18 us (12%)
  between operations  14.4 us (10%)
  waiting for transfers between devices  11.2 us (8%)
  local copies, waits for them, and re-layouts  10.4 us (7%)
    ppermute x12, starting transfers between devices, swap(): return lax.ppermute(block, axis, [(i, i ^ flip) for i in range(count)])  37 us
    all_to_all x3, starting transfers between devices, exchange(): lax.all_to_all(blocks, axes, split_axis=0, concat_axis=0, tiled=True, axi...  28.9 us
    all_to_all x2, blocking collectives, exchange(): lax.all_to_all(blocks, axes, split_axis=0, concat_axis=0, tiled=True, axi...  18.2 us
    pallas_call x6, Pallas kernels, run(): pl.pallas_call(kernel, out_shape=out_shape, in_specs=[pl.BlockSpec(memory...  18 us
    ppermute x12, waiting for transfers between devices, swap(): return lax.ppermute(block, axis, [(i, i ^ flip) for i in range(count)])  10.4 us
    all_gather x1, blocking collectives, on_device(): lax.all_gather(normed_t, 'ka', axis=0, tiled=False, axis_index_groups=gro...  6.96 us
  transfers between devices with their start and end apart: 16, of which 4 were waited for; matrix products, arithmetic and copies ran while one was open for 5% of the time, Pallas kernels for 10%

profile of v4, /device:TPU:1, one launch (start us, length us, event | category | flops | bytes accessed | tf_op | source)
XLA Modules:
  0.0 144.9 jit_solution(1423150955177998334)
XLA Ops:
  7.3 0.8 constant_dynamic-slice_fusion.2
  8.8 0.8 concatenate.6
  10.3 15.6 %all-to-all-start = ((bf16[4,12,1056]{2,1,0:T(8,128)(2,1)}), bf16[4,12,1056]{2,1,0:T(8,128)(2,1)S(1)}, u32[]{:S(2)}, u32[]{:S(2)}) async-start(bf16[4,12,1056]{2,1,0:T(8,128)(2,1)} %broadcast_in_dim.6), calls=%async_computation | async-start | bytes 294912 | tf_op jit(solution)/shard_map/all_to_all | solution.py:36
  26.7 1.0 copy-done
  28.4 1.8 %shard_map.145 = (f32[32,128]{1,0:T(8,128)S(1)}, f32[32,128]{1,0:T(8,128)S(1)}, f32[32,128]{1,0:T(8,128)S(1)}, f32[32,128]{1,0:T(8,128)S(1)}, f32[32,128]{1,0:T(...) custom-call(bf16[64,32,128]{2,1,0:T(8,128)(2,1)S(1)} %bitcast.13, ...), custom_call_target="tpu_custom_call" | custom-call | flops 50331648 | bytes 655360 | tf_op jit(solution)/shard_map/pallas_call | solution.py:232
  30.7 2.9 %collective-permute-start = (f32[32,128]{1,0:T(8,128)S(1)}, f32[32,128]{1,0:T(8,128)S(1)}, u32[]{:S(2)}, u32[]{:S(2)}) collective-permute-start(f32[32,128]{1,0:T(8,128)S(1)} %get-tuple-element.41), channel_id=1, source_target_pairs={{0,1},{1,0},{2,3},{3,2},{4,5},{5,4},{6,7},{7,6},{8,9},{9,8},{10,11... | collective-permute-start | bytes 49160 | tf_op jit(solution)/shard_map/ppermute | solution.py:51
  33.6 2.6 %collective-permute-start.1 = (f32[32,128]{1,0:T(8,128)S(1)}, f32[32,128]{1,0:T(8,128)S(1)}, u32[]{:S(2)}, u32[]{:S(2)}) collective-permute-start(f32[32,128]{1,0:T(8,128)S(1)} %get-tuple-element.42), channel_id=1, source_target_pairs={{0,2},{1,3},{2,0},{3,1},{4,6},{5,7},{6,4},{7,5},{8,10},{9,11},{10,... | collective-permute-start | bytes 49160 | tf_op jit(solution)/shard_map/ppermute | solution.py:51
  36.3 2.8 %collective-permute-start.2 = (f32[32,128]{1,0:T(8,128)S(1)}, f32[32,128]{1,0:T(8,128)S(1)}, u32[]{:S(2)}, u32[]{:S(2)}) collective-permute-start(f32[32,128]{1,0:T(8,128)S(1)} %get-tuple-element.43), channel_id=1, source_target_pairs={{0,3},{1,2},{2,1},{3,0},{4,7},{5,6},{6,5},{7,4},{8,11},{9,10},{10,... | collective-permute-start | bytes 49160 | tf_op jit(solution)/shard_map/ppermute | solution.py:51
  39.1 2.3 %collective-permute-done.2.refs_3_ = f32[32,128]{1,0:T(8,128)S(1)} collective-permute-done((f32[32,128]{1,0:T(8,128)S(1)}, f32[32,128]{1,0:T(8,128)S(1)}, u32[]{:S(2)}, u32[]{:S(2)}) %collective-permute-start.2) | collective-permute-done | bytes 16416 | tf_op jit(solution)/shard_map/ppermute | solution.py:51
  41.6 0.9 broadcast_in_dim.7
  42.5 6.8 %all-to-all-start.1 = ((bf16[16,48,384]{2,1,0:T(8,128)(2,1)}), bf16[16,48,384]{2,1,0:T(8,128)(2,1)S(1)}, u32[]{:S(2)}, u32[]{:S(2)}) async-start(bf16[16,48,384]{2,1,0:T(8,128)(2,1)} %broadcast_in_dim.7), calls=%async_computation.1 | async-start | bytes 1179648 | tf_op jit(solution)/shard_map/all_to_all | solution.py:36
  49.2 3.4 %collective-permute-start.3 = (bf16[48,672]{1,0:T(8,128)(2,1)S(1)}, bf16[48,672]{1,0:T(8,128)(2,1)S(1)}, u32[]{:S(2)}, u32[]{:S(2)}) collective-permute-start(bf16[48,672]{1,0:T(8,128)(2,1)S(1)} %slice.49), channel_id=1, source_target_pairs={{0,4},{1,5},{2,6},{3,7},{4,0},{5,1},{6,2},{7,3},{8,12},{9,13},{10,... | collective-permute-start | bytes 193544 | tf_op jit(solution)/shard_map/ppermute | solution.py:51
  52.8 2.4 %collective-permute-start.4 = (bf16[48,96]{1,0:T(8,128)(2,1)S(1)}, bf16[48,96]{1,0:T(8,128)(2,1)S(1)}, u32[]{:S(2)}, u32[]{:S(2)}) collective-permute-start(bf16[48,96]{1,0:T(8,128)(2,1)S(1)} %slice.50), channel_id=1, source_target_pairs={{0,2},{1,3},{2,0},{3,1},{4,6},{5,7},{6,4},{7,5},{8,10},{9,11},{10,... | collective-permute-start | bytes 27656 | tf_op jit(solution)/shard_map/ppermute | solution.py:51
  55.1 3.5 %collective-permute-start.5 = (bf16[48,96]{1,0:T(8,128)(2,1)S(1)}, bf16[48,96]{1,0:T(8,128)(2,1)S(1)}, u32[]{:S(2)}, u32[]{:S(2)}) collective-permute-start(bf16[48,96]{1,0:T(8,128)(2,1)S(1)} %slice.50), channel_id=1, source_target_pairs={{0,6},{1,7},{2,4},{3,5},{4,2},{5,3},{6,0},{7,1},{8,14},{9,15},{10,... | collective-permute-start | bytes 27656 | tf_op jit(solution)/shard_map/ppermute | solution.py:51
  58.8 2.8 %collective-permute-done.5 = bf16[48,96]{1,0:T(8,128)(2,1)S(1)} collective-permute-done((bf16[48,96]{1,0:T(8,128)(2,1)S(1)}, bf16[48,96]{1,0:T(8,128)(2,1)S(1)}, u32[]{:S(2)}, u32[]{:S(2)}) %collective-permute-start.5) | collective-permute-done | bytes 9248 | tf_op jit(solution)/shard_map/ppermute | solution.py:51
  61.8 1.7 %broadcast_in_dim.8 = bf16[16,48,1536]{2,1,0:T(8,128)(2,1)} broadcast(bf16[48,1536]{1,0:T(8,128)(2,1)S(1)} %concatenate.7), dimensions={1,2} | broadcast | bytes 2506752 | tf_op jit(solution)/shard_map/broadcast_in_dim | solution.py:319
  63.5 6.5 %all-to-all-start.2 = ((bf16[16,48,1536]{2,1,0:T(8,128)(2,1)}), bf16[16,48,1536]{2,1,0:T(8,128)(2,1)}, u32[]{:S(2)}, u32[]{:S(2)}) async-start(bf16[16,48,1536]{2,1,0:T(8,128)(2,1)} %broadcast_in_dim.8), calls=%async_computation.2 | async-start | bytes 4718592 | tf_op jit(solution)/shard_map/all_to_all | solution.py:36
  70.0 1.9 %collective-permute-start.6 = (f32[32,128]{1,0:T(8,128)S(1)}, f32[32,128]{1,0:T(8,128)S(1)}, u32[]{:S(2)}, u32[]{:S(2)}) collective-permute-start(f32[32,128]{1,0:T(8,128)S(1)} %get-tuple-element.52), channel_id=1, source_target_pairs={{0,4},{1,5},{2,6},{3,7},{4,0},{5,1},{6,2},{7,3},{8,12},{9,13},{10,... | collective-permute-start | bytes 49160 | tf_op jit(solution)/shard_map/ppermute | solution.py:51
  71.9 7.9 %collective-permute-start.7 = (f32[32,128]{1,0:T(8,128)S(1)}, f32[32,128]{1,0:T(8,128)S(1)}, u32[]{:S(2)}, u32[]{:S(2)}) collective-permute-start(f32[32,128]{1,0:T(8,128)S(1)} %get-tuple-element.53), channel_id=1, source_target_pairs={{0,5},{1,4},{2,7},{3,6},{4,1},{5,0},{6,3},{7,2},{8,13},{9,12},{10,... | collective-permute-start | bytes 49160 | tf_op jit(solution)/shard_map/ppermute | solution.py:51
  79.8 3.4 %collective-permute-start.8 = (f32[32,128]{1,0:T(8,128)S(1)}, f32[32,128]{1,0:T(8,128)S(1)}, u32[]{:S(2)}, u32[]{:S(2)}) collective-permute-start(f32[32,128]{1,0:T(8,128)S(1)} %get-tuple-element.54), channel_id=1, source_target_pairs={{0,6},{1,7},{2,4},{3,5},{4,2},{5,3},{6,0},{7,1},{8,14},{9,15},{10,... | collective-permute-start | bytes 49160 | tf_op jit(solution)/shard_map/ppermute | solution.py:51
  83.2 1.9 %collective-permute-start.9 = (f32[32,128]{1,0:T(8,128)S(1)}, f32[32,128]{1,0:T(8,128)S(1)}, u32[]{:S(2)}, u32[]{:S(2)}) collective-permute-start(f32[32,128]{1,0:T(8,128)S(1)} %get-tuple-element.55), channel_id=1, source_target_pairs={{0,7},{1,6},{2,5},{3,4},{4,3},{5,2},{6,1},{7,0},{8,15},{9,14},{10,... | collective-permute-start | bytes 49160 | tf_op jit(solution)/shard_map/ppermute | solution.py:51
  85.2 1.3 collective-permute-done.8.refs_6_
  86.5 4.0 %collective-permute-done.9.refs_7_ = f32[32,128]{1,0:T(8,128)S(1)} collective-permute-done((f32[32,128]{1,0:T(8,128)S(1)}, f32[32,128]{1,0:T(8,128)S(1)}, u32[]{:S(2)}, u32[]{:S(2)}) %collective-permute-start.9) | collective-permute-done | bytes 16416 | tf_op jit(solution)/shard_map/ppermute | solution.py:51
  90.5 1.9 %collective-permute-start.10 = (bf16[16,64,768]{2,1,0:T(8,128)(2,1)}, bf16[16,64,768]{2,1,0:T(8,128)(2,1)}, u32[]{:S(2)}, u32[]{:S(2)}) collective-permute-start(bf16[16,64,768]{2,1,0:T(8,128)(2,1)} %all-gather.3.cloned.1.call-done.x_ref), channel_id=1, source_target_pairs={{0,1},{1,0},{2,3},{3,2},{4,5},{5,4},{6,7},{7,6},{8,9},{9,8},{10,11... | collective-permute-start | bytes 4718600 | tf_op jit(solution)/shard_map/ppermute | solution.py:51
  93.0 5.4 %shard_map.146 = (bf16[8,128,192]{2,1,0:T(8,128)(2,1)}, f32[256,192]{1,0:T(8,128)}) custom-call(bf16[16,64,768]{2,1,0:T(8,128)(2,1)} %all-gather.3.cloned.1.call-done.x_ref, f32[768]{0:T(1024)} %gain_ref.6, bf16[16,48,384]{2,1,0:T(8,128)(2,1)} %copy-done.5), custom_call_target="tpu_custom_call" | custom-call | flops 452984832 | bytes 2162688 | tf_op jit(solution)/shard_map/pallas_call | solution.py:232
  98.5 7.1 %shard_map.147 = bf16[8,64,96]{2,1,0:T(8,128)(2,1)} custom-call(s32[1]{0:T(128)S(6)} %copy.21.length_ref, bf16[16,64,768]{2,1,0:T(8,128)(2,1)} %collective-permute-done.10.x_ref, f32[768]{0:T(1024)} %gain_ref.6, bf16[16,48,384]{2,1,0:T(8,128)(2,1)} %copy-done.5, bf16[8,128,192]{2,1,0:T(8,128)(2,1)} %get-tuple-element.58.kv_ref, ...), custom_call_target="tpu_custom_call" | custom-call | flops 452984832 | bytes 2162688 | tf_op jit(solution)/shard_map/pallas_call | solution.py:232
  105.6 1.1 slice.47.w_ref
  106.8 2.4 %collective-permute-start.11 = (bf16[16,48,384]{2,1,0:T(8,128)(2,1)S(1)}, bf16[16,48,384]{2,1,0:T(8,128)(2,1)S(1)}, u32[]{:S(2)}, u32[]{:S(2)}) collective-permute-start(bf16[16,48,384]{2,1,0:T(8,128)(2,1)S(1)} %slice.47.w_ref), channel_id=1, source_target_pairs={{0,1},{1,0},{2,3},{3,2},{4,5},{5,4},{6,7},{7,6},{8,9},{9,8},{10,11... | collective-permute-start | bytes 1769480 | tf_op jit(solution)/shard_map/ppermute | solution.py:51
  109.2 9.2 %all_to_all.25.gated_ref = bf16[8,64,96]{2,1,0:T(8,128)(2,1)S(1)} all-to-all(bf16[8,64,96]{2,1,0:T(8,128)(2,1)} %shard_map.147), channel_id=1, replica_groups=mesh['grp'=16,'pb'=4,'ka'=8] {'ka'}, dimensions={0} | all-to-all | bytes 196608 | tf_op jit(solution)/shard_map/all_to_all | solution.py:36
  119.2 7.0 %all-gather = bf16[256,768]{1,0:T(8,128)(2,1)S(1)} all-gather(bf16[64,768]{1,0:T(8,128)(2,1)S(1)} %get-tuple-element.72), channel_id=2, replica_groups={{0,1,2,3},{4,5,6,7},{8,9,10,11},{12,13,14,15},{16,17,18,19},{20,21,22,2..., dimensions={0}, use_global_device_ids=true | all-gather | bytes 491520 | tf_op jit(solution)/shard_map/all_gather | solution.py:371
  126.1 2.2 %shard_map.149 = bf16[4,64,768]{2,1,0:T(8,128)(2,1)S(1)} custom-call(bf16[4,64,768]{2,1,0:T(8,128)(2,1)S(1)} %bitcast.12, bf16[16,48,1536]{2,1,0:T(8,128)(2,1)} %all-to-all-done.2.w_ref), custom_call_target="tpu_custom_call" | custom-call | flops 452984832 | bytes 1769472 | tf_op jit(solution)/shard_map/pallas_call | solution.py:232
  128.4 9.0 %all_to_all.26.part_ref = bf16[4,64,768]{2,1,0:T(8,128)(2,1)S(1)} all-to-all(bf16[4,64,768]{2,1,0:T(8,128)(2,1)S(1)} %shard_map.149), channel_id=1, replica_groups={{0,1,2,3},{4,5,6,7},{8,9,10,11},{12,13,14,15},{16,17,18,19},{20,21,22,2..., dimensions={0} | all-to-all | bytes 786432 | tf_op jit(solution)/shard_map/all_to_all | solution.py:36
  (53 shorter events, 6.2 us)
Async XLA Ops:
  6.5 83.9 %all-gather.3.cloned.1.call-start = ((), (), s32[]{:S(2)}) async-start(), calls=%async_computation.5 | async-start | bytes 1671168 | tf_op jit(solution)/shard_map/all_gather | solution.py:280
  10.3 31.1 %all-to-all-start = ((bf16[4,12,1056]{2,1,0:T(8,128)(2,1)}), bf16[4,12,1056]{2,1,0:T(8,128)(2,1)S(1)}, u32[]{:S(2)}, u32[]{:S(2)}) async-start(bf16[4,12,1056]{2,1,0:T(8,128)(2,1)} %broadcast_in_dim.6), calls=%async_computation | async-start | bytes 294912 | tf_op jit(solution)/shard_map/all_to_all | solution.py:36
  26.7 1.0 copy-start
  27.7 0.7 copy-start.4
  30.1 0.6 copy-start.2
  30.7 8.3 %collective-permute-start = (f32[32,128]{1,0:T(8,128)S(1)}, f32[32,128]{1,0:T(8,128)S(1)}, u32[]{:S(2)}, u32[]{:S(2)}) collective-permute-start(f32[32,128]{1,0:T(8,128)S(1)} %get-tuple-element.41), channel_id=1, source_target_pairs={{0,1},{1,0},{2,3},{3,2},{4,5},{5,4},{6,7},{7,6},{8,9},{9,8},{10,11... | collective-permute-start | bytes 49160 | tf_op jit(solution)/shard_map/ppermute | solution.py:51
  33.6 5.5 %collective-permute-start.1 = (f32[32,128]{1,0:T(8,128)S(1)}, f32[32,128]{1,0:T(8,128)S(1)}, u32[]{:S(2)}, u32[]{:S(2)}) collective-permute-start(f32[32,128]{1,0:T(8,128)S(1)} %get-tuple-element.42), channel_id=1, source_target_pairs={{0,2},{1,3},{2,0},{3,1},{4,6},{5,7},{6,4},{7,5},{8,10},{9,11},{10,... | collective-permute-start | bytes 49160 | tf_op jit(solution)/shard_map/ppermute | solution.py:51
  36.3 5.2 %collective-permute-start.2 = (f32[32,128]{1,0:T(8,128)S(1)}, f32[32,128]{1,0:T(8,128)S(1)}, u32[]{:S(2)}, u32[]{:S(2)}) collective-permute-start(f32[32,128]{1,0:T(8,128)S(1)} %get-tuple-element.43), channel_id=1, source_target_pairs={{0,3},{1,2},{2,1},{3,0},{4,7},{5,6},{6,5},{7,4},{8,11},{9,10},{10,... | collective-permute-start | bytes 49160 | tf_op jit(solution)/shard_map/ppermute | solution.py:51
  39.1 24.4 %copy-start.6 = (f32[32,128]{1,0:T(8,128)}, f32[32,128]{1,0:T(8,128)S(1)}, u32[]{:S(2)}) copy-start(f32[32,128]{1,0:T(8,128)S(1)} %collective-permute-done.refs_1_) | copy-start | bytes 49156
  39.1 24.4 %copy-start.7 = (f32[32,128]{1,0:T(8,128)}, f32[32,128]{1,0:T(8,128)S(1)}, u32[]{:S(2)}) copy-start(f32[32,128]{1,0:T(8,128)S(1)} %collective-permute-done.1.refs_2_) | copy-start | bytes 49156
  41.4 22.1 %copy-start.8 = (f32[32,128]{1,0:T(8,128)}, f32[32,128]{1,0:T(8,128)S(1)}, u32[]{:S(2)}) copy-start(f32[32,128]{1,0:T(8,128)S(1)} %collective-permute-done.2.refs_3_) | copy-start | bytes 49156
  42.5 19.3 %all-to-all-start.1 = ((bf16[16,48,384]{2,1,0:T(8,128)(2,1)}), bf16[16,48,384]{2,1,0:T(8,128)(2,1)S(1)}, u32[]{:S(2)}, u32[]{:S(2)}) async-start(bf16[16,48,384]{2,1,0:T(8,128)(2,1)} %broadcast_in_dim.7), calls=%async_computation.1 | async-start | bytes 1179648 | tf_op jit(solution)/shard_map/all_to_all | solution.py:36
  49.2 9.4 %collective-permute-start.3 = (bf16[48,672]{1,0:T(8,128)(2,1)S(1)}, bf16[48,672]{1,0:T(8,128)(2,1)S(1)}, u32[]{:S(2)}, u32[]{:S(2)}) collective-permute-start(bf16[48,672]{1,0:T(8,128)(2,1)S(1)} %slice.49), channel_id=1, source_target_pairs={{0,4},{1,5},{2,6},{3,7},{4,0},{5,1},{6,2},{7,3},{8,12},{9,13},{10,... | collective-permute-start | bytes 193544 | tf_op jit(solution)/shard_map/ppermute | solution.py:51
  52.8 6.1 %collective-permute-start.4 = (bf16[48,96]{1,0:T(8,128)(2,1)S(1)}, bf16[48,96]{1,0:T(8,128)(2,1)S(1)}, u32[]{:S(2)}, u32[]{:S(2)}) collective-permute-start(bf16[48,96]{1,0:T(8,128)(2,1)S(1)} %slice.50), channel_id=1, source_target_pairs={{0,2},{1,3},{2,0},{3,1},{4,6},{5,7},{6,4},{7,5},{8,10},{9,11},{10,... | collective-permute-start | bytes 27656 | tf_op jit(solution)/shard_map/ppermute | solution.py:51
  55.1 6.5 %collective-permute-start.5 = (bf16[48,96]{1,0:T(8,128)(2,1)S(1)}, bf16[48,96]{1,0:T(8,128)(2,1)S(1)}, u32[]{:S(2)}, u32[]{:S(2)}) collective-permute-start(bf16[48,96]{1,0:T(8,128)(2,1)S(1)} %slice.50), channel_id=1, source_target_pairs={{0,6},{1,7},{2,4},{3,5},{4,2},{5,3},{6,0},{7,1},{8,14},{9,15},{10,... | collective-permute-start | bytes 27656 | tf_op jit(solution)/shard_map/ppermute | solution.py:51
  61.8 1.7 %copy-start.5 = (bf16[16,48,384]{2,1,0:T(8,128)(2,1)}, bf16[16,48,384]{2,1,0:T(8,128)(2,1)S(1)}, u32[]{:S(2)}) copy-start(bf16[16,48,384]{2,1,0:T(8,128)(2,1)S(1)} %all-to-all-done.1.w_ref) | copy-start | bytes 1769476
  63.5 42.1 %all-to-all-start.2 = ((bf16[16,48,1536]{2,1,0:T(8,128)(2,1)}), bf16[16,48,1536]{2,1,0:T(8,128)(2,1)}, u32[]{:S(2)}, u32[]{:S(2)}) async-start(bf16[16,48,1536]{2,1,0:T(8,128)(2,1)} %broadcast_in_dim.8), calls=%async_computation.2 | async-start | bytes 4718592 | tf_op jit(solution)/shard_map/all_to_all | solution.py:36
  70.0 15.2 %collective-permute-start.6 = (f32[32,128]{1,0:T(8,128)S(1)}, f32[32,128]{1,0:T(8,128)S(1)}, u32[]{:S(2)}, u32[]{:S(2)}) collective-permute-start(f32[32,128]{1,0:T(8,128)S(1)} %get-tuple-element.52), channel_id=1, source_target_pairs={{0,4},{1,5},{2,6},{3,7},{4,0},{5,1},{6,2},{7,3},{8,12},{9,13},{10,... | collective-permute-start | bytes 49160 | tf_op jit(solution)/shard_map/ppermute | solution.py:51
  71.9 13.3 %collective-permute-start.7 = (f32[32,128]{1,0:T(8,128)S(1)}, f32[32,128]{1,0:T(8,128)S(1)}, u32[]{:S(2)}, u32[]{:S(2)}) collective-permute-start(f32[32,128]{1,0:T(8,128)S(1)} %get-tuple-element.53), channel_id=1, source_target_pairs={{0,5},{1,4},{2,7},{3,6},{4,1},{5,0},{6,3},{7,2},{8,13},{9,12},{10,... | collective-permute-start | bytes 49160 | tf_op jit(solution)/shard_map/ppermute | solution.py:51
  79.8 6.7 %collective-permute-start.8 = (f32[32,128]{1,0:T(8,128)S(1)}, f32[32,128]{1,0:T(8,128)S(1)}, u32[]{:S(2)}, u32[]{:S(2)}) collective-permute-start(f32[32,128]{1,0:T(8,128)S(1)} %get-tuple-element.54), channel_id=1, source_target_pairs={{0,6},{1,7},{2,4},{3,5},{4,2},{5,3},{6,0},{7,1},{8,14},{9,15},{10,... | collective-permute-start | bytes 49160 | tf_op jit(solution)/shard_map/ppermute | solution.py:51
  83.2 7.3 %collective-permute-start.9 = (f32[32,128]{1,0:T(8,128)S(1)}, f32[32,128]{1,0:T(8,128)S(1)}, u32[]{:S(2)}, u32[]{:S(2)}) collective-permute-start(f32[32,128]{1,0:T(8,128)S(1)} %get-tuple-element.55), channel_id=1, source_target_pairs={{0,7},{1,6},{2,5},{3,4},{4,3},{5,2},{6,1},{7,0},{8,15},{9,14},{10,... | collective-permute-start | bytes 49160 | tf_op jit(solution)/shard_map/ppermute | solution.py:51
  85.2 13.3 %copy-start.9 = (f32[32,128]{1,0:T(8,128)}, f32[32,128]{1,0:T(8,128)S(1)}, u32[]{:S(2)}) copy-start(f32[32,128]{1,0:T(8,128)S(1)} %collective-permute-done.6.refs_4_) | copy-start | bytes 49156
  85.2 13.3 %copy-start.10 = (f32[32,128]{1,0:T(8,128)}, f32[32,128]{1,0:T(8,128)S(1)}, u32[]{:S(2)}) copy-start(f32[32,128]{1,0:T(8,128)S(1)} %collective-permute-done.7.refs_5_) | copy-start | bytes 49156
  86.4 12.1 %copy-start.11 = (f32[32,128]{1,0:T(8,128)}, f32[32,128]{1,0:T(8,128)S(1)}, u32[]{:S(2)}) copy-start(f32[32,128]{1,0:T(8,128)S(1)} %collective-permute-done.8.refs_6_) | copy-start | bytes 49156
  90.5 8.0 %copy-start.12 = (f32[32,128]{1,0:T(8,128)}, f32[32,128]{1,0:T(8,128)S(1)}, u32[]{:S(2)}) copy-start(f32[32,128]{1,0:T(8,128)S(1)} %collective-permute-done.9.refs_7_) | copy-start | bytes 49156
  90.5 8.0 %collective-permute-start.10 = (bf16[16,64,768]{2,1,0:T(8,128)(2,1)}, bf16[16,64,768]{2,1,0:T(8,128)(2,1)}, u32[]{:S(2)}, u32[]{:S(2)}) collective-permute-start(bf16[16,64,768]{2,1,0:T(8,128)(2,1)} %all-gather.3.cloned.1.call-done.x_ref), channel_id=1, source_target_pairs={{0,1},{1,0},{2,3},{3,2},{4,5},{5,4},{6,7},{7,6},{8,9},{9,8},{10,11... | collective-permute-start | bytes 4718600 | tf_op jit(solution)/shard_map/ppermute | solution.py:51
  98.5 19.9 %copy-start.1 = (bf16[1,8,8,768]{3,2,1,0:T(8,128)(2,1)S(1)}, bf16[1,8,8,768]{3,2,1,0:T(8,128)(2,1)}, u32[]{:S(2)}) copy-start(bf16[1,8,8,768]{3,2,1,0:T(8,128)(2,1)} %param.16) | copy-start | bytes 294916
  98.5 19.9 %copy-start.3 = (f32[768]{0:T(1024)S(1)}, f32[768]{0:T(1024)}, u32[]{:S(2)}) copy-start(f32[768]{0:T(1024)} %gain_ref.7) | copy-start | bytes 9220
  106.8 11.6 %collective-permute-start.11 = (bf16[16,48,384]{2,1,0:T(8,128)(2,1)S(1)}, bf16[16,48,384]{2,1,0:T(8,128)(2,1)S(1)}, u32[]{:S(2)}, u32[]{:S(2)}) collective-permute-start(bf16[16,48,384]{2,1,0:T(8,128)(2,1)S(1)} %slice.47.w_ref), channel_id=1, source_target_pairs={{0,1},{1,0},{2,3},{3,2},{4,5},{5,4},{6,7},{7,6},{8,9},{9,8},{10,11... | collective-permute-start | bytes 1769480 | tf_op jit(solution)/shard_map/ppermute | solution.py:51
Sparse Core Ops, SparseCore 0:
  9.4 71.2 all-gather.2

commit v5 on v4

--- a/solution.py
+++ b/solution.py
@@ -73,52 +73,68 @@
         out_ref[...] = held[lax.axis_index("ka") ^ flip]
 
 
-def project_side(samples, x_ref, gain_ref, w_ref, raw_ref, held_ref, sems, kv_ref):
-    places, own_rows, width = x_ref.shape
-    feats = kv_ref.shape[2] // 2
-    each = own_rows // samples
-    blocks = lax.axis_size("pb")
-    chips = places // blocks
+def load_side(blocks, x_ref, w_ref, raw_ref, weights_ref, sems):
+    chips = x_ref.shape[0] // blocks
     copies = [
         pltpu.make_async_copy(
             x_ref.at[pl.ds(b * chips, chips)], raw_ref.at[pl.ds(b * chips, chips)], sems.at[b]
         )
         for b in range(blocks)
     ]
+    copies.append(pltpu.make_async_copy(w_ref, weights_ref, sems.at[blocks]))
     for copy in copies:
         copy.start()
-    weights = w_ref[...].reshape(width, 4 * feats)
-    for b, copy in enumerate(copies):
-        copy.wait()
+    return copies
+
+
+def project_side(samples, copies, gain_ref, raw_ref, weights_ref, held_ref, kv_ref):
+    places, own_rows, width = raw_ref.shape
+    feats = kv_ref.shape[2] // 2
+    each = own_rows // samples
+    blocks = len(copies) - 1
+    chips = places // blocks
+    for b in range(blocks):
+        copies[b].wait()
         part = slice(b * chips, (b + 1) * chips)
         x = raw_ref[part].reshape(chips * own_rows, width).astype(f32)
         normed = layer_norm(x, gain_ref[...].reshape(1, -1)).astype(bf16)
         held_ref[part] = normed.reshape(chips, own_rows, width)
-        proj = jnp.dot(normed, weights[:, : 2 * feats], preferred_element_type=f32)
-        proj = proj.reshape(chips, samples, each, 2 * feats)
-        rows = slice(b * chips * each, (b + 1) * chips * each)
-        for s in range(samples):
-            kv_ref[s, rows] = proj[:, s].reshape(chips * each, 2 * feats).astype(bf16)
+    copies[blocks].wait()
+    weights = weights_ref[...].reshape(width, 4 * feats)
+    normed = held_ref[...].reshape(places * own_rows, width)
+    proj = jnp.dot(normed, weights[:, : 2 * feats], preferred_element_type=f32)
+    proj = proj.reshape(places, samples, each, 2 * feats)
+    for s in range(samples):
+        kv_ref[s] = proj[:, s].reshape(places * each, 2 * feats).astype(bf16)
     rows = held_ref[pl.ds(lax.axis_index("pb") * chips, chips)].reshape(chips * own_rows, width)
     return jnp.dot(rows, weights[:, 2 * feats :], preferred_element_type=f32)
 
 
-def project_kernel(x_ref, gain_ref, w_ref, kv_ref, query_ref, raw_ref, held_ref, sems):
-    samples = kv_ref.shape[0]
+def project_kernel(x_ref, gain_ref, w_ref, kv_ref, query_ref, raw, weights, held, sems):
+    blocks = lax.axis_size("pb")
+    copies = load_side(blocks, x_ref, w_ref, raw, weights, sems)
     query_ref[...] = project_side(
-        samples, x_ref, gain_ref, w_ref, raw_ref, held_ref, sems, kv_ref
-    )
-
-
-def attention_kernel(length_ref, x_ref, gain_ref, w_ref, kv_ref, near_ref, *refs):
-    count = len(refs) - 8
+        kv_ref.shape[0], copies, gain_ref, raw, weights, held, kv_ref
+    )
+
+
+def attention_kernel(length_ref, x_ref, gain_ref, w_ref, near_kv_ref, near_ref, *refs):
+    count = len(refs) - 11
     bias_refs = refs[:count]
-    out_ref, raw, held_normed, sems, held_kv, held_bias, held_query, held_gate = refs[count:]
+    out_ref, raw, weights, held_normed, sems, kv_ref, near, held_kv = refs[count : count + 8]
+    held_bias, held_query, held_gate = refs[count + 8 :]
+    blocks = lax.axis_size("pb")
+    copies = load_side(blocks, x_ref, w_ref, raw, weights, sems)
+    later = [
+        pltpu.make_async_copy(near_ref, near, sems.at[blocks + 1]),
+        pltpu.make_async_copy(near_kv_ref, kv_ref, sems.at[blocks + 2]),
+    ]
+    for copy in later:
+        copy.start()
     places, own_rows, width = x_ref.shape
     samples, span, feats = kv_ref.shape
     feats = feats // 2
     chips = count // 2
-    blocks = places // chips
     keys_held, lanes = bias_refs[0].shape
     q_rows = lanes // 2
     each = q_rows // count
@@ -126,8 +142,10 @@
     head_dim = feats // 2
     length, at = length_ref[0], lax.axis_index("ka")
     core = at % 2
-    far = project_side(samples, x_ref, gain_ref, w_ref, raw, held_normed, sems, held_kv)
-    for side, proj in enumerate((near_ref[...], far)):
+    far = project_side(samples, copies, gain_ref, raw, weights, held_normed, held_kv)
+    for copy in later:
+        copy.wait()
+    for side, proj in enumerate((near[...], far)):
         for z in range(chips):
             k = 2 * z + (core ^ side)
             part = proj[z * own_rows : (z + 1) * own_rows]
@@ -330,12 +348,17 @@
     costs = dict(
         flops=2 * x.size * 3 * feats, moved=x.size * 2 + attn_w.size * 2, limit=MOST_VMEM
     )
-    rows_held = [pltpu.VMEM(x.shape, bf16)] * 2 + [pltpu.SemaphoreType.DMA((pb_count,))]
+    rows_held = [
+        pltpu.VMEM(x.shape, bf16),
+        pltpu.VMEM(attn_w.shape, bf16),
+        pltpu.VMEM(x.shape, bf16),
+        pltpu.SemaphoreType.DMA((pb_count + 3,)),
+    ]
     near_kv, near_query = call(
         project_kernel,
         (jax.ShapeDtypeStruct(kv_shape, bf16), jax.ShapeDtypeStruct(query_shape, f32)),
         scratch=rows_held,
-        left=(0,),
+        left=(0, 2),
         **costs,
     )(x, attn_gain, attn_w)
     gated = call(
@@ -344,12 +367,14 @@
         scratch=rows_held
         + [
             pltpu.VMEM(kv_shape, bf16),
+            pltpu.VMEM(query_shape, f32),
+            pltpu.VMEM(kv_shape, bf16),
             pltpu.VMEM((ka_count, keys_held, lanes), f32),
             pltpu.VMEM((ka_count, own_rows, feats), f32),
             pltpu.VMEM((ka_count, own_rows, feats), f32),
         ],
         scalars=1,
-        left=(1,),
+        left=(1, 3, 4, 5),
         **costs,
     )(lengths, other, attn_gain, attn_w, near_kv, near_query, *bias)
     gated, late = lax.optimization_barrier((gated, late))

time: 146 us -> 145 us (level)
  transfers between devices with their start and end apart: 16 -> 16, of which waited for: 4 -> 4; matrix products, arithmetic and copies ran while one was open for 5% -> 5% of each run, Pallas kernels for 10% -> 9%
where the time goes in v5:
time: 145 us; the launch traced here: 144 us
  starting transfers between devices  65.9 us (45%)
  blocking collectives  25.1 us (17%)
  Pallas kernels  16.6 us (11%)
  between operations  14.4 us (10%)
  waiting for transfers between devices  11.2 us (8%)
  local copies, waits for them, and re-layouts  10.4 us (7%)
    ppermute x12, starting transfers between devices, swap(): return lax.ppermute(block, axis, [(i, i ^ flip) for i in range(count)])  37 us
    all_to_all x3, starting transfers between devices, exchange(): lax.all_to_all(blocks, axes, split_axis=0, concat_axis=0, tiled=True, axi...  28.9 us
    all_to_all x2, blocking collectives, exchange(): lax.all_to_all(blocks, axes, split_axis=0, concat_axis=0, tiled=True, axi...  18.2 us
    pallas_call x6, Pallas kernels, run(): pl.pallas_call(kernel, out_shape=out_shape, in_specs=[pl.BlockSpec(memory...  16.6 us
    ppermute x12, waiting for transfers between devices, swap(): return lax.ppermute(block, axis, [(i, i ^ flip) for i in range(count)])  10.4 us
    all_gather x1, blocking collectives, on_device(): lax.all_gather(normed_t, 'ka', axis=0, tiled=False, axis_index_groups=gro...  6.96 us
  transfers between devices with their start and end apart: 16, of which 4 were waited for; matrix products, arithmetic and copies ran while one was open for 5% of the time, Pallas kernels for 9%

profile of v5, /device:TPU:1, one launch (start us, length us, event | category | flops | bytes accessed | tf_op | source)
XLA Modules:
  0.0 143.6 jit_solution(10493707590555773716)
XLA Ops:
  7.3 0.8 constant_dynamic-slice_fusion.2
  8.8 0.8 concatenate.6
  10.3 15.6 %all-to-all-start = ((bf16[4,12,1056]{2,1,0:T(8,128)(2,1)}), bf16[4,12,1056]{2,1,0:T(8,128)(2,1)S(1)}, u32[]{:S(2)}, u32[]{:S(2)}) async-start(bf16[4,12,1056]{2,1,0:T(8,128)(2,1)} %broadcast_in_dim.6), calls=%async_computation | async-start | bytes 294912 | tf_op jit(solution)/shard_map/all_to_all | solution.py:36
  26.7 1.0 copy-done
  28.4 1.8 %shard_map.145 = (f32[32,128]{1,0:T(8,128)S(1)}, f32[32,128]{1,0:T(8,128)S(1)}, f32[32,128]{1,0:T(8,128)S(1)}, f32[32,128]{1,0:T(8,128)S(1)}, f32[32,128]{1,0:T(...) custom-call(bf16[64,32,128]{2,1,0:T(8,128)(2,1)S(1)} %bitcast.13, ...), custom_call_target="tpu_custom_call" | custom-call | flops 50331648 | bytes 655360 | tf_op jit(solution)/shard_map/pallas_call | solution.py:250
  30.7 2.9 %collective-permute-start = (f32[32,128]{1,0:T(8,128)S(1)}, f32[32,128]{1,0:T(8,128)S(1)}, u32[]{:S(2)}, u32[]{:S(2)}) collective-permute-start(f32[32,128]{1,0:T(8,128)S(1)} %get-tuple-element.41), channel_id=1, source_target_pairs={{0,1},{1,0},{2,3},{3,2},{4,5},{5,4},{6,7},{7,6},{8,9},{9,8},{10,11... | collective-permute-start | bytes 49160 | tf_op jit(solution)/shard_map/ppermute | solution.py:51
  33.6 2.6 %collective-permute-start.1 = (f32[32,128]{1,0:T(8,128)S(1)}, f32[32,128]{1,0:T(8,128)S(1)}, u32[]{:S(2)}, u32[]{:S(2)}) collective-permute-start(f32[32,128]{1,0:T(8,128)S(1)} %get-tuple-element.42), channel_id=1, source_target_pairs={{0,2},{1,3},{2,0},{3,1},{4,6},{5,7},{6,4},{7,5},{8,10},{9,11},{10,... | collective-permute-start | bytes 49160 | tf_op jit(solution)/shard_map/ppermute | solution.py:51
  36.3 2.8 %collective-permute-start.2 = (f32[32,128]{1,0:T(8,128)S(1)}, f32[32,128]{1,0:T(8,128)S(1)}, u32[]{:S(2)}, u32[]{:S(2)}) collective-permute-start(f32[32,128]{1,0:T(8,128)S(1)} %get-tuple-element.43), channel_id=1, source_target_pairs={{0,3},{1,2},{2,1},{3,0},{4,7},{5,6},{6,5},{7,4},{8,11},{9,10},{10,... | collective-permute-start | bytes 49160 | tf_op jit(solution)/shard_map/ppermute | solution.py:51
  39.1 2.3 %collective-permute-done.2.refs_3_ = f32[32,128]{1,0:T(8,128)S(1)} collective-permute-done((f32[32,128]{1,0:T(8,128)S(1)}, f32[32,128]{1,0:T(8,128)S(1)}, u32[]{:S(2)}, u32[]{:S(2)}) %collective-permute-start.2) | collective-permute-done | bytes 16416 | tf_op jit(solution)/shard_map/ppermute | solution.py:51
  41.6 0.9 broadcast_in_dim.7
  42.5 6.8 %all-to-all-start.1 = ((bf16[16,48,384]{2,1,0:T(8,128)(2,1)}), bf16[16,48,384]{2,1,0:T(8,128)(2,1)S(1)}, u32[]{:S(2)}, u32[]{:S(2)}) async-start(bf16[16,48,384]{2,1,0:T(8,128)(2,1)} %broadcast_in_dim.7), calls=%async_computation.1 | async-start | bytes 1179648 | tf_op jit(solution)/shard_map/all_to_all | solution.py:36
  49.2 3.4 %collective-permute-start.3 = (bf16[48,672]{1,0:T(8,128)(2,1)S(1)}, bf16[48,672]{1,0:T(8,128)(2,1)S(1)}, u32[]{:S(2)}, u32[]{:S(2)}) collective-permute-start(bf16[48,672]{1,0:T(8,128)(2,1)S(1)} %slice.49), channel_id=1, source_target_pairs={{0,4},{1,5},{2,6},{3,7},{4,0},{5,1},{6,2},{7,3},{8,12},{9,13},{10,... | collective-permute-start | bytes 193544 | tf_op jit(solution)/shard_map/ppermute | solution.py:51
  52.8 2.4 %collective-permute-start.4 = (bf16[48,96]{1,0:T(8,128)(2,1)S(1)}, bf16[48,96]{1,0:T(8,128)(2,1)S(1)}, u32[]{:S(2)}, u32[]{:S(2)}) collective-permute-start(bf16[48,96]{1,0:T(8,128)(2,1)S(1)} %slice.50), channel_id=1, source_target_pairs={{0,2},{1,3},{2,0},{3,1},{4,6},{5,7},{6,4},{7,5},{8,10},{9,11},{10,... | collective-permute-start | bytes 27656 | tf_op jit(solution)/shard_map/ppermute | solution.py:51
  55.1 3.5 %collective-permute-start.5 = (bf16[48,96]{1,0:T(8,128)(2,1)S(1)}, bf16[48,96]{1,0:T(8,128)(2,1)S(1)}, u32[]{:S(2)}, u32[]{:S(2)}) collective-permute-start(bf16[48,96]{1,0:T(8,128)(2,1)S(1)} %slice.50), channel_id=1, source_target_pairs={{0,6},{1,7},{2,4},{3,5},{4,2},{5,3},{6,0},{7,1},{8,14},{9,15},{10,... | collective-permute-start | bytes 27656 | tf_op jit(solution)/shard_map/ppermute | solution.py:51
  58.8 2.8 %collective-permute-done.5 = bf16[48,96]{1,0:T(8,128)(2,1)S(1)} collective-permute-done((bf16[48,96]{1,0:T(8,128)(2,1)S(1)}, bf16[48,96]{1,0:T(8,128)(2,1)S(1)}, u32[]{:S(2)}, u32[]{:S(2)}) %collective-permute-start.5) | collective-permute-done | bytes 9248 | tf_op jit(solution)/shard_map/ppermute | solution.py:51
  61.8 1.7 %broadcast_in_dim.8 = bf16[16,48,1536]{2,1,0:T(8,128)(2,1)} broadcast(bf16[48,1536]{1,0:T(8,128)(2,1)S(1)} %concatenate.7), dimensions={1,2} | broadcast | bytes 2506752 | tf_op jit(solution)/shard_map/broadcast_in_dim | solution.py:337
  63.5 6.5 %all-to-all-start.2 = ((bf16[16,48,1536]{2,1,0:T(8,128)(2,1)}), bf16[16,48,1536]{2,1,0:T(8,128)(2,1)}, u32[]{:S(2)}, u32[]{:S(2)}) async-start(bf16[16,48,1536]{2,1,0:T(8,128)(2,1)} %broadcast_in_dim.8), calls=%async_computation.2 | async-start | bytes 4718592 | tf_op jit(solution)/shard_map/all_to_all | solution.py:36
  70.0 1.9 %collective-permute-start.6 = (f32[32,128]{1,0:T(8,128)S(1)}, f32[32,128]{1,0:T(8,128)S(1)}, u32[]{:S(2)}, u32[]{:S(2)}) collective-permute-start(f32[32,128]{1,0:T(8,128)S(1)} %get-tuple-element.52), channel_id=1, source_target_pairs={{0,4},{1,5},{2,6},{3,7},{4,0},{5,1},{6,2},{7,3},{8,12},{9,13},{10,... | collective-permute-start | bytes 49160 | tf_op jit(solution)/shard_map/ppermute | solution.py:51
  71.9 7.9 %collective-permute-start.7 = (f32[32,128]{1,0:T(8,128)S(1)}, f32[32,128]{1,0:T(8,128)S(1)}, u32[]{:S(2)}, u32[]{:S(2)}) collective-permute-start(f32[32,128]{1,0:T(8,128)S(1)} %get-tuple-element.53), channel_id=1, source_target_pairs={{0,5},{1,4},{2,7},{3,6},{4,1},{5,0},{6,3},{7,2},{8,13},{9,12},{10,... | collective-permute-start | bytes 49160 | tf_op jit(solution)/shard_map/ppermute | solution.py:51
  79.8 3.4 %collective-permute-start.8 = (f32[32,128]{1,0:T(8,128)S(1)}, f32[32,128]{1,0:T(8,128)S(1)}, u32[]{:S(2)}, u32[]{:S(2)}) collective-permute-start(f32[32,128]{1,0:T(8,128)S(1)} %get-tuple-element.54), channel_id=1, source_target_pairs={{0,6},{1,7},{2,4},{3,5},{4,2},{5,3},{6,0},{7,1},{8,14},{9,15},{10,... | collective-permute-start | bytes 49160 | tf_op jit(solution)/shard_map/ppermute | solution.py:51
  83.2 1.9 %collective-permute-start.9 = (f32[32,128]{1,0:T(8,128)S(1)}, f32[32,128]{1,0:T(8,128)S(1)}, u32[]{:S(2)}, u32[]{:S(2)}) collective-permute-start(f32[32,128]{1,0:T(8,128)S(1)} %get-tuple-element.55), channel_id=1, source_target_pairs={{0,7},{1,6},{2,5},{3,4},{4,3},{5,2},{6,1},{7,0},{8,15},{9,14},{10,... | collective-permute-start | bytes 49160 | tf_op jit(solution)/shard_map/ppermute | solution.py:51
  85.2 1.3 collective-permute-done.8.refs_6_
  86.5 4.0 %collective-permute-done.9.refs_7_ = f32[32,128]{1,0:T(8,128)S(1)} collective-permute-done((f32[32,128]{1,0:T(8,128)S(1)}, f32[32,128]{1,0:T(8,128)S(1)}, u32[]{:S(2)}, u32[]{:S(2)}) %collective-permute-start.9) | collective-permute-done | bytes 16416 | tf_op jit(solution)/shard_map/ppermute | solution.py:51
  90.5 1.9 %collective-permute-start.10 = (bf16[16,64,768]{2,1,0:T(8,128)(2,1)}, bf16[16,64,768]{2,1,0:T(8,128)(2,1)}, u32[]{:S(2)}, u32[]{:S(2)}) collective-permute-start(bf16[16,64,768]{2,1,0:T(8,128)(2,1)} %all-gather.3.cloned.1.call-done.x_ref), channel_id=1, source_target_pairs={{0,1},{1,0},{2,3},{3,2},{4,5},{5,4},{6,7},{7,6},{8,9},{9,8},{10,11... | collective-permute-start | bytes 4718600 | tf_op jit(solution)/shard_map/ppermute | solution.py:51
  93.0 4.4 %shard_map.146 = (bf16[8,128,192]{2,1,0:T(8,128)(2,1)}, f32[256,192]{1,0:T(8,128)}) custom-call(bf16[16,64,768]{2,1,0:T(8,128)(2,1)} %all-gather.3.cloned.1.call-done.x_ref, f32[768]{0:T(1024)} %gain_ref.6, bf16[16,48,384]{2,1,0:T(8,128)(2,1)} %copy-done.5), custom_call_target="tpu_custom_call" | custom-call | flops 452984832 | bytes 2162688 | tf_op jit(solution)/shard_map/pallas_call | solution.py:250
  97.6 6.7 %shard_map.147 = bf16[8,64,96]{2,1,0:T(8,128)(2,1)} custom-call(s32[1]{0:T(128)S(6)} %copy.21.length_ref, bf16[16,64,768]{2,1,0:T(8,128)(2,1)} %collective-permute-done.10.x_ref, f32[768]{0:T(1024)} %gain_ref.6, bf16[16,48,384]{2,1,0:T(8,128)(2,1)} %copy-done.5, bf16[8,128,192]{2,1,0:T(8,128)(2,1)} %get-tuple-element.58.near_kv_ref, ...), custom_call_target="tpu_custom_call" | custom-call | flops 452984832 | bytes 2162688 | tf_op jit(solution)/shard_map/pallas_call | solution.py:250
  104.3 1.1 slice.47.w_ref
  105.5 2.4 %collective-permute-start.11 = (bf16[16,48,384]{2,1,0:T(8,128)(2,1)S(1)}, bf16[16,48,384]{2,1,0:T(8,128)(2,1)S(1)}, u32[]{:S(2)}, u32[]{:S(2)}) collective-permute-start(bf16[16,48,384]{2,1,0:T(8,128)(2,1)S(1)} %slice.47.w_ref), channel_id=1, source_target_pairs={{0,1},{1,0},{2,3},{3,2},{4,5},{5,4},{6,7},{7,6},{8,9},{9,8},{10,11... | collective-permute-start | bytes 1769480 | tf_op jit(solution)/shard_map/ppermute | solution.py:51
  107.9 9.2 %all_to_all.25.gated_ref = bf16[8,64,96]{2,1,0:T(8,128)(2,1)S(1)} all-to-all(bf16[8,64,96]{2,1,0:T(8,128)(2,1)} %shard_map.147), channel_id=1, replica_groups=mesh['grp'=16,'pb'=4,'ka'=8] {'ka'}, dimensions={0} | all-to-all | bytes 196608 | tf_op jit(solution)/shard_map/all_to_all | solution.py:36
  117.9 7.0 %all-gather = bf16[256,768]{1,0:T(8,128)(2,1)S(1)} all-gather(bf16[64,768]{1,0:T(8,128)(2,1)S(1)} %get-tuple-element.72), channel_id=2, replica_groups={{0,1,2,3},{4,5,6,7},{8,9,10,11},{12,13,14,15},{16,17,18,19},{20,21,22,2..., dimensions={0}, use_global_device_ids=true | all-gather | bytes 491520 | tf_op jit(solution)/shard_map/all_gather | solution.py:396
  124.8 2.2 %shard_map.149 = bf16[4,64,768]{2,1,0:T(8,128)(2,1)S(1)} custom-call(bf16[4,64,768]{2,1,0:T(8,128)(2,1)S(1)} %bitcast.12, bf16[16,48,1536]{2,1,0:T(8,128)(2,1)} %all-to-all-done.2.w_ref), custom_call_target="tpu_custom_call" | custom-call | flops 452984832 | bytes 1769472 | tf_op jit(solution)/shard_map/pallas_call | solution.py:250
  127.1 9.0 %all_to_all.26.part_ref = bf16[4,64,768]{2,1,0:T(8,128)(2,1)S(1)} all-to-all(bf16[4,64,768]{2,1,0:T(8,128)(2,1)S(1)} %shard_map.149), channel_id=1, replica_groups={{0,1,2,3},{4,5,6,7},{8,9,10,11},{12,13,14,15},{16,17,18,19},{20,21,22,2..., dimensions={0} | all-to-all | bytes 786432 | tf_op jit(solution)/shard_map/all_to_all | solution.py:36
  (53 shorter events, 6.2 us)
Async XLA Ops:
  6.5 83.9 %all-gather.3.cloned.1.call-start = ((), (), s32[]{:S(2)}) async-start(), calls=%async_computation.5 | async-start | bytes 1671168 | tf_op jit(solution)/shard_map/all_gather | solution.py:298
  10.3 31.1 %all-to-all-start = ((bf16[4,12,1056]{2,1,0:T(8,128)(2,1)}), bf16[4,12,1056]{2,1,0:T(8,128)(2,1)S(1)}, u32[]{:S(2)}, u32[]{:S(2)}) async-start(bf16[4,12,1056]{2,1,0:T(8,128)(2,1)} %broadcast_in_dim.6), calls=%async_computation | async-start | bytes 294912 | tf_op jit(solution)/shard_map/all_to_all | solution.py:36
  26.7 1.0 copy-start
  27.7 0.7 copy-start.4
  30.1 0.6 copy-start.2
  30.7 8.3 %collective-permute-start = (f32[32,128]{1,0:T(8,128)S(1)}, f32[32,128]{1,0:T(8,128)S(1)}, u32[]{:S(2)}, u32[]{:S(2)}) collective-permute-start(f32[32,128]{1,0:T(8,128)S(1)} %get-tuple-element.41), channel_id=1, source_target_pairs={{0,1},{1,0},{2,3},{3,2},{4,5},{5,4},{6,7},{7,6},{8,9},{9,8},{10,11... | collective-permute-start | bytes 49160 | tf_op jit(solution)/shard_map/ppermute | solution.py:51
  33.6 5.5 %collective-permute-start.1 = (f32[32,128]{1,0:T(8,128)S(1)}, f32[32,128]{1,0:T(8,128)S(1)}, u32[]{:S(2)}, u32[]{:S(2)}) collective-permute-start(f32[32,128]{1,0:T(8,128)S(1)} %get-tuple-element.42), channel_id=1, source_target_pairs={{0,2},{1,3},{2,0},{3,1},{4,6},{5,7},{6,4},{7,5},{8,10},{9,11},{10,... | collective-permute-start | bytes 49160 | tf_op jit(solution)/shard_map/ppermute | solution.py:51
  36.3 5.2 %collective-permute-start.2 = (f32[32,128]{1,0:T(8,128)S(1)}, f32[32,128]{1,0:T(8,128)S(1)}, u32[]{:S(2)}, u32[]{:S(2)}) collective-permute-start(f32[32,128]{1,0:T(8,128)S(1)} %get-tuple-element.43), channel_id=1, source_target_pairs={{0,3},{1,2},{2,1},{3,0},{4,7},{5,6},{6,5},{7,4},{8,11},{9,10},{10,... | collective-permute-start | bytes 49160 | tf_op jit(solution)/shard_map/ppermute | solution.py:51
  39.1 24.4 %copy-start.6 = (f32[32,128]{1,0:T(8,128)}, f32[32,128]{1,0:T(8,128)S(1)}, u32[]{:S(2)}) copy-start(f32[32,128]{1,0:T(8,128)S(1)} %collective-permute-done.refs_1_) | copy-start | bytes 49156
  39.1 24.4 %copy-start.7 = (f32[32,128]{1,0:T(8,128)}, f32[32,128]{1,0:T(8,128)S(1)}, u32[]{:S(2)}) copy-start(f32[32,128]{1,0:T(8,128)S(1)} %collective-permute-done.1.refs_2_) | copy-start | bytes 49156
  41.4 22.1 %copy-start.8 = (f32[32,128]{1,0:T(8,128)}, f32[32,128]{1,0:T(8,128)S(1)}, u32[]{:S(2)}) copy-start(f32[32,128]{1,0:T(8,128)S(1)} %collective-permute-done.2.refs_3_) | copy-start | bytes 49156
  42.5 19.3 %all-to-all-start.1 = ((bf16[16,48,384]{2,1,0:T(8,128)(2,1)}), bf16[16,48,384]{2,1,0:T(8,128)(2,1)S(1)}, u32[]{:S(2)}, u32[]{:S(2)}) async-start(bf16[16,48,384]{2,1,0:T(8,128)(2,1)} %broadcast_in_dim.7), calls=%async_computation.1 | async-start | bytes 1179648 | tf_op jit(solution)/shard_map/all_to_all | solution.py:36
  49.2 9.4 %collective-permute-start.3 = (bf16[48,672]{1,0:T(8,128)(2,1)S(1)}, bf16[48,672]{1,0:T(8,128)(2,1)S(1)}, u32[]{:S(2)}, u32[]{:S(2)}) collective-permute-start(bf16[48,672]{1,0:T(8,128)(2,1)S(1)} %slice.49), channel_id=1, source_target_pairs={{0,4},{1,5},{2,6},{3,7},{4,0},{5,1},{6,2},{7,3},{8,12},{9,13},{10,... | collective-permute-start | bytes 193544 | tf_op jit(solution)/shard_map/ppermute | solution.py:51
  52.8 6.1 %collective-permute-start.4 = (bf16[48,96]{1,0:T(8,128)(2,1)S(1)}, bf16[48,96]{1,0:T(8,128)(2,1)S(1)}, u32[]{:S(2)}, u32[]{:S(2)}) collective-permute-start(bf16[48,96]{1,0:T(8,128)(2,1)S(1)} %slice.50), channel_id=1, source_target_pairs={{0,2},{1,3},{2,0},{3,1},{4,6},{5,7},{6,4},{7,5},{8,10},{9,11},{10,... | collective-permute-start | bytes 27656 | tf_op jit(solution)/shard_map/ppermute | solution.py:51
  55.1 6.5 %collective-permute-start.5 = (bf16[48,96]{1,0:T(8,128)(2,1)S(1)}, bf16[48,96]{1,0:T(8,128)(2,1)S(1)}, u32[]{:S(2)}, u32[]{:S(2)}) collective-permute-start(bf16[48,96]{1,0:T(8,128)(2,1)S(1)} %slice.50), channel_id=1, source_target_pairs={{0,6},{1,7},{2,4},{3,5},{4,2},{5,3},{6,0},{7,1},{8,14},{9,15},{10,... | collective-permute-start | bytes 27656 | tf_op jit(solution)/shard_map/ppermute | solution.py:51
  61.8 1.7 %copy-start.5 = (bf16[16,48,384]{2,1,0:T(8,128)(2,1)}, bf16[16,48,384]{2,1,0:T(8,128)(2,1)S(1)}, u32[]{:S(2)}) copy-start(bf16[16,48,384]{2,1,0:T(8,128)(2,1)S(1)} %all-to-all-done.1.w_ref) | copy-start | bytes 1769476
  63.5 40.8 %all-to-all-start.2 = ((bf16[16,48,1536]{2,1,0:T(8,128)(2,1)}), bf16[16,48,1536]{2,1,0:T(8,128)(2,1)}, u32[]{:S(2)}, u32[]{:S(2)}) async-start(bf16[16,48,1536]{2,1,0:T(8,128)(2,1)} %broadcast_in_dim.8), calls=%async_computation.2 | async-start | bytes 4718592 | tf_op jit(solution)/shard_map/all_to_all | solution.py:36
  70.0 15.2 %collective-permute-start.6 = (f32[32,128]{1,0:T(8,128)S(1)}, f32[32,128]{1,0:T(8,128)S(1)}, u32[]{:S(2)}, u32[]{:S(2)}) collective-permute-start(f32[32,128]{1,0:T(8,128)S(1)} %get-tuple-element.52), channel_id=1, source_target_pairs={{0,4},{1,5},{2,6},{3,7},{4,0},{5,1},{6,2},{7,3},{8,12},{9,13},{10,... | collective-permute-start | bytes 49160 | tf_op jit(solution)/shard_map/ppermute | solution.py:51
  71.9 13.3 %collective-permute-start.7 = (f32[32,128]{1,0:T(8,128)S(1)}, f32[32,128]{1,0:T(8,128)S(1)}, u32[]{:S(2)}, u32[]{:S(2)}) collective-permute-start(f32[32,128]{1,0:T(8,128)S(1)} %get-tuple-element.53), channel_id=1, source_target_pairs={{0,5},{1,4},{2,7},{3,6},{4,1},{5,0},{6,3},{7,2},{8,13},{9,12},{10,... | collective-permute-start | bytes 49160 | tf_op jit(solution)/shard_map/ppermute | solution.py:51
  79.8 6.7 %collective-permute-start.8 = (f32[32,128]{1,0:T(8,128)S(1)}, f32[32,128]{1,0:T(8,128)S(1)}, u32[]{:S(2)}, u32[]{:S(2)}) collective-permute-start(f32[32,128]{1,0:T(8,128)S(1)} %get-tuple-element.54), channel_id=1, source_target_pairs={{0,6},{1,7},{2,4},{3,5},{4,2},{5,3},{6,0},{7,1},{8,14},{9,15},{10,... | collective-permute-start | bytes 49160 | tf_op jit(solution)/shard_map/ppermute | solution.py:51
  83.2 7.3 %collective-permute-start.9 = (f32[32,128]{1,0:T(8,128)S(1)}, f32[32,128]{1,0:T(8,128)S(1)}, u32[]{:S(2)}, u32[]{:S(2)}) collective-permute-start(f32[32,128]{1,0:T(8,128)S(1)} %get-tuple-element.55), channel_id=1, source_target_pairs={{0,7},{1,6},{2,5},{3,4},{4,3},{5,2},{6,1},{7,0},{8,15},{9,14},{10,... | collective-permute-start | bytes 49160 | tf_op jit(solution)/shard_map/ppermute | solution.py:51
  85.2 12.4 %copy-start.9 = (f32[32,128]{1,0:T(8,128)}, f32[32,128]{1,0:T(8,128)S(1)}, u32[]{:S(2)}) copy-start(f32[32,128]{1,0:T(8,128)S(1)} %collective-permute-done.6.refs_4_) | copy-start | bytes 49156
  85.2 12.4 %copy-start.10 = (f32[32,128]{1,0:T(8,128)}, f32[32,128]{1,0:T(8,128)S(1)}, u32[]{:S(2)}) copy-start(f32[32,128]{1,0:T(8,128)S(1)} %collective-permute-done.7.refs_5_) | copy-start | bytes 49156
  86.4 11.1 %copy-start.11 = (f32[32,128]{1,0:T(8,128)}, f32[32,128]{1,0:T(8,128)S(1)}, u32[]{:S(2)}) copy-start(f32[32,128]{1,0:T(8,128)S(1)} %collective-permute-done.8.refs_6_) | copy-start | bytes 49156
  90.5 7.1 %copy-start.12 = (f32[32,128]{1,0:T(8,128)}, f32[32,128]{1,0:T(8,128)S(1)}, u32[]{:S(2)}) copy-start(f32[32,128]{1,0:T(8,128)S(1)} %collective-permute-done.9.refs_7_) | copy-start | bytes 49156
  90.5 7.0 %collective-permute-start.10 = (bf16[16,64,768]{2,1,0:T(8,128)(2,1)}, bf16[16,64,768]{2,1,0:T(8,128)(2,1)}, u32[]{:S(2)}, u32[]{:S(2)}) collective-permute-start(bf16[16,64,768]{2,1,0:T(8,128)(2,1)} %all-gather.3.cloned.1.call-done.x_ref), channel_id=1, source_target_pairs={{0,1},{1,0},{2,3},{3,2},{4,5},{5,4},{6,7},{7,6},{8,9},{9,8},{10,11... | collective-permute-start | bytes 4718600 | tf_op jit(solution)/shard_map/ppermute | solution.py:51
  97.5 19.6 %copy-start.1 = (bf16[1,8,8,768]{3,2,1,0:T(8,128)(2,1)S(1)}, bf16[1,8,8,768]{3,2,1,0:T(8,128)(2,1)}, u32[]{:S(2)}) copy-start(bf16[1,8,8,768]{3,2,1,0:T(8,128)(2,1)} %param.16) | copy-start | bytes 294916
  97.5 19.6 %copy-start.3 = (f32[768]{0:T(1024)S(1)}, f32[768]{0:T(1024)}, u32[]{:S(2)}) copy-start(f32[768]{0:T(1024)} %gain_ref.7) | copy-start | bytes 9220
  105.5 11.6 %collective-permute-start.11 = (bf16[16,48,384]{2,1,0:T(8,128)(2,1)S(1)}, bf16[16,48,384]{2,1,0:T(8,128)(2,1)S(1)}, u32[]{:S(2)}, u32[]{:S(2)}) collective-permute-start(bf16[16,48,384]{2,1,0:T(8,128)(2,1)S(1)} %slice.47.w_ref), channel_id=1, source_target_pairs={{0,1},{1,0},{2,3},{3,2},{4,5},{5,4},{6,7},{7,6},{8,9},{9,8},{10,11... | collective-permute-start | bytes 1769480 | tf_op jit(solution)/shard_map/ppermute | solution.py:51
Sparse Core Ops, SparseCore 0:
  9.4 71.2 all-gather.2

commit v6 on v3

--- a/solution.py
+++ b/solution.py
@@ -15,8 +15,8 @@
 very_negative = -1e30
 f32 = jnp.float32
 bf16 = jnp.bfloat16
-VMEM_LIMIT = 48 * 1024 * 1024
-MOST_VMEM = 63 * 1024 * 1024
+VMEM_LIMIT = 32 * 1024 * 1024
+MOST_VMEM = 32 * 1024 * 1024
 
 
 def layer_norm(inputs, scale_gain):
@@ -71,6 +71,11 @@
             held[:, start + j, :] = tile
     for flip, out_ref in enumerate(out_refs):
         out_ref[...] = held[lax.axis_index("ka") ^ flip]
+
+
+def place_kernel(*refs):
+    for flip, ref in enumerate(refs[:-1]):
+        refs[-1][lax.axis_index("ka") ^ flip] = ref[...]
 
 
 def project_side(samples, x_ref, gain_ref, w_ref, held_ref, kv_ref):
@@ -95,16 +100,14 @@
     query_ref[...] = project_side(samples, x_ref, gain_ref, w_ref, held_ref, kv_ref)
 
 
-def attention_kernel(length_ref, x_ref, gain_ref, w_ref, kv_ref, near_ref, *refs):
-    count = len(refs) - 6
-    bias_refs = refs[:count]
-    out_ref, held_normed, held_kv, held_bias, held_query, held_gate = refs[count:]
+def attention_kernel(length_ref, x_ref, gain_ref, w_ref, kv_ref, near_ref, bias_ref, *refs):
+    out_ref, held_normed, held_kv, held_query, held_gate = refs
+    count, keys_held, lanes = bias_ref.shape
     places, own_rows, width = x_ref.shape
     samples, span, feats = kv_ref.shape
     feats = feats // 2
     chips = count // 2
     blocks = places // chips
-    keys_held, lanes = bias_refs[0].shape
     q_rows = lanes // 2
     each = q_rows // count
     key_count = blocks * q_rows
@@ -118,11 +121,9 @@
             part = proj[z * own_rows : (z + 1) * own_rows]
             held_query[k] = part[:, :feats]
             held_gate[k] = part[:, feats:]
-    for flip in range(count):
-        held_bias[at ^ flip] = bias_refs[flip][...]
     bias = jnp.concatenate(
         [
-            held_bias[2 * z + (core ^ side), b * each : (b + 1) * each, :]
+            bias_ref[2 * z + (core ^ side), b * each : (b + 1) * each, :]
             for side in range(2)
             for b in range(blocks)
             for z in range(chips)
@@ -180,30 +181,20 @@
     mixed = (single_ref[...].astype(f32) + added).astype(bf16)
     mixed_ref[...] = mixed
     normed = layer_norm(mixed.astype(f32), gain_ref[...].reshape(1, -1)).astype(bf16)
-    for i in range(normed_ref.shape[0]):
-        normed_ref[i] = normed
-
-
-def transition_kernel(x_ref, w_ref, out_ref, swish, up, down, sems):
+    normed_ref[...] = normed
+
+
+def transition_kernel(x_ref, w_ref, out_ref):
     groups, rows, width = x_ref.shape
-    hidden_count = down.shape[2]
-    copies = [
-        pltpu.make_async_copy(
-            w_ref.at[:, :, pl.ds(i * hidden_count, hidden_count)], part, sems.at[i]
-        )
-        for i, part in ((1, swish), (2, up), (0, down))
-    ]
-    for copy in copies:
-        copy.start()
+    part = w_ref.shape[2] // 4
     x = x_ref[...].reshape(groups * rows, width)
-    copies[0].wait()
-    a = jnp.dot(x, swish[...].reshape(width, hidden_count), preferred_element_type=f32)
-    copies[1].wait()
-    b = jnp.dot(x, up[...].reshape(width, hidden_count), preferred_element_type=f32)
+    down, swish, up = (
+        w_ref[:, :, i * part : (i + 1) * part].reshape(width, part) for i in range(3)
+    )
+    a = jnp.dot(x, swish, preferred_element_type=f32)
+    b = jnp.dot(x, up, preferred_element_type=f32)
     hidden = ((a / (1.0 + jnp.exp(-a))) * b).astype(bf16)
-    copies[2].wait()
-    out = dot_last(hidden, down[...].reshape(width, hidden_count))
-    out_ref[...] = out.astype(bf16).reshape(groups, rows, width)
+    out_ref[...] = dot_last(hidden, down).astype(bf16).reshape(groups, rows, width)
 
 
 def finish_kernel(mixed_ref, part_ref, out_ref):
@@ -291,24 +282,26 @@
     early, near = lax.optimization_barrier((early, near))
     early = early.reshape(pb_count * w_rows, early.shape[2])
 
-    attn_w = spread(early[:, : 4 * feats], grp_count, "grp")
-
+    attn_w = jnp.broadcast_to(early[None, :, : 4 * feats], (grp_count, pb_count * w_rows, 4 * feats))
+    late = early[:, 4 * feats :]
     out_w = early[:, 4 * feats + 3 * hid :]
-    out_w = [out_w] + [swap(out_w, "ka", 2)]
-    late = jnp.concatenate([early[:, 4 * feats : 4 * feats + 3 * hid]] + out_w, axis=1)
+    attn_w, late, out_w = lax.optimization_barrier((attn_w, late, out_w))
+    attn_w = exchange(attn_w, "grp")
+
     late = [late] + [swap(late, "ka", TP)]
+    out_w = [late[0][:, 3 * hid :], swap(out_w, "ka", 2), late[1][:, 3 * hid :], swap(out_w, "ka", 6)]
     late = jnp.concatenate(
-        [w[:, i * hid : (i + 1) * hid] for i in range(3) for w in late]
-        + [w[:, 3 * hid :] for w in late],
-        axis=1,
-    )
-
+        [w[:, i * hid : (i + 1) * hid] for i in range(3) for w in late] + out_w, axis=1
+    )
+    late = jnp.broadcast_to(late[None], (grp_count,) + late.shape)
     late, attn_w, far = lax.optimization_barrier((late, attn_w, list(bias[4:])))
-    late = spread(late, grp_count, "grp")
+    late = exchange(late, "grp")
     far = [swap(block, "ka", i + 4) for i, block in enumerate(far)]
-    x, far = lax.optimization_barrier((x, far))
+    bias = call(
+        place_kernel, jax.ShapeDtypeStruct((ka_count, keys_held, lanes), f32)
+    )(bias[0], *near, *far)
+    x, bias = lax.optimization_barrier((x, bias))
     other = swap(x, "ka", 1)
-    bias = [bias[0]] + near + far
 
     line_rows = pb_count * chips * row_count
     kv_shape = (samples, line_rows, 2 * feats)
@@ -328,13 +321,12 @@
         scratch=[
             pltpu.VMEM(x.shape, bf16),
             pltpu.VMEM(kv_shape, bf16),
-            pltpu.VMEM((ka_count, keys_held, lanes), f32),
             pltpu.VMEM((ka_count, own_rows, feats), f32),
             pltpu.VMEM((ka_count, own_rows, feats), f32),
         ],
         scalars=1,
         **costs,
-    )(lengths, other, attn_gain, attn_w, near_kv, near_query, *bias)
+    )(lengths, other, attn_gain, attn_w, near_kv, near_query, bias)
     gated, late = lax.optimization_barrier((gated, late))
     gated = exchange(gated, "ka")
     out_w = late[:, :, held * 3 * hid :]
@@ -344,20 +336,18 @@
     shared = jax.ShapeDtypeStruct((TP, own_rows, width), bf16)
     mixed, normed_t = call(
         mix_kernel,
-        (rows, shared),
+        (rows, rows),
         scratch=[pltpu.VMEM((ka_count, own_rows, feats), f32)],
         flops=2 * own_rows * width * width,
         moved=width * width * 2,
     )(gated, out_w, other_w, own, trans_gain)
 
     groups = [list(range(i, i + TP)) for i in range(0, ka_count, TP)]
-    normed_t = exchange(normed_t, "ka", groups)
+    normed_t = lax.all_gather(normed_t, "ka", axis=0, tiled=False, axis_index_groups=groups)
     part = call(
         transition_kernel,
         shared,
-        scratch=[pltpu.VMEM((grp_count, pb_count * w_rows, held * hid), bf16)] * 3
-        + [pltpu.SemaphoreType.DMA((3,))],
-        left=(1,),
+
         flops=2 * own_rows * width * hid * ka_count * 3,
         moved=3 * width * hid * ka_count // TP * 2,
     )(normed_t, late)

time: 147 us -> 141 us (0.959)
  starting transfers between devices: 61.4 us -> 70.1 us
  Pallas kernels: 15.4 us -> 9.06 us
  blocking collectives: 29.1 us -> 24.6 us
  waiting for transfers between devices: 14.7 us -> 11.5 us
    all_to_all x3 -> x2, blocking collectives: 29.1 us -> 17.7 us  [exchange(): lax.all_to_all(blocks, axes, split_axis=0, concat_axis=0, tiled=True, axi...]
    ppermute x11 -> x12, starting transfers between devices: 33.5 us -> 41 us  [swap(): return lax.ppermute(block, axis, [(i, i ^ flip) for i in range(count)])]
    all_gather x0 -> x1, blocking collectives: none -> 6.96 us  [on_device(): lax.all_gather(normed_t, 'ka', axis=0, tiled=False, axis_index_groups=gro...]
    pallas_call x6 -> x7, Pallas kernels: 15.4 us -> 9.06 us  [run(): pl.pallas_call(kernel, out_shape=out_shape, in_specs=[pl.BlockSpec(memory...]
    ppermute x11 -> x12, waiting for transfers between devices: 13.9 us -> 10.8 us  [swap(): return lax.ppermute(block, axis, [(i, i ^ flip) for i in range(count)])]
    broadcast_in_dim x3 -> x1, local copies, waits for them, and re-layouts: 3.2 us -> 0.66 us  [spread(): return exchange(jnp.broadcast_to(block[None], (count,) + block.shape), axes)]
    broadcast_in_dim x0 -> x2, local copies, waits for them, and re-layouts: none -> 2.51 us  [the longest x1 1.64 us: on_device(): late = jnp.broadcast_to(late[None], (grp_count,) + late.shape)]
    unnamed x26 -> x12, local copies, waits for them, and re-layouts: 2.33 us -> 3.11 us
  transfers between devices with their start and end apart: 15 -> 16, of which waited for: 5 -> 6; matrix products, arithmetic and copies ran while one was open for 5% -> 5% of each run, Pallas kernels for 8% -> 5%
where the time goes in v6:
time: 141 us; the launch traced here: 140 us
  starting transfers between devices  70.1 us (50%)
  blocking collectives  24.6 us (17%)
  between operations  14.3 us (10%)
  waiting for transfers between devices  11.5 us (8%)
  local copies, waits for them, and re-layouts  10 us (7%)
  Pallas kernels  9.06 us (6%)
    ppermute x12, starting transfers between devices, swap(): return lax.ppermute(block, axis, [(i, i ^ flip) for i in range(count)])  41 us
    all_to_all x3, starting transfers between devices, exchange(): lax.all_to_all(blocks, axes, split_axis=0, concat_axis=0, tiled=True, axi...  29.1 us
    all_to_all x2, blocking collectives, exchange(): lax.all_to_all(blocks, axes, split_axis=0, concat_axis=0, tiled=True, axi...  17.7 us
    ppermute x12, waiting for transfers between devices, swap(): return lax.ppermute(block, axis, [(i, i ^ flip) for i in range(count)])  10.8 us
    pallas_call x7, Pallas kernels, run(): pl.pallas_call(kernel, out_shape=out_shape, in_specs=[pl.BlockSpec(memory...  9.06 us
    all_gather x1, blocking collectives, on_device(): lax.all_gather(normed_t, 'ka', axis=0, tiled=False, axis_index_groups=gro...  6.96 us
    unnamed x12, local copies, waits for them, and re-layouts  3.11 us
  transfers between devices with their start and end apart: 16, of which 6 were waited for; matrix products, arithmetic and copies ran while one was open for 5% of the time, Pallas kernels for 5%

profile of v6, /device:TPU:1, one launch (start us, length us, event | category | flops | bytes accessed | tf_op | source)
XLA Modules:
  0.0 139.6 jit_solution(14653269237850466999)
XLA Ops:
  7.3 0.8 constant_dynamic-slice_fusion.2
  8.8 0.8 concatenate.6
  10.3 15.6 %all-to-all-start = ((bf16[4,12,1056]{2,1,0:T(8,128)(2,1)}), bf16[4,12,1056]{2,1,0:T(8,128)(2,1)S(1)}, u32[]{:S(2)}, u32[]{:S(2)}) async-start(bf16[4,12,1056]{2,1,0:T(8,128)(2,1)} %broadcast_in_dim.6), calls=%async_computation | async-start | bytes 294912 | tf_op jit(solution)/shard_map/all_to_all | solution.py:36
  26.7 1.0 copy-done.1
  28.4 1.7 %shard_map.145 = (f32[32,128]{1,0:T(8,128)S(1)}, f32[32,128]{1,0:T(8,128)S(1)}, f32[32,128]{1,0:T(8,128)S(1)}, f32[32,128]{1,0:T(8,128)S(1)}, f32[32,128]{1,0:T(...) custom-call(bf16[64,32,128]{2,1,0:T(8,128)(2,1)S(1)} %bitcast.13, ...), custom_call_target="tpu_custom_call" | custom-call | flops 50331648 | bytes 655360 | tf_op jit(solution)/shard_map/pallas_call | solution.py:209
  30.1 2.9 %collective-permute-start = (f32[32,128]{1,0:T(8,128)S(1)}, f32[32,128]{1,0:T(8,128)S(1)}, u32[]{:S(2)}, u32[]{:S(2)}) collective-permute-start(f32[32,128]{1,0:T(8,128)S(1)} %get-tuple-element.39), channel_id=1, source_target_pairs={{0,1},{1,0},{2,3},{3,2},{4,5},{5,4},{6,7},{7,6},{8,9},{9,8},{10,11... | collective-permute-start | bytes 49160 | tf_op jit(solution)/shard_map/ppermute | solution.py:51
  33.0 2.6 %collective-permute-start.1 = (f32[32,128]{1,0:T(8,128)S(1)}, f32[32,128]{1,0:T(8,128)S(1)}, u32[]{:S(2)}, u32[]{:S(2)}) collective-permute-start(f32[32,128]{1,0:T(8,128)S(1)} %get-tuple-element.40), channel_id=1, source_target_pairs={{0,2},{1,3},{2,0},{3,1},{4,6},{5,7},{6,4},{7,5},{8,10},{9,11},{10,... | collective-permute-start | bytes 49160 | tf_op jit(solution)/shard_map/ppermute | solution.py:51
  35.6 2.8 %collective-permute-start.2 = (f32[32,128]{1,0:T(8,128)S(1)}, f32[32,128]{1,0:T(8,128)S(1)}, u32[]{:S(2)}, u32[]{:S(2)}) collective-permute-start(f32[32,128]{1,0:T(8,128)S(1)} %get-tuple-element.41), channel_id=1, source_target_pairs={{0,3},{1,2},{2,1},{3,0},{4,7},{5,6},{6,5},{7,4},{8,11},{9,10},{10,... | collective-permute-start | bytes 49160 | tf_op jit(solution)/shard_map/ppermute | solution.py:51
  38.5 2.5 %collective-permute-done.2.refs_3_ = f32[32,128]{1,0:T(8,128)S(1)} collective-permute-done((f32[32,128]{1,0:T(8,128)S(1)}, f32[32,128]{1,0:T(8,128)S(1)}, u32[]{:S(2)}, u32[]{:S(2)}) %collective-permute-start.2) | collective-permute-done | bytes 16416 | tf_op jit(solution)/shard_map/ppermute | solution.py:51
  41.1 0.9 broadcast_in_dim.7
  42.0 6.8 %all-to-all-start.1 = ((bf16[16,48,384]{2,1,0:T(8,128)(2,1)}), bf16[16,48,384]{2,1,0:T(8,128)(2,1)S(1)}, u32[]{:S(2)}, u32[]{:S(2)}) async-start(bf16[16,48,384]{2,1,0:T(8,128)(2,1)} %broadcast_in_dim.7), calls=%async_computation.1 | async-start | bytes 1179648 | tf_op jit(solution)/shard_map/all_to_all | solution.py:36
  48.8 3.5 %collective-permute-start.3 = (bf16[48,672]{1,0:T(8,128)(2,1)S(1)}, bf16[48,672]{1,0:T(8,128)(2,1)S(1)}, u32[]{:S(2)}, u32[]{:S(2)}) collective-permute-start(bf16[48,672]{1,0:T(8,128)(2,1)S(1)} %slice.49), channel_id=1, source_target_pairs={{0,4},{1,5},{2,6},{3,7},{4,0},{5,1},{6,2},{7,3},{8,12},{9,13},{10,... | collective-permute-start | bytes 193544 | tf_op jit(solution)/shard_map/ppermute | solution.py:51
  52.4 2.5 %collective-permute-start.4 = (bf16[48,96]{1,0:T(8,128)(2,1)S(1)}, bf16[48,96]{1,0:T(8,128)(2,1)S(1)}, u32[]{:S(2)}, u32[]{:S(2)}) collective-permute-start(bf16[48,96]{1,0:T(8,128)(2,1)S(1)} %slice.50), channel_id=1, source_target_pairs={{0,2},{1,3},{2,0},{3,1},{4,6},{5,7},{6,4},{7,5},{8,10},{9,11},{10,... | collective-permute-start | bytes 27656 | tf_op jit(solution)/shard_map/ppermute | solution.py:51
  54.9 3.3 %collective-permute-start.5 = (bf16[48,96]{1,0:T(8,128)(2,1)S(1)}, bf16[48,96]{1,0:T(8,128)(2,1)S(1)}, u32[]{:S(2)}, u32[]{:S(2)}) collective-permute-start(bf16[48,96]{1,0:T(8,128)(2,1)S(1)} %slice.50), channel_id=1, source_target_pairs={{0,6},{1,7},{2,4},{3,5},{4,2},{5,3},{6,0},{7,1},{8,14},{9,15},{10,... | collective-permute-start | bytes 27656 | tf_op jit(solution)/shard_map/ppermute | solution.py:51
  58.4 3.0 %collective-permute-done.5 = bf16[48,96]{1,0:T(8,128)(2,1)S(1)} collective-permute-done((bf16[48,96]{1,0:T(8,128)(2,1)S(1)}, bf16[48,96]{1,0:T(8,128)(2,1)S(1)}, u32[]{:S(2)}, u32[]{:S(2)}) %collective-permute-start.5) | collective-permute-done | bytes 9248 | tf_op jit(solution)/shard_map/ppermute | solution.py:51
  61.5 1.6 %broadcast_in_dim.8 = bf16[16,48,1536]{2,1,0:T(8,128)(2,1)} broadcast(bf16[48,1536]{1,0:T(8,128)(2,1)S(1)} %concatenate.7), dimensions={1,2} | broadcast | bytes 2506752 | tf_op jit(solution)/shard_map/broadcast_in_dim | solution.py:296
  63.1 6.7 %all-to-all-start.2 = ((bf16[16,48,1536]{2,1,0:T(8,128)(2,1)}), bf16[16,48,1536]{2,1,0:T(8,128)(2,1)S(1)}, u32[]{:S(2)}, u32[]{:S(2)}) async-start(bf16[16,48,1536]{2,1,0:T(8,128)(2,1)} %broadcast_in_dim.8), calls=%async_computation.2 | async-start | bytes 4718592 | tf_op jit(solution)/shard_map/all_to_all | solution.py:36
  69.8 2.0 %collective-permute-start.6 = (f32[32,128]{1,0:T(8,128)S(1)}, f32[32,128]{1,0:T(8,128)S(1)}, u32[]{:S(2)}, u32[]{:S(2)}) collective-permute-start(f32[32,128]{1,0:T(8,128)S(1)} %get-tuple-element.53), channel_id=1, source_target_pairs={{0,4},{1,5},{2,6},{3,7},{4,0},{5,1},{6,2},{7,3},{8,12},{9,13},{10,... | collective-permute-start | bytes 49160 | tf_op jit(solution)/shard_map/ppermute | solution.py:51
  71.8 7.9 %collective-permute-start.7 = (f32[32,128]{1,0:T(8,128)S(1)}, f32[32,128]{1,0:T(8,128)S(1)}, u32[]{:S(2)}, u32[]{:S(2)}) collective-permute-start(f32[32,128]{1,0:T(8,128)S(1)} %get-tuple-element.54), channel_id=1, source_target_pairs={{0,5},{1,4},{2,7},{3,6},{4,1},{5,0},{6,3},{7,2},{8,13},{9,12},{10,... | collective-permute-start | bytes 49160 | tf_op jit(solution)/shard_map/ppermute | solution.py:51
  79.8 3.5 %collective-permute-start.8 = (f32[32,128]{1,0:T(8,128)S(1)}, f32[32,128]{1,0:T(8,128)S(1)}, u32[]{:S(2)}, u32[]{:S(2)}) collective-permute-start(f32[32,128]{1,0:T(8,128)S(1)} %get-tuple-element.55), channel_id=1, source_target_pairs={{0,6},{1,7},{2,4},{3,5},{4,2},{5,3},{6,0},{7,1},{8,14},{9,15},{10,... | collective-permute-start | bytes 49160 | tf_op jit(solution)/shard_map/ppermute | solution.py:51
  83.2 1.9 %collective-permute-start.9 = (f32[32,128]{1,0:T(8,128)S(1)}, f32[32,128]{1,0:T(8,128)S(1)}, u32[]{:S(2)}, u32[]{:S(2)}) collective-permute-start(f32[32,128]{1,0:T(8,128)S(1)} %get-tuple-element.56), channel_id=1, source_target_pairs={{0,7},{1,6},{2,5},{3,4},{4,3},{5,2},{6,1},{7,0},{8,15},{9,14},{10,... | collective-permute-start | bytes 49160 | tf_op jit(solution)/shard_map/ppermute | solution.py:51
  85.2 1.2 collective-permute-done.8.refs_6_
  86.4 4.0 %collective-permute-done.9.refs_7_ = f32[32,128]{1,0:T(8,128)S(1)} collective-permute-done((f32[32,128]{1,0:T(8,128)S(1)}, f32[32,128]{1,0:T(8,128)S(1)}, u32[]{:S(2)}, u32[]{:S(2)}) %collective-permute-start.9) | collective-permute-done | bytes 16416 | tf_op jit(solution)/shard_map/ppermute | solution.py:51
  90.4 1.9 %collective-permute-start.10 = (bf16[16,64,768]{2,1,0:T(8,128)(2,1)}, bf16[16,64,768]{2,1,0:T(8,128)(2,1)S(1)}, u32[]{:S(2)}, u32[]{:S(2)}) collective-permute-start(bf16[16,64,768]{2,1,0:T(8,128)(2,1)} %all-gather.3.cloned.1.call-done.x_ref), channel_id=1, source_target_pairs={{0,1},{1,0},{2,3},{3,2},{4,5},{5,4},{6,7},{7,6},{8,9},{9,8},{10,11... | collective-permute-start | bytes 4718600 | tf_op jit(solution)/shard_map/ppermute | solution.py:51
  93.0 1.4 %copy-done = bf16[16,64,768]{2,1,0:T(8,128)(2,1)S(1)} copy-done((bf16[16,64,768]{2,1,0:T(8,128)(2,1)S(1)}, bf16[16,64,768]{2,1,0:T(8,128)(2,1)}, u32[]{:S(2)}) %copy-start) | copy-done | bytes 1572888
  94.4 1.4 %shard_map.147 = (bf16[8,128,192]{2,1,0:T(8,128)(2,1)S(1)}, f32[256,192]{1,0:T(8,128)S(1)}) custom-call(bf16[16,64,768]{2,1,0:T(8,128)(2,1)S(1)} %copy-done, f32[768]{0:T(1024)S(1)} %copy-done.3, bf16[16,48,384]{2,1,0:T(8,128)(2,1)S(1)} %all-to-all-done.1.w_ref), custom_call_target="tpu_custom_call" | custom-call | flops 452984832 | bytes 2162688 | tf_op jit(solution)/shard_map/pallas_call | solution.py:209
  96.0 3.6 %shard_map.148 = bf16[8,64,96]{2,1,0:T(8,128)(2,1)S(1)} custom-call(s32[1]{0:T(128)S(6)} %copy.21.length_ref, bf16[16,64,768]{2,1,0:T(8,128)(2,1)S(1)} %collective-permute-done.10.x_ref, f32[768]{0:T(1024)S(1)} %copy-done.3, bf16[16,48,384]{2,1,0:T(8,128)(2,1)S(1)} %all-to-all-done.1.w_ref, bf16[8,128,192]{2,1,0:T(8,128)(2,1)S(1)} %get-tuple-element.59.kv_ref, ...), custom_call_target="tpu_custom_call" | custom-call | flops 452984832 | bytes 2162688 | tf_op jit(solution)/shard_map/pallas_call | solution.py:209
  99.6 6.2 %collective-permute-start.11 = (bf16[16,48,384]{2,1,0:T(8,128)(2,1)S(1)}, bf16[16,48,384]{2,1,0:T(8,128)(2,1)S(1)}, u32[]{:S(2)}, u32[]{:S(2)}) collective-permute-start(bf16[16,48,384]{2,1,0:T(8,128)(2,1)S(1)} %slice.47.w_ref), channel_id=1, source_target_pairs={{0,1},{1,0},{2,3},{3,2},{4,5},{5,4},{6,7},{7,6},{8,9},{9,8},{10,11... | collective-permute-start | bytes 1769480 | tf_op jit(solution)/shard_map/ppermute | solution.py:51
  105.8 8.7 %all_to_all.25.gated_ref = bf16[8,64,96]{2,1,0:T(8,128)(2,1)S(1)} all-to-all(bf16[8,64,96]{2,1,0:T(8,128)(2,1)S(1)} %shard_map.148), channel_id=1, replica_groups=mesh['grp'=16,'pb'=4,'ka'=8] {'ka'}, dimensions={0} | all-to-all | bytes 196608 | tf_op jit(solution)/shard_map/all_to_all | solution.py:36
  115.3 7.0 %all-gather = bf16[256,768]{1,0:T(8,128)(2,1)S(1)} all-gather(bf16[64,768]{1,0:T(8,128)(2,1)S(1)} %get-tuple-element.66), channel_id=2, replica_groups={{0,1,2,3},{4,5,6,7},{8,9,10,11},{12,13,14,15},{16,17,18,19},{20,21,22,2..., dimensions={0}, use_global_device_ids=true | all-gather | bytes 491520 | tf_op jit(solution)/shard_map/all_gather | solution.py:346
  122.3 0.8 shard_map.150
  123.1 9.0 %all_to_all.26.part_ref = bf16[4,64,768]{2,1,0:T(8,128)(2,1)S(1)} all-to-all(bf16[4,64,768]{2,1,0:T(8,128)(2,1)S(1)} %shard_map.150), channel_id=1, replica_groups={{0,1,2,3},{4,5,6,7},{8,9,10,11},{12,13,14,15},{16,17,18,19},{20,21,22,2..., dimensions={0} | all-to-all | bytes 786432 | tf_op jit(solution)/shard_map/all_to_all | solution.py:36
  (40 shorter events, 5.8 us)
Async XLA Ops:
  6.5 83.9 %all-gather.3.cloned.1.call-start = ((), (), s32[]{:S(2)}) async-start(), calls=%async_computation.5 | async-start | bytes 1671168 | tf_op jit(solution)/shard_map/all_gather | solution.py:257
  10.3 30.6 %all-to-all-start = ((bf16[4,12,1056]{2,1,0:T(8,128)(2,1)}), bf16[4,12,1056]{2,1,0:T(8,128)(2,1)S(1)}, u32[]{:S(2)}, u32[]{:S(2)}) async-start(bf16[4,12,1056]{2,1,0:T(8,128)(2,1)} %broadcast_in_dim.6), calls=%async_computation | async-start | bytes 294912 | tf_op jit(solution)/shard_map/all_to_all | solution.py:36
  26.7 1.0 copy-start.1
  27.7 0.7 copy-start.5
  30.1 8.3 %collective-permute-start = (f32[32,128]{1,0:T(8,128)S(1)}, f32[32,128]{1,0:T(8,128)S(1)}, u32[]{:S(2)}, u32[]{:S(2)}) collective-permute-start(f32[32,128]{1,0:T(8,128)S(1)} %get-tuple-element.39), channel_id=1, source_target_pairs={{0,1},{1,0},{2,3},{3,2},{4,5},{5,4},{6,7},{7,6},{8,9},{9,8},{10,11... | collective-permute-start | bytes 49160 | tf_op jit(solution)/shard_map/ppermute | solution.py:51
  33.0 5.5 %collective-permute-start.1 = (f32[32,128]{1,0:T(8,128)S(1)}, f32[32,128]{1,0:T(8,128)S(1)}, u32[]{:S(2)}, u32[]{:S(2)}) collective-permute-start(f32[32,128]{1,0:T(8,128)S(1)} %get-tuple-element.40), channel_id=1, source_target_pairs={{0,2},{1,3},{2,0},{3,1},{4,6},{5,7},{6,4},{7,5},{8,10},{9,11},{10,... | collective-permute-start | bytes 49160 | tf_op jit(solution)/shard_map/ppermute | solution.py:51
  35.6 5.4 %collective-permute-start.2 = (f32[32,128]{1,0:T(8,128)S(1)}, f32[32,128]{1,0:T(8,128)S(1)}, u32[]{:S(2)}, u32[]{:S(2)}) collective-permute-start(f32[32,128]{1,0:T(8,128)S(1)} %get-tuple-element.41), channel_id=1, source_target_pairs={{0,3},{1,2},{2,1},{3,0},{4,7},{5,6},{6,5},{7,4},{8,11},{9,10},{10,... | collective-permute-start | bytes 49160 | tf_op jit(solution)/shard_map/ppermute | solution.py:51
  42.0 19.5 %all-to-all-start.1 = ((bf16[16,48,384]{2,1,0:T(8,128)(2,1)}), bf16[16,48,384]{2,1,0:T(8,128)(2,1)S(1)}, u32[]{:S(2)}, u32[]{:S(2)}) async-start(bf16[16,48,384]{2,1,0:T(8,128)(2,1)} %broadcast_in_dim.7), calls=%async_computation.1 | async-start | bytes 1179648 | tf_op jit(solution)/shard_map/all_to_all | solution.py:36
  48.8 9.4 %collective-permute-start.3 = (bf16[48,672]{1,0:T(8,128)(2,1)S(1)}, bf16[48,672]{1,0:T(8,128)(2,1)S(1)}, u32[]{:S(2)}, u32[]{:S(2)}) collective-permute-start(bf16[48,672]{1,0:T(8,128)(2,1)S(1)} %slice.49), channel_id=1, source_target_pairs={{0,4},{1,5},{2,6},{3,7},{4,0},{5,1},{6,2},{7,3},{8,12},{9,13},{10,... | collective-permute-start | bytes 193544 | tf_op jit(solution)/shard_map/ppermute | solution.py:51
  52.4 6.0 %collective-permute-start.4 = (bf16[48,96]{1,0:T(8,128)(2,1)S(1)}, bf16[48,96]{1,0:T(8,128)(2,1)S(1)}, u32[]{:S(2)}, u32[]{:S(2)}) collective-permute-start(bf16[48,96]{1,0:T(8,128)(2,1)S(1)} %slice.50), channel_id=1, source_target_pairs={{0,2},{1,3},{2,0},{3,1},{4,6},{5,7},{6,4},{7,5},{8,10},{9,11},{10,... | collective-permute-start | bytes 27656 | tf_op jit(solution)/shard_map/ppermute | solution.py:51
  54.9 6.4 %collective-permute-start.5 = (bf16[48,96]{1,0:T(8,128)(2,1)S(1)}, bf16[48,96]{1,0:T(8,128)(2,1)S(1)}, u32[]{:S(2)}, u32[]{:S(2)}) collective-permute-start(bf16[48,96]{1,0:T(8,128)(2,1)S(1)} %slice.50), channel_id=1, source_target_pairs={{0,6},{1,7},{2,4},{3,5},{4,2},{5,3},{6,0},{7,1},{8,14},{9,15},{10,... | collective-permute-start | bytes 27656 | tf_op jit(solution)/shard_map/ppermute | solution.py:51
  63.1 29.9 %copy-start.3 = (f32[768]{0:T(1024)S(1)}, f32[768]{0:T(1024)}, u32[]{:S(2)}) copy-start(f32[768]{0:T(1024)} %gain_ref.6) | copy-start | bytes 9220
  63.1 36.4 %all-to-all-start.2 = ((bf16[16,48,1536]{2,1,0:T(8,128)(2,1)}), bf16[16,48,1536]{2,1,0:T(8,128)(2,1)S(1)}, u32[]{:S(2)}, u32[]{:S(2)}) async-start(bf16[16,48,1536]{2,1,0:T(8,128)(2,1)} %broadcast_in_dim.8), calls=%async_computation.2 | async-start | bytes 4718592 | tf_op jit(solution)/shard_map/all_to_all | solution.py:36
  69.8 15.4 %collective-permute-start.6 = (f32[32,128]{1,0:T(8,128)S(1)}, f32[32,128]{1,0:T(8,128)S(1)}, u32[]{:S(2)}, u32[]{:S(2)}) collective-permute-start(f32[32,128]{1,0:T(8,128)S(1)} %get-tuple-element.53), channel_id=1, source_target_pairs={{0,4},{1,5},{2,6},{3,7},{4,0},{5,1},{6,2},{7,3},{8,12},{9,13},{10,... | collective-permute-start | bytes 49160 | tf_op jit(solution)/shard_map/ppermute | solution.py:51
  71.8 13.4 %collective-permute-start.7 = (f32[32,128]{1,0:T(8,128)S(1)}, f32[32,128]{1,0:T(8,128)S(1)}, u32[]{:S(2)}, u32[]{:S(2)}) collective-permute-start(f32[32,128]{1,0:T(8,128)S(1)} %get-tuple-element.54), channel_id=1, source_target_pairs={{0,5},{1,4},{2,7},{3,6},{4,1},{5,0},{6,3},{7,2},{8,13},{9,12},{10,... | collective-permute-start | bytes 49160 | tf_op jit(solution)/shard_map/ppermute | solution.py:51
  79.8 6.6 %collective-permute-start.8 = (f32[32,128]{1,0:T(8,128)S(1)}, f32[32,128]{1,0:T(8,128)S(1)}, u32[]{:S(2)}, u32[]{:S(2)}) collective-permute-start(f32[32,128]{1,0:T(8,128)S(1)} %get-tuple-element.55), channel_id=1, source_target_pairs={{0,6},{1,7},{2,4},{3,5},{4,2},{5,3},{6,0},{7,1},{8,14},{9,15},{10,... | collective-permute-start | bytes 49160 | tf_op jit(solution)/shard_map/ppermute | solution.py:51
  83.2 7.2 %collective-permute-start.9 = (f32[32,128]{1,0:T(8,128)S(1)}, f32[32,128]{1,0:T(8,128)S(1)}, u32[]{:S(2)}, u32[]{:S(2)}) collective-permute-start(f32[32,128]{1,0:T(8,128)S(1)} %get-tuple-element.56), channel_id=1, source_target_pairs={{0,7},{1,6},{2,5},{3,4},{4,3},{5,2},{6,1},{7,0},{8,15},{9,14},{10,... | collective-permute-start | bytes 49160 | tf_op jit(solution)/shard_map/ppermute | solution.py:51
  90.4 5.5 %collective-permute-start.10 = (bf16[16,64,768]{2,1,0:T(8,128)(2,1)}, bf16[16,64,768]{2,1,0:T(8,128)(2,1)S(1)}, u32[]{:S(2)}, u32[]{:S(2)}) collective-permute-start(bf16[16,64,768]{2,1,0:T(8,128)(2,1)} %all-gather.3.cloned.1.call-done.x_ref), channel_id=1, source_target_pairs={{0,1},{1,0},{2,3},{3,2},{4,5},{5,4},{6,7},{7,6},{8,9},{9,8},{10,11... | collective-permute-start | bytes 4718600 | tf_op jit(solution)/shard_map/ppermute | solution.py:51
  93.0 1.4 %copy-start = (bf16[16,64,768]{2,1,0:T(8,128)(2,1)S(1)}, bf16[16,64,768]{2,1,0:T(8,128)(2,1)}, u32[]{:S(2)}) copy-start(bf16[16,64,768]{2,1,0:T(8,128)(2,1)} %all-gather.3.cloned.1.call-done.x_ref) | copy-start | bytes 4718596
  95.9 18.7 %copy-start.2 = (bf16[1,8,8,768]{3,2,1,0:T(8,128)(2,1)S(1)}, bf16[1,8,8,768]{3,2,1,0:T(8,128)(2,1)}, u32[]{:S(2)}) copy-start(bf16[1,8,8,768]{3,2,1,0:T(8,128)(2,1)} %param.16) | copy-start | bytes 294916
  95.9 18.7 %copy-start.4 = (f32[768]{0:T(1024)S(1)}, f32[768]{0:T(1024)}, u32[]{:S(2)}) copy-start(f32[768]{0:T(1024)} %gain_ref.7) | copy-start | bytes 9220
  99.6 14.9 %collective-permute-start.11 = (bf16[16,48,384]{2,1,0:T(8,128)(2,1)S(1)}, bf16[16,48,384]{2,1,0:T(8,128)(2,1)S(1)}, u32[]{:S(2)}, u32[]{:S(2)}) collective-permute-start(bf16[16,48,384]{2,1,0:T(8,128)(2,1)S(1)} %slice.47.w_ref), channel_id=1, source_target_pairs={{0,1},{1,0},{2,3},{3,2},{4,5},{5,4},{6,7},{7,6},{8,9},{9,8},{10,11... | collective-permute-start | bytes 1769480 | tf_op jit(solution)/shard_map/ppermute | solution.py:51
Sparse Core Ops, SparseCore 0:
  9.4 70.7 all-gather.2

commit v7 on v6

--- a/solution.py
+++ b/solution.py
@@ -51,10 +51,9 @@
     return lax.ppermute(block, axis, [(i, i ^ flip) for i in range(count)])
 
 
-def bias_kernel(x_ref, gain_ref, proj_ref, *refs):
-    out_refs, rows, held = refs[:-2], refs[-2], refs[-1]
+def bias_kernel(x_ref, gain_ref, proj_ref, keep_ref, send_ref, rows, held):
     queries, keys, channels = x_ref.shape
-    pairs = len(out_refs)
+    pairs = held.shape[0]
     normed = layer_norm(
         x_ref[...].reshape(queries * keys, channels).astype(f32), gain_ref[...].reshape(1, -1)
     )
@@ -69,13 +68,32 @@
             cols = slice(j * queries, (j + 1) * queries)
             tile = jnp.concatenate([bias[:pairs, cols], bias[pairs:, cols]], axis=1)
             held[:, start + j, :] = tile
-    for flip, out_ref in enumerate(out_refs):
-        out_ref[...] = held[lax.axis_index("ka") ^ flip]
-
-
-def place_kernel(*refs):
-    for flip, ref in enumerate(refs[:-1]):
-        refs[-1][lax.axis_index("ka") ^ flip] = ref[...]
+    for i in range(pairs // 2):
+        keep_ref[i] = held[lax.axis_index("ka") ^ (2 * i)]
+        send_ref[i] = held[lax.axis_index("ka") ^ (2 * i + 1)]
+
+
+def second_kernel(keep_ref, one_ref, out_ref):
+    for i in range(2):
+        out_ref[2 * i] = keep_ref[2 * i + 1]
+        out_ref[2 * i + 1] = one_ref[2 * i + 1]
+
+
+def third_kernel(keep_ref, one_ref, two_ref, out_ref):
+    out_ref[0] = keep_ref[2]
+    out_ref[1] = one_ref[2]
+    out_ref[2] = two_ref[2]
+    out_ref[3] = two_ref[3]
+
+
+def place_kernel(keep_ref, one_ref, two_ref, four_ref, out_ref):
+    at = lax.axis_index("ka")
+    out_ref[at] = keep_ref[0]
+    out_ref[at ^ 1] = one_ref[0]
+    out_ref[at ^ 2] = two_ref[0]
+    out_ref[at ^ 3] = two_ref[1]
+    for i in range(four_ref.shape[0]):
+        out_ref[at ^ (4 + i)] = four_ref[i]
 
 
 def project_side(samples, x_ref, gain_ref, w_ref, held_ref, kv_ref):
@@ -83,7 +101,7 @@
     feats = kv_ref.shape[2] // 2
     each = own_rows // samples
     chips = places // lax.axis_size("pb")
-    weights = w_ref[...].reshape(width, 4 * feats)
+    weights = w_ref[:, :, : 4 * feats].reshape(width, 4 * feats)
     x = x_ref[...].reshape(places * own_rows, width).astype(f32)
     normed = layer_norm(x, gain_ref[...].reshape(1, -1)).astype(bf16)
     held_ref[...] = normed.reshape(places, own_rows, width)
@@ -175,8 +193,8 @@
     for side, ref in enumerate((w_ref, other_ref)):
         weights = ref[...].reshape(width, chips * feats)
         added = jnp.dot(gated, weights, preferred_element_type=f32)
-        for flip in range(chips):
-            held[at ^ (2 * flip + side)] = added[:, flip * feats : (flip + 1) * feats]
+        for i, flip in enumerate((0, 4, 2, 6)):
+            held[at ^ (flip + side)] = added[:, i * feats : (i + 1) * feats]
     added = jnp.concatenate([held[k] for k in range(ka_count)], axis=1)
     mixed = (single_ref[...].astype(f32) + added).astype(bf16)
     mixed_ref[...] = mixed
@@ -186,7 +204,7 @@
 
 def transition_kernel(x_ref, w_ref, out_ref):
     groups, rows, width = x_ref.shape
-    part = w_ref.shape[2] // 4
+    part = w_ref.shape[2] // 3
     x = x_ref[...].reshape(groups * rows, width)
     down, swish, up = (
         w_ref[:, :, i * part : (i + 1) * part].reshape(width, part) for i in range(3)
@@ -260,7 +278,7 @@
         lax.dynamic_slice_in_dim(w, ka_index * feats, feats, 1)
         for w in (w_key, w_value, w_query, w_gate)
     ]
-    early = jnp.concatenate(early + [w_down.T, w_swish, w_up, w_out], axis=1)
+    early = jnp.concatenate(early + [w_out, w_down.T, w_swish, w_up], axis=1)
     early, pair_rep = lax.optimization_barrier((early, pair_rep))
     early = spread(early, pb_count, "pb")
 
@@ -268,9 +286,10 @@
     keys_held = key_blocks * key_rows
     lanes = 2 * queries
     proj = pair_proj.reshape(channels, HEADS // 2, 2).transpose(2, 1, 0).reshape(HEADS, channels)
-    bias = call(
+    half = jax.ShapeDtypeStruct((ka_count // 2, keys_held, lanes), f32)
+    keep, one = call(
         bias_kernel,
-        (jax.ShapeDtypeStruct((keys_held, lanes), f32),) * ka_count,
+        (half, half),
         scratch=[
             pltpu.VMEM((queries * keys_held, channels), f32),
             pltpu.VMEM((ka_count, keys_held, lanes), f32),
@@ -278,30 +297,34 @@
         flops=2 * 6 * queries * keys_held * channels * HEADS,
         moved=queries * keys_held * channels * 2 + 4 * ka_count * keys_held * lanes,
     )(pair_rep.reshape(queries, keys_held, channels), pair_gain, proj)
-    near = [swap(bias[i], "ka", i) for i in (1, 2, 3)]
-    early, near = lax.optimization_barrier((early, near))
+    one = swap(one, "ka", 1)
+    two = swap(call(second_kernel, half)(keep, one), "ka", 2)
+    early, two = lax.optimization_barrier((early, two))
     early = early.reshape(pb_count * w_rows, early.shape[2])
 
-    attn_w = jnp.broadcast_to(early[None, :, : 4 * feats], (grp_count, pb_count * w_rows, 4 * feats))
-    late = early[:, 4 * feats :]
-    out_w = early[:, 4 * feats + 3 * hid :]
-    attn_w, late, out_w = lax.optimization_barrier((attn_w, late, out_w))
+    split = 5 * feats
+    attn_w = jnp.broadcast_to(early[None, :, :split], (grp_count, pb_count * w_rows, split))
+    late = early[:, split:]
+    attn_w, late = lax.optimization_barrier((attn_w, late))
     attn_w = exchange(attn_w, "grp")
 
-    late = [late] + [swap(late, "ka", TP)]
-    out_w = [late[0][:, 3 * hid :], swap(out_w, "ka", 2), late[1][:, 3 * hid :], swap(out_w, "ka", 6)]
-    late = jnp.concatenate(
-        [w[:, i * hid : (i + 1) * hid] for i in range(3) for w in late] + out_w, axis=1
-    )
+    late = [late, swap(late, "ka", TP)]
+    late = jnp.concatenate([w[:, i * hid : (i + 1) * hid] for i in range(3) for w in late], axis=1)
     late = jnp.broadcast_to(late[None], (grp_count,) + late.shape)
-    late, attn_w, far = lax.optimization_barrier((late, attn_w, list(bias[4:])))
+    late, attn_w, two = lax.optimization_barrier((late, attn_w, two))
     late = exchange(late, "grp")
-    far = [swap(block, "ka", i + 4) for i, block in enumerate(far)]
+    four = swap(call(third_kernel, half)(keep, one, two), "ka", 4)
     bias = call(
         place_kernel, jax.ShapeDtypeStruct((ka_count, keys_held, lanes), f32)
-    )(bias[0], *near, *far)
-    x, bias = lax.optimization_barrier((x, bias))
+    )(keep, one, two, four)
+
+    out_w = attn_w[:, :, 4 * feats :]
+    for flip in (4, 2):
+        out_w = jnp.concatenate([out_w, swap(out_w, "ka", flip)], axis=2)
+    x, bias, out_w = lax.optimization_barrier((x, bias, out_w))
     other = swap(x, "ka", 1)
+    other_w = swap(out_w, "ka", 1)
+    attn_w, late = lax.optimization_barrier((attn_w, late))
 
     line_rows = pb_count * chips * row_count
     kv_shape = (samples, line_rows, 2 * feats)
@@ -327,10 +350,7 @@
         scalars=1,
         **costs,
     )(lengths, other, attn_gain, attn_w, near_kv, near_query, bias)
-    gated, late = lax.optimization_barrier((gated, late))
     gated = exchange(gated, "ka")
-    out_w = late[:, :, held * 3 * hid :]
-    other_w = swap(out_w, "ka", 1)
 
     rows = jax.ShapeDtypeStruct((own_rows, width), bf16)
     shared = jax.ShapeDtypeStruct((TP, own_rows, width), bf16)

time: 141 us -> 158 us (1.12)
  waiting for transfers between devices: 11.5 us -> 34.4 us
  blocking collectives: 24.6 us -> 15.9 us
  Pallas kernels: 9.06 us -> 12.3 us
  starting transfers between devices: 70.1 us -> 67.8 us
  other arithmetic: 0 us -> 1.68 us
    all_to_all x3 -> x4, waiting for transfers between devices: 0.01 us -> 20.4 us  [exchange(): lax.all_to_all(blocks, axes, split_axis=0, concat_axis=0, tiled=True, axi...]
    ppermute x12 -> x8, starting transfers between devices: 41 us -> 28.7 us  [swap(): return lax.ppermute(block, axis, [(i, i ^ flip) for i in range(count)])]
    all_to_all x3 -> x4, starting transfers between devices: 29.1 us -> 39.1 us  [exchange(): lax.all_to_all(blocks, axes, split_axis=0, concat_axis=0, tiled=True, axi...]
    all_to_all x2 -> x1, blocking collectives: 17.7 us -> 8.96 us  [exchange(): lax.all_to_all(blocks, axes, split_axis=0, concat_axis=0, tiled=True, axi...]
    pallas_call x7 -> x9, Pallas kernels: 9.06 us -> 12.3 us  [run(): pl.pallas_call(kernel, out_shape=out_shape, in_specs=[pl.BlockSpec(memory...]
    ppermute x12 -> x8, waiting for transfers between devices: 10.8 us -> 13.3 us  [swap(): return lax.ppermute(block, axis, [(i, i ^ flip) for i in range(count)])]
    concatenate x0 -> x2, other arithmetic: none -> 1.68 us  [on_device(): out_w = jnp.concatenate([out_w, swap(out_w, 'ka', flip)], axis=2)]
    unnamed x12 -> x16, local copies, waits for them, and re-layouts: 3.11 us -> 3.6 us
  transfers between devices with their start and end apart: 16 -> 13, of which waited for: 6 -> 7; matrix products, arithmetic and copies ran while one was open for 5% -> 5% of each run, Pallas kernels for 5% -> 6%
where the time goes in v7:
time: 158 us; the launch traced here: 156 us
  starting transfers between devices  67.8 us (43%)
  waiting for transfers between devices  34.4 us (22%)
  blocking collectives  15.9 us (10%)
  between operations  14.3 us (9%)
  Pallas kernels  12.3 us (8%)
  local copies, waits for them, and re-layouts  10.2 us (6%)
  other arithmetic  1.68 us (1%)
    all_to_all x4, starting transfers between devices, exchange(): lax.all_to_all(blocks, axes, split_axis=0, concat_axis=0, tiled=True, axi...  39.1 us
    ppermute x8, starting transfers between devices, swap(): return lax.ppermute(block, axis, [(i, i ^ flip) for i in range(count)])  28.7 us
    all_to_all x4, waiting for transfers between devices, exchange(): lax.all_to_all(blocks, axes, split_axis=0, concat_axis=0, tiled=True, axi...  20.4 us
    ppermute x8, waiting for transfers between devices, swap(): return lax.ppermute(block, axis, [(i, i ^ flip) for i in range(count)])  13.3 us
    pallas_call x9, Pallas kernels, run(): pl.pallas_call(kernel, out_shape=out_shape, in_specs=[pl.BlockSpec(memory...  12.3 us
    all_to_all x1, blocking collectives, exchange(): lax.all_to_all(blocks, axes, split_axis=0, concat_axis=0, tiled=True, axi...  8.96 us
    all_gather x1, blocking collectives, on_device(): lax.all_gather(normed_t, 'ka', axis=0, tiled=False, axis_index_groups=gro...  6.96 us
    unnamed x16, local copies, waits for them, and re-layouts  3.6 us
  transfers between devices with their start and end apart: 13, of which 7 were waited for; matrix products, arithmetic and copies ran while one was open for 5% of the time, Pallas kernels for 6%

profile of v7, /device:TPU:1, one launch (start us, length us, event | category | flops | bytes accessed | tf_op | source)
XLA Modules:
  0.0 156.5 jit_solution(10427448836188320945)
XLA Ops:
  8.8 0.8 concatenate.13
  10.4 15.6 %all-to-all-start = ((bf16[4,12,1056]{2,1,0:T(8,128)(2,1)}), bf16[4,12,1056]{2,1,0:T(8,128)(2,1)S(1)}, u32[]{:S(2)}, u32[]{:S(2)}) async-start(bf16[4,12,1056]{2,1,0:T(8,128)(2,1)} %broadcast_in_dim.6), calls=%async_computation | async-start | bytes 294912 | tf_op jit(solution)/shard_map/all_to_all | solution.py:36
  26.7 1.0 copy-done.1
  28.4 1.8 %shard_map.145 = (f32[4,32,128]{2,1,0:T(8,128)S(1)}, f32[4,32,128]{2,1,0:T(8,128)S(1)}) custom-call(bf16[64,32,128]{2,1,0:T(8,128)(2,1)S(1)} %bitcast.13, f32[128]{0:T(128)S(1)} %copy-done.5, f32[16,128]{1,0:T(8,128)S(1)} %bitcast.16), custom_call_target="tpu_custom_call" | custom-call | flops 50331648 | bytes 655360 | tf_op jit(solution)/shard_map/pallas_call | solution.py:227
  30.2 2.9 %collective-permute-start = (f32[4,32,128]{2,1,0:T(8,128)S(1)}, f32[4,32,128]{2,1,0:T(8,128)S(1)}, u32[]{:S(2)}, u32[]{:S(2)}) collective-permute-start(f32[4,32,128]{2,1,0:T(8,128)S(1)} %get-tuple-element.27), channel_id=1, source_target_pairs={{0,1},{1,0},{2,3},{3,2},{4,5},{5,4},{6,7},{7,6},{8,9},{9,8},{10,11... | collective-permute-start | bytes 196616 | tf_op jit(solution)/shard_map/ppermute | solution.py:51
  33.0 0.9 collective-permute-done.one_ref
  33.9 2.6 %collective-permute-start.1 = (f32[4,32,128]{2,1,0:T(8,128)S(1)}, f32[4,32,128]{2,1,0:T(8,128)S(1)}, u32[]{:S(2)}, u32[]{:S(2)}) collective-permute-start(f32[4,32,128]{2,1,0:T(8,128)S(1)} %shard_map.146), channel_id=1, source_target_pairs={{0,2},{1,3},{2,0},{3,1},{4,6},{5,7},{6,4},{7,5},{8,10},{9,11},{10,... | collective-permute-start | bytes 196616 | tf_op jit(solution)/shard_map/ppermute | solution.py:51
  36.6 2.8 %collective-permute-done.1.two_ref = f32[4,32,128]{2,1,0:T(8,128)S(1)} collective-permute-done((f32[4,32,128]{2,1,0:T(8,128)S(1)}, f32[4,32,128]{2,1,0:T(8,128)S(1)}, u32[]{:S(2)}, u32[]{:S(2)}) %collective-permute-start.1) | collective-permute-done | bytes 65568 | tf_op jit(solution)/shard_map/ppermute | solution.py:51
  39.5 1.0 broadcast_in_dim.7
  40.4 6.8 %all-to-all-start.1 = ((bf16[16,48,480]{2,1,0:T(8,128)(2,1)}), bf16[16,48,480]{2,1,0:T(8,128)(2,1)S(1)}, u32[]{:S(2)}, u32[]{:S(2)}) async-start(bf16[16,48,480]{2,1,0:T(8,128)(2,1)} %broadcast_in_dim.7), calls=%async_computation.1 | async-start | bytes 1572864 | tf_op jit(solution)/shard_map/all_to_all | solution.py:36
  47.2 4.5 %collective-permute-start.2 = (bf16[48,576]{1,0:T(8,128)(2,1)S(1)}, bf16[48,576]{1,0:T(8,128)(2,1)S(1)}, u32[]{:S(2)}, u32[]{:S(2)}) collective-permute-start(bf16[48,576]{1,0:T(8,128)(2,1)S(1)} %slice.37), channel_id=1, source_target_pairs={{0,4},{1,5},{2,6},{3,7},{4,0},{5,1},{6,2},{7,3},{8,12},{9,13},{10,... | collective-permute-start | bytes 165896 | tf_op jit(solution)/shard_map/ppermute | solution.py:51
  51.8 1.9 %collective-permute-done.2 = bf16[48,576]{1,0:T(8,128)(2,1)S(1)} collective-permute-done((bf16[48,576]{1,0:T(8,128)(2,1)S(1)}, bf16[48,576]{1,0:T(8,128)(2,1)S(1)}, u32[]{:S(2)}, u32[]{:S(2)}) %collective-permute-start.2) | collective-permute-done | bytes 55328 | tf_op jit(solution)/shard_map/ppermute | solution.py:51
  53.9 4.0 %all-to-all-done.1.w_ref = bf16[16,48,480]{2,1,0:T(8,128)(2,1)S(1)} async-done(((bf16[16,48,480]{2,1,0:T(8,128)(2,1)}), bf16[16,48,480]{2,1,0:T(8,128)(2,1)S(1)}, u32[]{:S(2)}, u32[]{:S(2)}) %all-to-all-start.1) | async-done | bytes 737312 | tf_op jit(solution)/shard_map/all_to_all | solution.py:36
  57.9 1.4 broadcast_in_dim.8
  59.3 4.4 %collective-permute-start.4 = (bf16[16,48,96]{2,1,0:T(8,128)(2,1)S(1)}, bf16[16,48,96]{2,1,0:T(8,128)(2,1)S(1)}, u32[]{:S(2)}, u32[]{:S(2)}) collective-permute-start(bf16[16,48,96]{2,1,0:T(8,128)(2,1)S(1)} %slice.35), channel_id=1, source_target_pairs={{0,4},{1,5},{2,6},{3,7},{4,0},{5,1},{6,2},{7,3},{8,12},{9,13},{10,... | collective-permute-start | bytes 442376 | tf_op jit(solution)/shard_map/ppermute | solution.py:51
  63.7 7.7 %collective-permute-done.4 = bf16[16,48,96]{2,1,0:T(8,128)(2,1)S(1)} collective-permute-done((bf16[16,48,96]{2,1,0:T(8,128)(2,1)S(1)}, bf16[16,48,96]{2,1,0:T(8,128)(2,1)S(1)}, u32[]{:S(2)}, u32[]{:S(2)}) %collective-permute-start.4) | collective-permute-done | bytes 147488 | tf_op jit(solution)/shard_map/ppermute | solution.py:51
  72.1 1.9 %collective-permute-start.5 = (bf16[16,48,192]{2,1,0:T(8,128)(2,1)S(1)}, bf16[16,48,192]{2,1,0:T(8,128)(2,1)}, u32[]{:S(2)}, u32[]{:S(2)}) collective-permute-start(bf16[16,48,192]{2,1,0:T(8,128)(2,1)S(1)} %pad_maximum_fusion.1), channel_id=1, source_target_pairs={{0,2},{1,3},{2,0},{3,1},{4,6},{5,7},{6,4},{7,5},{8,10},{9,11},{10,... | collective-permute-start | bytes 884744 | tf_op jit(solution)/shard_map/ppermute | solution.py:51
  74.0 3.4 %collective-permute-start.3 = (f32[4,32,128]{2,1,0:T(8,128)S(1)}, f32[4,32,128]{2,1,0:T(8,128)S(1)}, u32[]{:S(2)}, u32[]{:S(2)}) collective-permute-start(f32[4,32,128]{2,1,0:T(8,128)S(1)} %shard_map.147), channel_id=1, source_target_pairs={{0,4},{1,5},{2,6},{3,7},{4,0},{5,1},{6,2},{7,3},{8,12},{9,13},{10,... | collective-permute-start | bytes 196616 | tf_op jit(solution)/shard_map/ppermute | solution.py:51
  77.4 8.0 %all-to-all-start.2 = ((bf16[16,48,1152]{2,1,0:T(8,128)(2,1)}), bf16[16,48,1152]{2,1,0:T(8,128)(2,1)S(1)}, u32[]{:S(2)}, u32[]{:S(2)}) async-start(bf16[16,48,1152]{2,1,0:T(8,128)(2,1)} %broadcast_in_dim.8), calls=%async_computation.2 | async-start | bytes 3538944 | tf_op jit(solution)/shard_map/all_to_all | solution.py:36
  85.5 1.5 pad_maximum_fusion.w_ref
  87.0 7.0 %collective-permute-start.6 = (bf16[16,64,768]{2,1,0:T(8,128)(2,1)}, bf16[16,64,768]{2,1,0:T(8,128)(2,1)}, u32[]{:S(2)}, u32[]{:S(2)}) collective-permute-start(bf16[16,64,768]{2,1,0:T(8,128)(2,1)} %all-gather.3.cloned.1.call-done.x_ref), channel_id=1, source_target_pairs={{0,1},{1,0},{2,3},{3,2},{4,5},{5,4},{6,7},{7,6},{8,9},{9,8},{10,11... | collective-permute-start | bytes 4718600 | tf_op jit(solution)/shard_map/ppermute | solution.py:51
  94.0 1.9 %collective-permute-start.7 = (bf16[16,48,384]{2,1,0:T(8,128)(2,1)S(1)}, bf16[16,48,384]{2,1,0:T(8,128)(2,1)}, u32[]{:S(2)}, u32[]{:S(2)}) collective-permute-start(bf16[16,48,384]{2,1,0:T(8,128)(2,1)S(1)} %pad_maximum_fusion.w_ref), channel_id=1, source_target_pairs={{0,1},{1,0},{2,3},{3,2},{4,5},{5,4},{6,7},{7,6},{8,9},{9,8},{10,11... | collective-permute-start | bytes 1769480 | tf_op jit(solution)/shard_map/ppermute | solution.py:51
  96.6 10.6 %all-to-all-done.2.w_ref = bf16[16,48,1152]{2,1,0:T(8,128)(2,1)S(1)} async-done(((bf16[16,48,1152]{2,1,0:T(8,128)(2,1)}), bf16[16,48,1152]{2,1,0:T(8,128)(2,1)S(1)}, u32[]{:S(2)}, u32[]{:S(2)}) %all-to-all-start.2) | async-done | bytes 1769504 | tf_op jit(solution)/shard_map/all_to_all | solution.py:36
  107.2 1.4 copy-done
  108.6 1.4 shard_map.149
  110.0 5.7 %shard_map.150 = bf16[8,64,96]{2,1,0:T(8,128)(2,1)} custom-call(s32[1]{0:T(128)S(6)} %copy.21.length_ref, bf16[16,64,768]{2,1,0:T(8,128)(2,1)} %collective-permute-done.6.x_ref, f32[768]{0:T(1024)S(1)} %copy-done.3, bf16[16,48,480]{2,1,0:T(8,128)(2,1)S(1)} %all-to-all-done.1.w_ref, bf16[8,128,192]{2,1,0:T(8,128)(2,1)S(1)} %get-tuple-element.38.kv_ref, ...), custom_call_target="tpu_custom_call" | custom-call | flops 452984832 | bytes 2310144 | tf_op jit(solution)/shard_map/pallas_call | solution.py:227
  115.7 8.8 %all-to-all-start.3 = ((bf16[8,64,96]{2,1,0:T(8,128)(2,1)}), bf16[8,64,96]{2,1,0:T(8,128)(2,1)S(1)}, u32[]{:S(2)}, u32[]{:S(2)}) async-start(bf16[8,64,96]{2,1,0:T(8,128)(2,1)} %shard_map.150), calls=%async_computation.3 | async-start | bytes 262144 | tf_op jit(solution)/shard_map/all_to_all | solution.py:36
  124.5 5.8 %all-to-all-done.3.gated_ref = bf16[8,64,96]{2,1,0:T(8,128)(2,1)S(1)} async-done(((bf16[8,64,96]{2,1,0:T(8,128)(2,1)}), bf16[8,64,96]{2,1,0:T(8,128)(2,1)S(1)}, u32[]{:S(2)}, u32[]{:S(2)}) %all-to-all-start.3) | async-done | bytes 98336 | tf_op jit(solution)/shard_map/all_to_all | solution.py:36
  130.3 1.8 %shard_map.151 = (bf16[64,768]{1,0:T(8,128)(2,1)S(1)}, bf16[64,768]{1,0:T(8,128)(2,1)S(1)}) custom-call(bf16[8,64,96]{2,1,0:T(8,128)(2,1)S(1)} %all-to-all-done.3.gated_ref, bf16[16,48,384]{2,1,0:T(8,128)(2,1)S(1)} %pad_maximum_fusion.w_ref, bf16[16,48,384]{2,1,0:T(8,128)(2,1)} %collective-permute-done.7.other_ref, bf16[64,768]{1,0:T(8,128)(2,1)S(1)} %bitcast.15, ...), custom_call_target="tpu_custom_call" | custom-call | flops 75497472 | bytes 1179648 | tf_op jit(solution)/shard_map/pallas_call | solution.py:227
  132.2 7.0 %all-gather = bf16[256,768]{1,0:T(8,128)(2,1)S(1)} all-gather(bf16[64,768]{1,0:T(8,128)(2,1)S(1)} %get-tuple-element.43), channel_id=2, replica_groups={{0,1,2,3},{4,5,6,7},{8,9,10,11},{12,13,14,15},{16,17,18,19},{20,21,22,2..., dimensions={0}, use_global_device_ids=true | all-gather | bytes 491520 | tf_op jit(solution)/shard_map/all_gather | solution.py:366
  139.1 0.8 shard_map.152
  140.0 9.0 %all_to_all.25.part_ref = bf16[4,64,768]{2,1,0:T(8,128)(2,1)S(1)} all-to-all(bf16[4,64,768]{2,1,0:T(8,128)(2,1)S(1)} %shard_map.152), channel_id=1, replica_groups={{0,1,2,3},{4,5,6,7},{8,9,10,11},{12,13,14,15},{16,17,18,19},{20,21,22,2..., dimensions={0} | all-to-all | bytes 786432 | tf_op jit(solution)/shard_map/all_to_all | solution.py:36
  (38 shorter events, 6.2 us)
Async XLA Ops:
  6.5 80.4 %all-gather.3.cloned.1.call-start = ((), (), s32[]{:S(2)}) async-start(), calls=%async_computation.5 | async-start | bytes 1671168 | tf_op jit(solution)/shard_map/all_gather | solution.py:275
  10.4 28.9 %all-to-all-start = ((bf16[4,12,1056]{2,1,0:T(8,128)(2,1)}), bf16[4,12,1056]{2,1,0:T(8,128)(2,1)S(1)}, u32[]{:S(2)}, u32[]{:S(2)}) async-start(bf16[4,12,1056]{2,1,0:T(8,128)(2,1)} %broadcast_in_dim.6), calls=%async_computation | async-start | bytes 294912 | tf_op jit(solution)/shard_map/all_to_all | solution.py:36
  26.7 1.0 copy-start.1
  27.7 0.7 copy-start.5
  30.2 3.8 %collective-permute-start = (f32[4,32,128]{2,1,0:T(8,128)S(1)}, f32[4,32,128]{2,1,0:T(8,128)S(1)}, u32[]{:S(2)}, u32[]{:S(2)}) collective-permute-start(f32[4,32,128]{2,1,0:T(8,128)S(1)} %get-tuple-element.27), channel_id=1, source_target_pairs={{0,1},{1,0},{2,3},{3,2},{4,5},{5,4},{6,7},{7,6},{8,9},{9,8},{10,11... | collective-permute-start | bytes 196616 | tf_op jit(solution)/shard_map/ppermute | solution.py:51
  33.9 5.4 %collective-permute-start.1 = (f32[4,32,128]{2,1,0:T(8,128)S(1)}, f32[4,32,128]{2,1,0:T(8,128)S(1)}, u32[]{:S(2)}, u32[]{:S(2)}) collective-permute-start(f32[4,32,128]{2,1,0:T(8,128)S(1)} %shard_map.146), channel_id=1, source_target_pairs={{0,2},{1,3},{2,0},{3,1},{4,6},{5,7},{6,4},{7,5},{8,10},{9,11},{10,... | collective-permute-start | bytes 196616 | tf_op jit(solution)/shard_map/ppermute | solution.py:51
  40.4 17.4 %all-to-all-start.1 = ((bf16[16,48,480]{2,1,0:T(8,128)(2,1)}), bf16[16,48,480]{2,1,0:T(8,128)(2,1)S(1)}, u32[]{:S(2)}, u32[]{:S(2)}) async-start(bf16[16,48,480]{2,1,0:T(8,128)(2,1)} %broadcast_in_dim.7), calls=%async_computation.1 | async-start | bytes 1572864 | tf_op jit(solution)/shard_map/all_to_all | solution.py:36
  47.2 6.5 %collective-permute-start.2 = (bf16[48,576]{1,0:T(8,128)(2,1)S(1)}, bf16[48,576]{1,0:T(8,128)(2,1)S(1)}, u32[]{:S(2)}, u32[]{:S(2)}) collective-permute-start(bf16[48,576]{1,0:T(8,128)(2,1)S(1)} %slice.37), channel_id=1, source_target_pairs={{0,4},{1,5},{2,6},{3,7},{4,0},{5,1},{6,2},{7,3},{8,12},{9,13},{10,... | collective-permute-start | bytes 165896 | tf_op jit(solution)/shard_map/ppermute | solution.py:51
  59.3 12.3 %copy-start.6 = (bf16[16,48,96]{2,1,0:T(8,128)(2,1)}, bf16[16,48,96]{2,1,0:T(8,128)(2,1)S(1)}, u32[]{:S(2)}) copy-start(bf16[16,48,96]{2,1,0:T(8,128)(2,1)S(1)} %slice.35) | copy-start | bytes 442372
  59.3 12.1 %collective-permute-start.4 = (bf16[16,48,96]{2,1,0:T(8,128)(2,1)S(1)}, bf16[16,48,96]{2,1,0:T(8,128)(2,1)S(1)}, u32[]{:S(2)}, u32[]{:S(2)}) collective-permute-start(bf16[16,48,96]{2,1,0:T(8,128)(2,1)S(1)} %slice.35), channel_id=1, source_target_pairs={{0,4},{1,5},{2,6},{3,7},{4,0},{5,1},{6,2},{7,3},{8,12},{9,13},{10,... | collective-permute-start | bytes 442376 | tf_op jit(solution)/shard_map/ppermute | solution.py:51
  71.4 0.7 copy-start.7
  72.1 13.4 %collective-permute-start.5 = (bf16[16,48,192]{2,1,0:T(8,128)(2,1)S(1)}, bf16[16,48,192]{2,1,0:T(8,128)(2,1)}, u32[]{:S(2)}, u32[]{:S(2)}) collective-permute-start(bf16[16,48,192]{2,1,0:T(8,128)(2,1)S(1)} %pad_maximum_fusion.1), channel_id=1, source_target_pairs={{0,2},{1,3},{2,0},{3,1},{4,6},{5,7},{6,4},{7,5},{8,10},{9,11},{10,... | collective-permute-start | bytes 884744 | tf_op jit(solution)/shard_map/ppermute | solution.py:51
  74.0 11.4 %collective-permute-start.3 = (f32[4,32,128]{2,1,0:T(8,128)S(1)}, f32[4,32,128]{2,1,0:T(8,128)S(1)}, u32[]{:S(2)}, u32[]{:S(2)}) collective-permute-start(f32[4,32,128]{2,1,0:T(8,128)S(1)} %shard_map.147), channel_id=1, source_target_pairs={{0,4},{1,5},{2,6},{3,7},{4,0},{5,1},{6,2},{7,3},{8,12},{9,13},{10,... | collective-permute-start | bytes 196616 | tf_op jit(solution)/shard_map/ppermute | solution.py:51
  77.4 29.7 %all-to-all-start.2 = ((bf16[16,48,1152]{2,1,0:T(8,128)(2,1)}), bf16[16,48,1152]{2,1,0:T(8,128)(2,1)S(1)}, u32[]{:S(2)}, u32[]{:S(2)}) async-start(bf16[16,48,1152]{2,1,0:T(8,128)(2,1)} %broadcast_in_dim.8), calls=%async_computation.2 | async-start | bytes 3538944 | tf_op jit(solution)/shard_map/all_to_all | solution.py:36
  85.4 21.8 %copy-start.3 = (f32[768]{0:T(1024)S(1)}, f32[768]{0:T(1024)}, u32[]{:S(2)}) copy-start(f32[768]{0:T(1024)} %gain_ref.6) | copy-start | bytes 9220
  87.0 23.0 %collective-permute-start.6 = (bf16[16,64,768]{2,1,0:T(8,128)(2,1)}, bf16[16,64,768]{2,1,0:T(8,128)(2,1)}, u32[]{:S(2)}, u32[]{:S(2)}) collective-permute-start(bf16[16,64,768]{2,1,0:T(8,128)(2,1)} %all-gather.3.cloned.1.call-done.x_ref), channel_id=1, source_target_pairs={{0,1},{1,0},{2,3},{3,2},{4,5},{5,4},{6,7},{7,6},{8,9},{9,8},{10,11... | collective-permute-start | bytes 4718600 | tf_op jit(solution)/shard_map/ppermute | solution.py:51
  94.0 30.5 %collective-permute-start.7 = (bf16[16,48,384]{2,1,0:T(8,128)(2,1)S(1)}, bf16[16,48,384]{2,1,0:T(8,128)(2,1)}, u32[]{:S(2)}, u32[]{:S(2)}) collective-permute-start(bf16[16,48,384]{2,1,0:T(8,128)(2,1)S(1)} %pad_maximum_fusion.w_ref), channel_id=1, source_target_pairs={{0,1},{1,0},{2,3},{3,2},{4,5},{5,4},{6,7},{7,6},{8,9},{9,8},{10,11... | collective-permute-start | bytes 1769480 | tf_op jit(solution)/shard_map/ppermute | solution.py:51
  107.2 1.4 copy-start
  110.0 20.3 %copy-start.2 = (bf16[1,8,8,768]{3,2,1,0:T(8,128)(2,1)S(1)}, bf16[1,8,8,768]{3,2,1,0:T(8,128)(2,1)}, u32[]{:S(2)}) copy-start(bf16[1,8,8,768]{3,2,1,0:T(8,128)(2,1)} %param.16) | copy-start | bytes 294916
  110.0 20.3 %copy-start.4 = (f32[768]{0:T(1024)S(1)}, f32[768]{0:T(1024)}, u32[]{:S(2)}) copy-start(f32[768]{0:T(1024)} %gain_ref.7) | copy-start | bytes 9220
  115.7 14.6 %all-to-all-start.3 = ((bf16[8,64,96]{2,1,0:T(8,128)(2,1)}), bf16[8,64,96]{2,1,0:T(8,128)(2,1)S(1)}, u32[]{:S(2)}, u32[]{:S(2)}) async-start(bf16[8,64,96]{2,1,0:T(8,128)(2,1)} %shard_map.150), calls=%async_computation.3 | async-start | bytes 262144 | tf_op jit(solution)/shard_map/all_to_all | solution.py:36
Sparse Core Ops, SparseCore 0:
  9.4 74.8 all-gather.2

commit v8 on v7

--- a/solution.py
+++ b/solution.py
@@ -101,7 +101,7 @@
     feats = kv_ref.shape[2] // 2
     each = own_rows // samples
     chips = places // lax.axis_size("pb")
-    weights = w_ref[:, :, : 4 * feats].reshape(width, 4 * feats)
+    weights = w_ref[...].reshape(width, 4 * feats)
     x = x_ref[...].reshape(places * own_rows, width).astype(f32)
     normed = layer_norm(x, gain_ref[...].reshape(1, -1)).astype(bf16)
     held_ref[...] = normed.reshape(places, own_rows, width)
@@ -193,8 +193,8 @@
     for side, ref in enumerate((w_ref, other_ref)):
         weights = ref[...].reshape(width, chips * feats)
         added = jnp.dot(gated, weights, preferred_element_type=f32)
-        for i, flip in enumerate((0, 4, 2, 6)):
-            held[at ^ (flip + side)] = added[:, i * feats : (i + 1) * feats]
+        for flip in range(chips):
+            held[at ^ (2 * flip + side)] = added[:, flip * feats : (flip + 1) * feats]
     added = jnp.concatenate([held[k] for k in range(ka_count)], axis=1)
     mixed = (single_ref[...].astype(f32) + added).astype(bf16)
     mixed_ref[...] = mixed
@@ -204,7 +204,7 @@
 
 def transition_kernel(x_ref, w_ref, out_ref):
     groups, rows, width = x_ref.shape
-    part = w_ref.shape[2] // 3
+    part = w_ref.shape[2] // 4
     x = x_ref[...].reshape(groups * rows, width)
     down, swish, up = (
         w_ref[:, :, i * part : (i + 1) * part].reshape(width, part) for i in range(3)
@@ -278,7 +278,7 @@
         lax.dynamic_slice_in_dim(w, ka_index * feats, feats, 1)
         for w in (w_key, w_value, w_query, w_gate)
     ]
-    early = jnp.concatenate(early + [w_out, w_down.T, w_swish, w_up], axis=1)
+    early = jnp.concatenate(early + [w_down.T, w_swish, w_up, w_out], axis=1)
     early, pair_rep = lax.optimization_barrier((early, pair_rep))
     early = spread(early, pb_count, "pb")
 
@@ -302,29 +302,24 @@
     early, two = lax.optimization_barrier((early, two))
     early = early.reshape(pb_count * w_rows, early.shape[2])
 
-    split = 5 * feats
-    attn_w = jnp.broadcast_to(early[None, :, :split], (grp_count, pb_count * w_rows, split))
-    late = early[:, split:]
-    attn_w, late = lax.optimization_barrier((attn_w, late))
-    attn_w = exchange(attn_w, "grp")
-
+    late = early[:, 4 * feats :]
+    out_w = early[:, 4 * feats + 3 * hid :]
     late = [late, swap(late, "ka", TP)]
-    late = jnp.concatenate([w[:, i * hid : (i + 1) * hid] for i in range(3) for w in late], axis=1)
+    out_w = [late[0][:, 3 * hid :], swap(out_w, "ka", 2), late[1][:, 3 * hid :], swap(out_w, "ka", 6)]
+    late = jnp.concatenate(
+        [w[:, i * hid : (i + 1) * hid] for i in range(3) for w in late] + out_w, axis=1
+    )
     late = jnp.broadcast_to(late[None], (grp_count,) + late.shape)
-    late, attn_w, two = lax.optimization_barrier((late, attn_w, two))
-    late = exchange(late, "grp")
     four = swap(call(third_kernel, half)(keep, one, two), "ka", 4)
     bias = call(
         place_kernel, jax.ShapeDtypeStruct((ka_count, keys_held, lanes), f32)
     )(keep, one, two, four)
 
-    out_w = attn_w[:, :, 4 * feats :]
-    for flip in (4, 2):
-        out_w = jnp.concatenate([out_w, swap(out_w, "ka", flip)], axis=2)
-    x, bias, out_w = lax.optimization_barrier((x, bias, out_w))
+    late, attn_w, bias = lax.optimization_barrier((late, early[:, : 4 * feats], bias))
+    late = exchange(late, "grp")
+    attn_w = gather(attn_w, "grp")
+    x, attn_w = lax.optimization_barrier((x, attn_w))
     other = swap(x, "ka", 1)
-    other_w = swap(out_w, "ka", 1)
-    attn_w, late = lax.optimization_barrier((attn_w, late))
 
     line_rows = pb_count * chips * row_count
     kv_shape = (samples, line_rows, 2 * feats)
@@ -350,7 +345,10 @@
         scalars=1,
         **costs,
     )(lengths, other, attn_gain, attn_w, near_kv, near_query, bias)
+    gated, late = lax.optimization_barrier((gated, late))
     gated = exchange(gated, "ka")
+    out_w = late[:, :, held * 3 * hid :]
+    other_w = swap(out_w, "ka", 1)
 
     rows = jax.ShapeDtypeStruct((own_rows, width), bf16)
     shared = jax.ShapeDtypeStruct((TP, own_rows, width), bf16)

time: 158 us -> 161 us (1.019)
  blocking collectives: 15.9 us -> 67.8 us
  waiting for transfers between devices: 34.4 us -> 8.93 us
  starting transfers between devices: 67.8 us -> 51.4 us
  Pallas kernels: 12.3 us -> 9.12 us
  other arithmetic: 1.68 us -> 0 us
    all_gather x0 -> x1, blocking collectives: none -> 42.8 us  [gather(): return lax.all_gather(block, axes, axis=0, tiled=False)]
    all_to_all x4 -> x2, waiting for transfers between devices: 20.4 us -> 0.01 us  [exchange(): lax.all_to_all(blocks, axes, split_axis=0, concat_axis=0, tiled=True, axi...]
    all_to_all x4 -> x2, starting transfers between devices: 39.1 us -> 22.6 us  [exchange(): lax.all_to_all(blocks, axes, split_axis=0, concat_axis=0, tiled=True, axi...]
    all_to_all x1 -> x2, blocking collectives: 8.96 us -> 18 us  [exchange(): lax.all_to_all(blocks, axes, split_axis=0, concat_axis=0, tiled=True, axi...]
    ppermute x8, waiting for transfers between devices: 13.3 us -> 8.22 us  [swap(): return lax.ppermute(block, axis, [(i, i ^ flip) for i in range(count)])]
    pallas_call x9, Pallas kernels: 12.3 us -> 9.12 us  [run(): pl.pallas_call(kernel, out_shape=out_shape, in_specs=[pl.BlockSpec(memory...]
    concatenate x2 -> x0, other arithmetic: 1.68 us -> none  [on_device(): out_w = jnp.concatenate([out_w, swap(out_w, 'ka', flip)], axis=2)]
    unnamed x16 -> x12, local copies, waits for them, and re-layouts: 3.6 us -> 3.11 us
  transfers between devices with their start and end apart: 13 -> 11, of which waited for: 7 -> 3; matrix products, arithmetic and copies ran while one was open for 5% -> 4% of each run, Pallas kernels for 6% -> 4%
where the time goes in v8:
time: 161 us
  blocking collectives  67.8 us (42%)
  starting transfers between devices  51.4 us (32%)
  between operations  14.3 us (9%)
  local copies, waits for them, and re-layouts  9.13 us (6%)
  Pallas kernels  9.12 us (6%)
  waiting for transfers between devices  8.93 us (6%)
    all_gather x1, blocking collectives, gather(): return lax.all_gather(block, axes, axis=0, tiled=False)  42.8 us
    ppermute x8, starting transfers between devices, swap(): return lax.ppermute(block, axis, [(i, i ^ flip) for i in range(count)])  28.8 us
    all_to_all x2, starting transfers between devices, exchange(): lax.all_to_all(blocks, axes, split_axis=0, concat_axis=0, tiled=True, axi...  22.6 us
    all_to_all x2, blocking collectives, exchange(): lax.all_to_all(blocks, axes, split_axis=0, concat_axis=0, tiled=True, axi...  18 us
    pallas_call x9, Pallas kernels, run(): pl.pallas_call(kernel, out_shape=out_shape, in_specs=[pl.BlockSpec(memory...  9.12 us
    ppermute x8, waiting for transfers between devices, swap(): return lax.ppermute(block, axis, [(i, i ^ flip) for i in range(count)])  8.22 us
    all_gather x1, blocking collectives, on_device(): lax.all_gather(normed_t, 'ka', axis=0, tiled=False, axis_index_groups=gro...  6.96 us
  transfers between devices with their start and end apart: 11, of which 3 were waited for; matrix products, arithmetic and copies ran while one was open for 4% of the time, Pallas kernels for 4%

profile of v8, /device:TPU:1, one launch (start us, length us, event | category | flops | bytes accessed | tf_op | source)
XLA Modules:
  0.0 160.6 jit_solution(17420223217848008332)
XLA Ops:
  6.5 0.7 all-gather.4.cloned.1.call-update
  7.3 0.8 constant_dynamic-slice_fusion.2
  8.1 0.8 constant_dynamic-slice_fusion
  8.8 0.8 concatenate.6
  9.7 0.7 broadcast_in_dim.4
  10.4 15.6 %all-to-all-start = ((bf16[4,12,1056]{2,1,0:T(8,128)(2,1)}), bf16[4,12,1056]{2,1,0:T(8,128)(2,1)S(1)}, u32[]{:S(2)}, u32[]{:S(2)}) async-start(bf16[4,12,1056]{2,1,0:T(8,128)(2,1)} %broadcast_in_dim.4), calls=%async_computation | async-start | bytes 294912 | tf_op jit(solution)/shard_map/all_to_all | solution.py:36
  26.0 0.7 copy.20
  26.7 1.0 copy-done.1
  28.4 1.8 %shard_map.145 = (f32[4,32,128]{2,1,0:T(8,128)S(1)}, f32[4,32,128]{2,1,0:T(8,128)S(1)}) custom-call(bf16[64,32,128]{2,1,0:T(8,128)(2,1)S(1)} %bitcast.16, f32[128]{0:T(128)S(1)} %copy-done.5, f32[16,128]{1,0:T(8,128)S(1)} %bitcast.19), custom_call_target="tpu_custom_call" | custom-call | flops 50331648 | bytes 655360 | tf_op jit(solution)/shard_map/pallas_call | solution.py:227
  30.1 2.9 %collective-permute-start = (f32[4,32,128]{2,1,0:T(8,128)S(1)}, f32[4,32,128]{2,1,0:T(8,128)S(1)}, u32[]{:S(2)}, u32[]{:S(2)}) collective-permute-start(f32[4,32,128]{2,1,0:T(8,128)S(1)} %get-tuple-element.25), channel_id=1, source_target_pairs={{0,1},{1,0},{2,3},{3,2},{4,5},{5,4},{6,7},{7,6},{8,9},{9,8},{10,11... | collective-permute-start | bytes 196616 | tf_op jit(solution)/shard_map/ppermute | solution.py:51
  33.0 0.9 collective-permute-done.one_ref
  33.9 2.6 %collective-permute-start.1 = (f32[4,32,128]{2,1,0:T(8,128)S(1)}, f32[4,32,128]{2,1,0:T(8,128)S(1)}, u32[]{:S(2)}, u32[]{:S(2)}) collective-permute-start(f32[4,32,128]{2,1,0:T(8,128)S(1)} %shard_map.146), channel_id=1, source_target_pairs={{0,2},{1,3},{2,0},{3,1},{4,6},{5,7},{6,4},{7,5},{8,10},{9,11},{10,... | collective-permute-start | bytes 196616 | tf_op jit(solution)/shard_map/ppermute | solution.py:51
  36.5 2.8 %collective-permute-done.1.two_ref = f32[4,32,128]{2,1,0:T(8,128)S(1)} collective-permute-done((f32[4,32,128]{2,1,0:T(8,128)S(1)}, f32[4,32,128]{2,1,0:T(8,128)S(1)}, u32[]{:S(2)}, u32[]{:S(2)}) %collective-permute-start.1) | collective-permute-done | bytes 65568 | tf_op jit(solution)/shard_map/ppermute | solution.py:51
  39.4 4.4 %collective-permute-start.2 = (bf16[48,672]{1,0:T(8,128)(2,1)S(1)}, bf16[48,672]{1,0:T(8,128)(2,1)S(1)}, u32[]{:S(2)}, u32[]{:S(2)}) collective-permute-start(bf16[48,672]{1,0:T(8,128)(2,1)S(1)} %slice.50), channel_id=1, source_target_pairs={{0,4},{1,5},{2,6},{3,7},{4,0},{5,1},{6,2},{7,3},{8,12},{9,13},{10,... | collective-permute-start | bytes 193544 | tf_op jit(solution)/shard_map/ppermute | solution.py:51
  44.0 1.9 %collective-permute-start.3 = (bf16[48,96]{1,0:T(8,128)(2,1)S(1)}, bf16[48,96]{1,0:T(8,128)(2,1)S(1)}, u32[]{:S(2)}, u32[]{:S(2)}) collective-permute-start(bf16[48,96]{1,0:T(8,128)(2,1)S(1)} %slice.56), channel_id=1, source_target_pairs={{0,2},{1,3},{2,0},{3,1},{4,6},{5,7},{6,4},{7,5},{8,10},{9,11},{10,... | collective-permute-start | bytes 27656 | tf_op jit(solution)/shard_map/ppermute | solution.py:51
  45.9 3.5 %collective-permute-start.4 = (bf16[48,96]{1,0:T(8,128)(2,1)S(1)}, bf16[48,96]{1,0:T(8,128)(2,1)S(1)}, u32[]{:S(2)}, u32[]{:S(2)}) collective-permute-start(bf16[48,96]{1,0:T(8,128)(2,1)S(1)} %slice.56), channel_id=1, source_target_pairs={{0,6},{1,7},{2,4},{3,5},{4,2},{5,3},{6,0},{7,1},{8,14},{9,15},{10,... | collective-permute-start | bytes 27656 | tf_op jit(solution)/shard_map/ppermute | solution.py:51
  49.5 2.9 %collective-permute-start.5 = (f32[4,32,128]{2,1,0:T(8,128)S(1)}, f32[4,32,128]{2,1,0:T(8,128)S(1)}, u32[]{:S(2)}, u32[]{:S(2)}) collective-permute-start(f32[4,32,128]{2,1,0:T(8,128)S(1)} %shard_map.147), channel_id=1, source_target_pairs={{0,4},{1,5},{2,6},{3,7},{4,0},{5,1},{6,2},{7,3},{8,12},{9,13},{10,... | collective-permute-start | bytes 196616 | tf_op jit(solution)/shard_map/ppermute | solution.py:51
  52.7 4.6 %collective-permute-done.5.four_ref = f32[4,32,128]{2,1,0:T(8,128)S(1)} collective-permute-done((f32[4,32,128]{2,1,0:T(8,128)S(1)}, f32[4,32,128]{2,1,0:T(8,128)S(1)}, u32[]{:S(2)}, u32[]{:S(2)}) %collective-permute-start.5) | collective-permute-done | bytes 65568 | tf_op jit(solution)/shard_map/ppermute | solution.py:51
  57.3 1.7 %broadcast_in_dim.5 = bf16[16,48,1536]{2,1,0:T(8,128)(2,1)} broadcast(bf16[48,1536]{1,0:T(8,128)(2,1)S(1)} %concatenate.7), dimensions={1,2} | broadcast | bytes 2506752 | tf_op jit(solution)/shard_map/broadcast_in_dim | solution.py:312
  59.0 7.0 %all-to-all-start.1 = ((bf16[16,48,1536]{2,1,0:T(8,128)(2,1)}), bf16[16,48,1536]{2,1,0:T(8,128)(2,1)S(1)}, u32[]{:S(2)}, u32[]{:S(2)}) async-start(bf16[16,48,1536]{2,1,0:T(8,128)(2,1)} %broadcast_in_dim.5), calls=%async_computation.1 | async-start | bytes 4718592 | tf_op jit(solution)/shard_map/all_to_all | solution.py:36
  66.0 42.8 %all-gather = bf16[768,384]{1,0:T(8,128)(2,1)S(1)} all-gather(bf16[48,384]{1,0:T(8,128)(2,1)S(1)} %slice.58), channel_id=2, replica_groups=mesh['grp'=16,'pb'=4,'ka'=8] {'grp'}, dimensions={0}, use_global_device_ids=true | all-gather | bytes 626688 | tf_op jit(solution)/shard_map/all_gather | solution.py:46
  108.8 8.5 %collective-permute-start.6 = (bf16[16,64,768]{2,1,0:T(8,128)(2,1)}, bf16[16,64,768]{2,1,0:T(8,128)(2,1)S(1)}, u32[]{:S(2)}, u32[]{:S(2)}) collective-permute-start(bf16[16,64,768]{2,1,0:T(8,128)(2,1)} %all-gather.4.cloned.1.call-done.x_ref), channel_id=1, source_target_pairs={{0,1},{1,0},{2,3},{3,2},{4,5},{5,4},{6,7},{7,6},{8,9},{9,8},{10,11... | collective-permute-start | bytes 4718600 | tf_op jit(solution)/shard_map/ppermute | solution.py:51
  118.0 1.4 copy-done
  119.4 1.5 shard_map.149
  120.9 3.6 %shard_map.150 = bf16[8,64,96]{2,1,0:T(8,128)(2,1)S(1)} custom-call(s32[1]{0:T(128)S(6)} %copy.21.length_ref, bf16[16,64,768]{2,1,0:T(8,128)(2,1)S(1)} %collective-permute-done.6.x_ref, f32[768]{0:T(1024)S(1)} %copy-done.3, bf16[16,48,384]{2,1,0:T(8,128)(2,1)S(1)} %bitcast.14, bf16[8,128,192]{2,1,0:T(8,128)(2,1)S(1)} %get-tuple-element.31.kv_ref, ...), custom_call_target="tpu_custom_call" | custom-call | flops 452984832 | bytes 2162688 | tf_op jit(solution)/shard_map/pallas_call | solution.py:227
  124.6 2.0 %collective-permute-start.7 = (bf16[16,48,384]{2,1,0:T(8,128)(2,1)S(1)}, bf16[16,48,384]{2,1,0:T(8,128)(2,1)S(1)}, u32[]{:S(2)}, u32[]{:S(2)}) collective-permute-start(bf16[16,48,384]{2,1,0:T(8,128)(2,1)S(1)} %slice.48.w_ref), channel_id=1, source_target_pairs={{0,1},{1,0},{2,3},{3,2},{4,5},{5,4},{6,7},{7,6},{8,9},{9,8},{10,11... | collective-permute-start | bytes 1769480 | tf_op jit(solution)/shard_map/ppermute | solution.py:51
  126.5 9.0 %all_to_all.20.gated_ref = bf16[8,64,96]{2,1,0:T(8,128)(2,1)S(1)} all-to-all(bf16[8,64,96]{2,1,0:T(8,128)(2,1)S(1)} %shard_map.150), channel_id=1, replica_groups=mesh['grp'=16,'pb'=4,'ka'=8] {'ka'}, dimensions={0} | all-to-all | bytes 196608 | tf_op jit(solution)/shard_map/all_to_all | solution.py:36
  135.6 0.8 shard_map.151
  136.3 7.0 %all-gather.1 = bf16[256,768]{1,0:T(8,128)(2,1)S(1)} all-gather(bf16[64,768]{1,0:T(8,128)(2,1)S(1)} %get-tuple-element.38), channel_id=3, replica_groups={{0,1,2,3},{4,5,6,7},{8,9,10,11},{12,13,14,15},{16,17,18,19},{20,21,22,2..., dimensions={0}, use_global_device_ids=true | all-gather | bytes 491520 | tf_op jit(solution)/shard_map/all_gather | solution.py:364
  143.3 0.8 shard_map.152
  144.1 9.0 %all_to_all.21.part_ref = bf16[4,64,768]{2,1,0:T(8,128)(2,1)S(1)} all-to-all(bf16[4,64,768]{2,1,0:T(8,128)(2,1)S(1)} %shard_map.152), channel_id=1, replica_groups={{0,1,2,3},{4,5,6,7},{8,9,10,11},{12,13,14,15},{16,17,18,19},{20,21,22,2..., dimensions={0} | all-to-all | bytes 786432 | tf_op jit(solution)/shard_map/all_to_all | solution.py:36
  153.1 0.7 shard_map.153
  (31 shorter events, 1.3 us)
Async XLA Ops:
  6.5 102.3 %all-gather.4.cloned.1.call-start = ((), (), s32[]{:S(2)}) async-start(), calls=%async_computation.4 | async-start | bytes 1671168 | tf_op jit(solution)/shard_map/all_gather | solution.py:275
  10.4 28.9 %all-to-all-start = ((bf16[4,12,1056]{2,1,0:T(8,128)(2,1)}), bf16[4,12,1056]{2,1,0:T(8,128)(2,1)S(1)}, u32[]{:S(2)}, u32[]{:S(2)}) async-start(bf16[4,12,1056]{2,1,0:T(8,128)(2,1)} %broadcast_in_dim.4), calls=%async_computation | async-start | bytes 294912 | tf_op jit(solution)/shard_map/all_to_all | solution.py:36
  26.7 1.0 copy-start.1
  27.7 0.7 copy-start.5
  30.1 3.8 %collective-permute-start = (f32[4,32,128]{2,1,0:T(8,128)S(1)}, f32[4,32,128]{2,1,0:T(8,128)S(1)}, u32[]{:S(2)}, u32[]{:S(2)}) collective-permute-start(f32[4,32,128]{2,1,0:T(8,128)S(1)} %get-tuple-element.25), channel_id=1, source_target_pairs={{0,1},{1,0},{2,3},{3,2},{4,5},{5,4},{6,7},{7,6},{8,9},{9,8},{10,11... | collective-permute-start | bytes 196616 | tf_op jit(solution)/shard_map/ppermute | solution.py:51
  33.9 5.4 %collective-permute-start.1 = (f32[4,32,128]{2,1,0:T(8,128)S(1)}, f32[4,32,128]{2,1,0:T(8,128)S(1)}, u32[]{:S(2)}, u32[]{:S(2)}) collective-permute-start(f32[4,32,128]{2,1,0:T(8,128)S(1)} %shard_map.146), channel_id=1, source_target_pairs={{0,2},{1,3},{2,0},{3,1},{4,6},{5,7},{6,4},{7,5},{8,10},{9,11},{10,... | collective-permute-start | bytes 196616 | tf_op jit(solution)/shard_map/ppermute | solution.py:51
  39.4 13.0 %collective-permute-start.2 = (bf16[48,672]{1,0:T(8,128)(2,1)S(1)}, bf16[48,672]{1,0:T(8,128)(2,1)S(1)}, u32[]{:S(2)}, u32[]{:S(2)}) collective-permute-start(bf16[48,672]{1,0:T(8,128)(2,1)S(1)} %slice.50), channel_id=1, source_target_pairs={{0,4},{1,5},{2,6},{3,7},{4,0},{5,1},{6,2},{7,3},{8,12},{9,13},{10,... | collective-permute-start | bytes 193544 | tf_op jit(solution)/shard_map/ppermute | solution.py:51
  44.0 8.6 %collective-permute-start.3 = (bf16[48,96]{1,0:T(8,128)(2,1)S(1)}, bf16[48,96]{1,0:T(8,128)(2,1)S(1)}, u32[]{:S(2)}, u32[]{:S(2)}) collective-permute-start(bf16[48,96]{1,0:T(8,128)(2,1)S(1)} %slice.56), channel_id=1, source_target_pairs={{0,2},{1,3},{2,0},{3,1},{4,6},{5,7},{6,4},{7,5},{8,10},{9,11},{10,... | collective-permute-start | bytes 27656 | tf_op jit(solution)/shard_map/ppermute | solution.py:51
  45.9 6.7 %collective-permute-start.4 = (bf16[48,96]{1,0:T(8,128)(2,1)S(1)}, bf16[48,96]{1,0:T(8,128)(2,1)S(1)}, u32[]{:S(2)}, u32[]{:S(2)}) collective-permute-start(bf16[48,96]{1,0:T(8,128)(2,1)S(1)} %slice.56), channel_id=1, source_target_pairs={{0,6},{1,7},{2,4},{3,5},{4,2},{5,3},{6,0},{7,1},{8,14},{9,15},{10,... | collective-permute-start | bytes 27656 | tf_op jit(solution)/shard_map/ppermute | solution.py:51
  49.5 7.8 %collective-permute-start.5 = (f32[4,32,128]{2,1,0:T(8,128)S(1)}, f32[4,32,128]{2,1,0:T(8,128)S(1)}, u32[]{:S(2)}, u32[]{:S(2)}) collective-permute-start(f32[4,32,128]{2,1,0:T(8,128)S(1)} %shard_map.147), channel_id=1, source_target_pairs={{0,4},{1,5},{2,6},{3,7},{4,0},{5,1},{6,2},{7,3},{8,12},{9,13},{10,... | collective-permute-start | bytes 196616 | tf_op jit(solution)/shard_map/ppermute | solution.py:51
  59.0 59.0 %copy-start.3 = (f32[768]{0:T(1024)S(1)}, f32[768]{0:T(1024)}, u32[]{:S(2)}) copy-start(f32[768]{0:T(1024)} %gain_ref.6) | copy-start | bytes 9220
  59.0 65.5 %all-to-all-start.1 = ((bf16[16,48,1536]{2,1,0:T(8,128)(2,1)}), bf16[16,48,1536]{2,1,0:T(8,128)(2,1)S(1)}, u32[]{:S(2)}, u32[]{:S(2)}) async-start(bf16[16,48,1536]{2,1,0:T(8,128)(2,1)} %broadcast_in_dim.5), calls=%async_computation.1 | async-start | bytes 4718592 | tf_op jit(solution)/shard_map/all_to_all | solution.py:36
  108.8 12.1 %collective-permute-start.6 = (bf16[16,64,768]{2,1,0:T(8,128)(2,1)}, bf16[16,64,768]{2,1,0:T(8,128)(2,1)S(1)}, u32[]{:S(2)}, u32[]{:S(2)}) collective-permute-start(bf16[16,64,768]{2,1,0:T(8,128)(2,1)} %all-gather.4.cloned.1.call-done.x_ref), channel_id=1, source_target_pairs={{0,1},{1,0},{2,3},{3,2},{4,5},{5,4},{6,7},{7,6},{8,9},{9,8},{10,11... | collective-permute-start | bytes 4718600 | tf_op jit(solution)/shard_map/ppermute | solution.py:51
  118.0 1.4 copy-start
  120.9 14.7 %copy-start.2 = (bf16[1,8,8,768]{3,2,1,0:T(8,128)(2,1)S(1)}, bf16[1,8,8,768]{3,2,1,0:T(8,128)(2,1)}, u32[]{:S(2)}) copy-start(bf16[1,8,8,768]{3,2,1,0:T(8,128)(2,1)} %param.16) | copy-start | bytes 294916
  120.9 14.7 %copy-start.4 = (f32[768]{0:T(1024)S(1)}, f32[768]{0:T(1024)}, u32[]{:S(2)}) copy-start(f32[768]{0:T(1024)} %gain_ref.7) | copy-start | bytes 9220
  124.6 11.0 %collective-permute-start.7 = (bf16[16,48,384]{2,1,0:T(8,128)(2,1)S(1)}, bf16[16,48,384]{2,1,0:T(8,128)(2,1)S(1)}, u32[]{:S(2)}, u32[]{:S(2)}) collective-permute-start(bf16[16,48,384]{2,1,0:T(8,128)(2,1)S(1)} %slice.48.w_ref), channel_id=1, source_target_pairs={{0,1},{1,0},{2,3},{3,2},{4,5},{5,4},{6,7},{7,6},{8,9},{9,8},{10,11... | collective-permute-start | bytes 1769480 | tf_op jit(solution)/shard_map/ppermute | solution.py:51
Sparse Core Ops, SparseCore 0:
  9.4 70.8 all-gather.3

commit v9 on v6

--- a/solution.py
+++ b/solution.py
@@ -288,8 +288,11 @@
     attn_w, late, out_w = lax.optimization_barrier((attn_w, late, out_w))
     attn_w = exchange(attn_w, "grp")
 
-    late = [late] + [swap(late, "ka", TP)]
-    out_w = [late[0][:, 3 * hid :], swap(out_w, "ka", 2), late[1][:, 3 * hid :], swap(out_w, "ka", 6)]
+    farthest = swap(out_w, "ka", 6)
+    half = swap(late, "ka", TP)
+    out_w, half = lax.optimization_barrier((out_w, half))
+    late = [late, half]
+    out_w = [late[0][:, 3 * hid :], swap(out_w, "ka", 2), late[1][:, 3 * hid :], farthest]
     late = jnp.concatenate(
         [w[:, i * hid : (i + 1) * hid] for i in range(3) for w in late] + out_w, axis=1
     )

time: 141 us -> 141 us (level)
    ppermute x12, waiting for transfers between devices: 10.8 us -> 9.35 us  [swap(): return lax.ppermute(block, axis, [(i, i ^ flip) for i in range(count)])]
  transfers between devices with their start and end apart: 16 -> 16, of which waited for: 6 -> 7; matrix products, arithmetic and copies ran while one was open for 5% -> 5% of each run, Pallas kernels for 5% -> 5%
where the time goes in v9:
time: 141 us; the launch traced here: 140 us
  starting transfers between devices  71.3 us (51%)
  blocking collectives  25.1 us (18%)
  between operations  14.3 us (10%)
  waiting for transfers between devices  10.1 us (7%)
  local copies, waits for them, and re-layouts  10 us (7%)
  Pallas kernels  9.06 us (6%)
    ppermute x12, starting transfers between devices, swap(): return lax.ppermute(block, axis, [(i, i ^ flip) for i in range(count)])  42.1 us
    all_to_all x3, starting transfers between devices, exchange(): lax.all_to_all(blocks, axes, split_axis=0, concat_axis=0, tiled=True, axi...  29.2 us
    all_to_all x2, blocking collectives, exchange(): lax.all_to_all(blocks, axes, split_axis=0, concat_axis=0, tiled=True, axi...  18.1 us
    ppermute x12, waiting for transfers between devices, swap(): return lax.ppermute(block, axis, [(i, i ^ flip) for i in range(count)])  9.35 us
    pallas_call x7, Pallas kernels, run(): pl.pallas_call(kernel, out_shape=out_shape, in_specs=[pl.BlockSpec(memory...  9.06 us
    all_gather x1, blocking collectives, on_device(): lax.all_gather(normed_t, 'ka', axis=0, tiled=False, axis_index_groups=gro...  6.96 us
    unnamed x12, local copies, waits for them, and re-layouts  3.11 us
  transfers between devices with their start and end apart: 16, of which 7 were waited for; matrix products, arithmetic and copies ran while one was open for 5% of the time, Pallas kernels for 5%

profile of v9, /device:TPU:1, one launch (start us, length us, event | category | flops | bytes accessed | tf_op | source)
XLA Modules:
  0.0 139.9 jit_solution(11677987787108791090)
XLA Ops:
  7.3 0.8 constant_dynamic-slice_fusion.2
  8.1 0.8 constant_dynamic-slice_fusion
  8.8 0.8 concatenate.6
  10.3 15.6 %all-to-all-start = ((bf16[4,12,1056]{2,1,0:T(8,128)(2,1)}), bf16[4,12,1056]{2,1,0:T(8,128)(2,1)S(1)}, u32[]{:S(2)}, u32[]{:S(2)}) async-start(bf16[4,12,1056]{2,1,0:T(8,128)(2,1)} %broadcast_in_dim.6), calls=%async_computation | async-start | bytes 294912 | tf_op jit(solution)/shard_map/all_to_all | solution.py:36
  26.7 1.0 copy-done.1
  28.4 1.7 %shard_map.145 = (f32[32,128]{1,0:T(8,128)S(1)}, f32[32,128]{1,0:T(8,128)S(1)}, f32[32,128]{1,0:T(8,128)S(1)}, f32[32,128]{1,0:T(8,128)S(1)}, f32[32,128]{1,0:T(...) custom-call(bf16[64,32,128]{2,1,0:T(8,128)(2,1)S(1)} %bitcast.13, ...), custom_call_target="tpu_custom_call" | custom-call | flops 50331648 | bytes 655360 | tf_op jit(solution)/shard_map/pallas_call | solution.py:209
  30.1 2.9 %collective-permute-start = (f32[32,128]{1,0:T(8,128)S(1)}, f32[32,128]{1,0:T(8,128)S(1)}, u32[]{:S(2)}, u32[]{:S(2)}) collective-permute-start(f32[32,128]{1,0:T(8,128)S(1)} %get-tuple-element.41), channel_id=1, source_target_pairs={{0,1},{1,0},{2,3},{3,2},{4,5},{5,4},{6,7},{7,6},{8,9},{9,8},{10,11... | collective-permute-start | bytes 49160 | tf_op jit(solution)/shard_map/ppermute | solution.py:51
  33.0 2.6 %collective-permute-start.1 = (f32[32,128]{1,0:T(8,128)S(1)}, f32[32,128]{1,0:T(8,128)S(1)}, u32[]{:S(2)}, u32[]{:S(2)}) collective-permute-start(f32[32,128]{1,0:T(8,128)S(1)} %get-tuple-element.42), channel_id=1, source_target_pairs={{0,2},{1,3},{2,0},{3,1},{4,6},{5,7},{6,4},{7,5},{8,10},{9,11},{10,... | collective-permute-start | bytes 49160 | tf_op jit(solution)/shard_map/ppermute | solution.py:51
  35.6 2.8 %collective-permute-start.2 = (f32[32,128]{1,0:T(8,128)S(1)}, f32[32,128]{1,0:T(8,128)S(1)}, u32[]{:S(2)}, u32[]{:S(2)}) collective-permute-start(f32[32,128]{1,0:T(8,128)S(1)} %get-tuple-element.43), channel_id=1, source_target_pairs={{0,3},{1,2},{2,1},{3,0},{4,7},{5,6},{6,5},{7,4},{8,11},{9,10},{10,... | collective-permute-start | bytes 49160 | tf_op jit(solution)/shard_map/ppermute | solution.py:51
  38.5 2.5 %collective-permute-done.2.refs_3_ = f32[32,128]{1,0:T(8,128)S(1)} collective-permute-done((f32[32,128]{1,0:T(8,128)S(1)}, f32[32,128]{1,0:T(8,128)S(1)}, u32[]{:S(2)}, u32[]{:S(2)}) %collective-permute-start.2) | collective-permute-done | bytes 16416 | tf_op jit(solution)/shard_map/ppermute | solution.py:51
  41.1 0.9 broadcast_in_dim.7
  42.0 6.8 %all-to-all-start.1 = ((bf16[16,48,384]{2,1,0:T(8,128)(2,1)}), bf16[16,48,384]{2,1,0:T(8,128)(2,1)S(1)}, u32[]{:S(2)}, u32[]{:S(2)}) async-start(bf16[16,48,384]{2,1,0:T(8,128)(2,1)} %broadcast_in_dim.7), calls=%async_computation.1 | async-start | bytes 1179648 | tf_op jit(solution)/shard_map/all_to_all | solution.py:36
  48.8 3.5 %collective-permute-start.3 = (bf16[48,672]{1,0:T(8,128)(2,1)S(1)}, bf16[48,672]{1,0:T(8,128)(2,1)S(1)}, u32[]{:S(2)}, u32[]{:S(2)}) collective-permute-start(bf16[48,672]{1,0:T(8,128)(2,1)S(1)} %slice.49), channel_id=1, source_target_pairs={{0,4},{1,5},{2,6},{3,7},{4,0},{5,1},{6,2},{7,3},{8,12},{9,13},{10,... | collective-permute-start | bytes 193544 | tf_op jit(solution)/shard_map/ppermute | solution.py:51
  52.4 3.5 %collective-permute-start.5 = (bf16[48,96]{1,0:T(8,128)(2,1)S(1)}, bf16[48,96]{1,0:T(8,128)(2,1)S(1)}, u32[]{:S(2)}, u32[]{:S(2)}) collective-permute-start(bf16[48,96]{1,0:T(8,128)(2,1)S(1)} %slice.50), channel_id=1, source_target_pairs={{0,6},{1,7},{2,4},{3,5},{4,2},{5,3},{6,0},{7,1},{8,14},{9,15},{10,... | collective-permute-start | bytes 27656 | tf_op jit(solution)/shard_map/ppermute | solution.py:51
  56.0 2.1 %collective-permute-start.4 = (bf16[48,96]{1,0:T(8,128)(2,1)S(1)}, bf16[48,96]{1,0:T(8,128)(2,1)S(1)}, u32[]{:S(2)}, u32[]{:S(2)}) collective-permute-start(bf16[48,96]{1,0:T(8,128)(2,1)S(1)} %slice.50), channel_id=1, source_target_pairs={{0,2},{1,3},{2,0},{3,1},{4,6},{5,7},{6,4},{7,5},{8,10},{9,11},{10,... | collective-permute-start | bytes 27656 | tf_op jit(solution)/shard_map/ppermute | solution.py:51
  58.9 1.9 %collective-permute-done.4 = bf16[48,96]{1,0:T(8,128)(2,1)S(1)} collective-permute-done((bf16[48,96]{1,0:T(8,128)(2,1)S(1)}, bf16[48,96]{1,0:T(8,128)(2,1)S(1)}, u32[]{:S(2)}, u32[]{:S(2)}) %collective-permute-start.4) | collective-permute-done | bytes 9248 | tf_op jit(solution)/shard_map/ppermute | solution.py:51
  60.9 1.6 %broadcast_in_dim.8 = bf16[16,48,1536]{2,1,0:T(8,128)(2,1)} broadcast(bf16[48,1536]{1,0:T(8,128)(2,1)S(1)} %concatenate.7), dimensions={1,2} | broadcast | bytes 2506752 | tf_op jit(solution)/shard_map/broadcast_in_dim | solution.py:299
  62.6 6.9 %all-to-all-start.2 = ((bf16[16,48,1536]{2,1,0:T(8,128)(2,1)}), bf16[16,48,1536]{2,1,0:T(8,128)(2,1)S(1)}, u32[]{:S(2)}, u32[]{:S(2)}) async-start(bf16[16,48,1536]{2,1,0:T(8,128)(2,1)} %broadcast_in_dim.8), calls=%async_computation.2 | async-start | bytes 4718592 | tf_op jit(solution)/shard_map/all_to_all | solution.py:36
  69.5 2.7 %collective-permute-start.6 = (f32[32,128]{1,0:T(8,128)S(1)}, f32[32,128]{1,0:T(8,128)S(1)}, u32[]{:S(2)}, u32[]{:S(2)}) collective-permute-start(f32[32,128]{1,0:T(8,128)S(1)} %get-tuple-element.57), channel_id=1, source_target_pairs={{0,4},{1,5},{2,6},{3,7},{4,0},{5,1},{6,2},{7,3},{8,12},{9,13},{10,... | collective-permute-start | bytes 49160 | tf_op jit(solution)/shard_map/ppermute | solution.py:51
  72.2 7.6 %collective-permute-start.7 = (f32[32,128]{1,0:T(8,128)S(1)}, f32[32,128]{1,0:T(8,128)S(1)}, u32[]{:S(2)}, u32[]{:S(2)}) collective-permute-start(f32[32,128]{1,0:T(8,128)S(1)} %get-tuple-element.58), channel_id=1, source_target_pairs={{0,5},{1,4},{2,7},{3,6},{4,1},{5,0},{6,3},{7,2},{8,13},{9,12},{10,... | collective-permute-start | bytes 49160 | tf_op jit(solution)/shard_map/ppermute | solution.py:51
  79.8 3.5 %collective-permute-start.8 = (f32[32,128]{1,0:T(8,128)S(1)}, f32[32,128]{1,0:T(8,128)S(1)}, u32[]{:S(2)}, u32[]{:S(2)}) collective-permute-start(f32[32,128]{1,0:T(8,128)S(1)} %get-tuple-element.59), channel_id=1, source_target_pairs={{0,6},{1,7},{2,4},{3,5},{4,2},{5,3},{6,0},{7,1},{8,14},{9,15},{10,... | collective-permute-start | bytes 49160 | tf_op jit(solution)/shard_map/ppermute | solution.py:51
  83.3 2.9 %collective-permute-start.9 = (f32[32,128]{1,0:T(8,128)S(1)}, f32[32,128]{1,0:T(8,128)S(1)}, u32[]{:S(2)}, u32[]{:S(2)}) collective-permute-start(f32[32,128]{1,0:T(8,128)S(1)} %get-tuple-element.60), channel_id=1, source_target_pairs={{0,7},{1,6},{2,5},{3,4},{4,3},{5,2},{6,1},{7,0},{8,15},{9,14},{10,... | collective-permute-start | bytes 49160 | tf_op jit(solution)/shard_map/ppermute | solution.py:51
  86.4 4.0 %collective-permute-done.9.refs_7_ = f32[32,128]{1,0:T(8,128)S(1)} collective-permute-done((f32[32,128]{1,0:T(8,128)S(1)}, f32[32,128]{1,0:T(8,128)S(1)}, u32[]{:S(2)}, u32[]{:S(2)}) %collective-permute-start.9) | collective-permute-done | bytes 16416 | tf_op jit(solution)/shard_map/ppermute | solution.py:51
  90.4 1.9 %collective-permute-start.10 = (bf16[16,64,768]{2,1,0:T(8,128)(2,1)}, bf16[16,64,768]{2,1,0:T(8,128)(2,1)S(1)}, u32[]{:S(2)}, u32[]{:S(2)}) collective-permute-start(bf16[16,64,768]{2,1,0:T(8,128)(2,1)} %all-gather.3.cloned.1.call-done.x_ref), channel_id=1, source_target_pairs={{0,1},{1,0},{2,3},{3,2},{4,5},{5,4},{6,7},{7,6},{8,9},{9,8},{10,11... | collective-permute-start | bytes 4718600 | tf_op jit(solution)/shard_map/ppermute | solution.py:51
  93.0 1.4 %copy-done = bf16[16,64,768]{2,1,0:T(8,128)(2,1)S(1)} copy-done((bf16[16,64,768]{2,1,0:T(8,128)(2,1)S(1)}, bf16[16,64,768]{2,1,0:T(8,128)(2,1)}, u32[]{:S(2)}) %copy-start) | copy-done | bytes 1572888
  94.4 1.4 %shard_map.147 = (bf16[8,128,192]{2,1,0:T(8,128)(2,1)S(1)}, f32[256,192]{1,0:T(8,128)S(1)}) custom-call(bf16[16,64,768]{2,1,0:T(8,128)(2,1)S(1)} %copy-done, f32[768]{0:T(1024)S(1)} %copy-done.3, bf16[16,48,384]{2,1,0:T(8,128)(2,1)S(1)} %all-to-all-done.1.w_ref), custom_call_target="tpu_custom_call" | custom-call | flops 452984832 | bytes 2162688 | tf_op jit(solution)/shard_map/pallas_call | solution.py:209
  96.0 3.6 %shard_map.148 = bf16[8,64,96]{2,1,0:T(8,128)(2,1)S(1)} custom-call(s32[1]{0:T(128)S(6)} %copy.21.length_ref, bf16[16,64,768]{2,1,0:T(8,128)(2,1)S(1)} %collective-permute-done.10.x_ref, f32[768]{0:T(1024)S(1)} %copy-done.3, bf16[16,48,384]{2,1,0:T(8,128)(2,1)S(1)} %all-to-all-done.1.w_ref, bf16[8,128,192]{2,1,0:T(8,128)(2,1)S(1)} %get-tuple-element.63.kv_ref, ...), custom_call_target="tpu_custom_call" | custom-call | flops 452984832 | bytes 2162688 | tf_op jit(solution)/shard_map/pallas_call | solution.py:209
  99.6 6.0 %collective-permute-start.11 = (bf16[16,48,384]{2,1,0:T(8,128)(2,1)S(1)}, bf16[16,48,384]{2,1,0:T(8,128)(2,1)S(1)}, u32[]{:S(2)}, u32[]{:S(2)}) collective-permute-start(bf16[16,48,384]{2,1,0:T(8,128)(2,1)S(1)} %slice.47.w_ref), channel_id=1, source_target_pairs={{0,1},{1,0},{2,3},{3,2},{4,5},{5,4},{6,7},{7,6},{8,9},{9,8},{10,11... | collective-permute-start | bytes 1769480 | tf_op jit(solution)/shard_map/ppermute | solution.py:51
  105.6 9.2 %all_to_all.25.gated_ref = bf16[8,64,96]{2,1,0:T(8,128)(2,1)S(1)} all-to-all(bf16[8,64,96]{2,1,0:T(8,128)(2,1)S(1)} %shard_map.148), channel_id=1, replica_groups=mesh['grp'=16,'pb'=4,'ka'=8] {'ka'}, dimensions={0} | all-to-all | bytes 196608 | tf_op jit(solution)/shard_map/all_to_all | solution.py:36
  115.6 7.0 %all-gather = bf16[256,768]{1,0:T(8,128)(2,1)S(1)} all-gather(bf16[64,768]{1,0:T(8,128)(2,1)S(1)} %get-tuple-element.70), channel_id=2, replica_groups={{0,1,2,3},{4,5,6,7},{8,9,10,11},{12,13,14,15},{16,17,18,19},{20,21,22,2..., dimensions={0}, use_global_device_ids=true | all-gather | bytes 491520 | tf_op jit(solution)/shard_map/all_gather | solution.py:349
  122.5 0.8 shard_map.150
  123.4 9.0 %all_to_all.26.part_ref = bf16[4,64,768]{2,1,0:T(8,128)(2,1)S(1)} all-to-all(bf16[4,64,768]{2,1,0:T(8,128)(2,1)S(1)} %shard_map.150), channel_id=1, replica_groups={{0,1,2,3},{4,5,6,7},{8,9,10,11},{12,13,14,15},{16,17,18,19},{20,21,22,2..., dimensions={0} | all-to-all | bytes 786432 | tf_op jit(solution)/shard_map/all_to_all | solution.py:36
  (40 shorter events, 5.9 us)
Async XLA Ops:
  6.5 83.9 %all-gather.3.cloned.1.call-start = ((), (), s32[]{:S(2)}) async-start(), calls=%async_computation.5 | async-start | bytes 1671168 | tf_op jit(solution)/shard_map/all_gather | solution.py:257
  10.3 30.6 %all-to-all-start = ((bf16[4,12,1056]{2,1,0:T(8,128)(2,1)}), bf16[4,12,1056]{2,1,0:T(8,128)(2,1)S(1)}, u32[]{:S(2)}, u32[]{:S(2)}) async-start(bf16[4,12,1056]{2,1,0:T(8,128)(2,1)} %broadcast_in_dim.6), calls=%async_computation | async-start | bytes 294912 | tf_op jit(solution)/shard_map/all_to_all | solution.py:36
  26.7 1.0 copy-start.1
  27.7 0.7 copy-start.5
  30.1 8.3 %collective-permute-start = (f32[32,128]{1,0:T(8,128)S(1)}, f32[32,128]{1,0:T(8,128)S(1)}, u32[]{:S(2)}, u32[]{:S(2)}) collective-permute-start(f32[32,128]{1,0:T(8,128)S(1)} %get-tuple-element.41), channel_id=1, source_target_pairs={{0,1},{1,0},{2,3},{3,2},{4,5},{5,4},{6,7},{7,6},{8,9},{9,8},{10,11... | collective-permute-start | bytes 49160 | tf_op jit(solution)/shard_map/ppermute | solution.py:51
  33.0 5.5 %collective-permute-start.1 = (f32[32,128]{1,0:T(8,128)S(1)}, f32[32,128]{1,0:T(8,128)S(1)}, u32[]{:S(2)}, u32[]{:S(2)}) collective-permute-start(f32[32,128]{1,0:T(8,128)S(1)} %get-tuple-element.42), channel_id=1, source_target_pairs={{0,2},{1,3},{2,0},{3,1},{4,6},{5,7},{6,4},{7,5},{8,10},{9,11},{10,... | collective-permute-start | bytes 49160 | tf_op jit(solution)/shard_map/ppermute | solution.py:51
  35.6 5.4 %collective-permute-start.2 = (f32[32,128]{1,0:T(8,128)S(1)}, f32[32,128]{1,0:T(8,128)S(1)}, u32[]{:S(2)}, u32[]{:S(2)}) collective-permute-start(f32[32,128]{1,0:T(8,128)S(1)} %get-tuple-element.43), channel_id=1, source_target_pairs={{0,3},{1,2},{2,1},{3,0},{4,7},{5,6},{6,5},{7,4},{8,11},{9,10},{10,... | collective-permute-start | bytes 49160 | tf_op jit(solution)/shard_map/ppermute | solution.py:51
  42.0 18.9 %all-to-all-start.1 = ((bf16[16,48,384]{2,1,0:T(8,128)(2,1)}), bf16[16,48,384]{2,1,0:T(8,128)(2,1)S(1)}, u32[]{:S(2)}, u32[]{:S(2)}) async-start(bf16[16,48,384]{2,1,0:T(8,128)(2,1)} %broadcast_in_dim.7), calls=%async_computation.1 | async-start | bytes 1179648 | tf_op jit(solution)/shard_map/all_to_all | solution.py:36
  48.8 7.2 %collective-permute-start.3 = (bf16[48,672]{1,0:T(8,128)(2,1)S(1)}, bf16[48,672]{1,0:T(8,128)(2,1)S(1)}, u32[]{:S(2)}, u32[]{:S(2)}) collective-permute-start(bf16[48,672]{1,0:T(8,128)(2,1)S(1)} %slice.49), channel_id=1, source_target_pairs={{0,4},{1,5},{2,6},{3,7},{4,0},{5,1},{6,2},{7,3},{8,12},{9,13},{10,... | collective-permute-start | bytes 193544 | tf_op jit(solution)/shard_map/ppermute | solution.py:51
  52.4 6.5 %collective-permute-start.5 = (bf16[48,96]{1,0:T(8,128)(2,1)S(1)}, bf16[48,96]{1,0:T(8,128)(2,1)S(1)}, u32[]{:S(2)}, u32[]{:S(2)}) collective-permute-start(bf16[48,96]{1,0:T(8,128)(2,1)S(1)} %slice.50), channel_id=1, source_target_pairs={{0,6},{1,7},{2,4},{3,5},{4,2},{5,3},{6,0},{7,1},{8,14},{9,15},{10,... | collective-permute-start | bytes 27656 | tf_op jit(solution)/shard_map/ppermute | solution.py:51
  56.0 4.8 %collective-permute-start.4 = (bf16[48,96]{1,0:T(8,128)(2,1)S(1)}, bf16[48,96]{1,0:T(8,128)(2,1)S(1)}, u32[]{:S(2)}, u32[]{:S(2)}) collective-permute-start(bf16[48,96]{1,0:T(8,128)(2,1)S(1)} %slice.50), channel_id=1, source_target_pairs={{0,2},{1,3},{2,0},{3,1},{4,6},{5,7},{6,4},{7,5},{8,10},{9,11},{10,... | collective-permute-start | bytes 27656 | tf_op jit(solution)/shard_map/ppermute | solution.py:51
  62.6 30.4 %copy-start.3 = (f32[768]{0:T(1024)S(1)}, f32[768]{0:T(1024)}, u32[]{:S(2)}) copy-start(f32[768]{0:T(1024)} %gain_ref.6) | copy-start | bytes 9220
  62.6 37.0 %all-to-all-start.2 = ((bf16[16,48,1536]{2,1,0:T(8,128)(2,1)}), bf16[16,48,1536]{2,1,0:T(8,128)(2,1)S(1)}, u32[]{:S(2)}, u32[]{:S(2)}) async-start(bf16[16,48,1536]{2,1,0:T(8,128)(2,1)} %broadcast_in_dim.8), calls=%async_computation.2 | async-start | bytes 4718592 | tf_op jit(solution)/shard_map/all_to_all | solution.py:36
  69.5 16.7 %collective-permute-start.6 = (f32[32,128]{1,0:T(8,128)S(1)}, f32[32,128]{1,0:T(8,128)S(1)}, u32[]{:S(2)}, u32[]{:S(2)}) collective-permute-start(f32[32,128]{1,0:T(8,128)S(1)} %get-tuple-element.57), channel_id=1, source_target_pairs={{0,4},{1,5},{2,6},{3,7},{4,0},{5,1},{6,2},{7,3},{8,12},{9,13},{10,... | collective-permute-start | bytes 49160 | tf_op jit(solution)/shard_map/ppermute | solution.py:51
  72.2 14.0 %collective-permute-start.7 = (f32[32,128]{1,0:T(8,128)S(1)}, f32[32,128]{1,0:T(8,128)S(1)}, u32[]{:S(2)}, u32[]{:S(2)}) collective-permute-start(f32[32,128]{1,0:T(8,128)S(1)} %get-tuple-element.58), channel_id=1, source_target_pairs={{0,5},{1,4},{2,7},{3,6},{4,1},{5,0},{6,3},{7,2},{8,13},{9,12},{10,... | collective-permute-start | bytes 49160 | tf_op jit(solution)/shard_map/ppermute | solution.py:51
  79.8 6.6 %collective-permute-start.8 = (f32[32,128]{1,0:T(8,128)S(1)}, f32[32,128]{1,0:T(8,128)S(1)}, u32[]{:S(2)}, u32[]{:S(2)}) collective-permute-start(f32[32,128]{1,0:T(8,128)S(1)} %get-tuple-element.59), channel_id=1, source_target_pairs={{0,6},{1,7},{2,4},{3,5},{4,2},{5,3},{6,0},{7,1},{8,14},{9,15},{10,... | collective-permute-start | bytes 49160 | tf_op jit(solution)/shard_map/ppermute | solution.py:51
  83.3 7.2 %collective-permute-start.9 = (f32[32,128]{1,0:T(8,128)S(1)}, f32[32,128]{1,0:T(8,128)S(1)}, u32[]{:S(2)}, u32[]{:S(2)}) collective-permute-start(f32[32,128]{1,0:T(8,128)S(1)} %get-tuple-element.60), channel_id=1, source_target_pairs={{0,7},{1,6},{2,5},{3,4},{4,3},{5,2},{6,1},{7,0},{8,15},{9,14},{10,... | collective-permute-start | bytes 49160 | tf_op jit(solution)/shard_map/ppermute | solution.py:51
  90.4 5.5 %collective-permute-start.10 = (bf16[16,64,768]{2,1,0:T(8,128)(2,1)}, bf16[16,64,768]{2,1,0:T(8,128)(2,1)S(1)}, u32[]{:S(2)}, u32[]{:S(2)}) collective-permute-start(bf16[16,64,768]{2,1,0:T(8,128)(2,1)} %all-gather.3.cloned.1.call-done.x_ref), channel_id=1, source_target_pairs={{0,1},{1,0},{2,3},{3,2},{4,5},{5,4},{6,7},{7,6},{8,9},{9,8},{10,11... | collective-permute-start | bytes 4718600 | tf_op jit(solution)/shard_map/ppermute | solution.py:51
  93.0 1.4 %copy-start = (bf16[16,64,768]{2,1,0:T(8,128)(2,1)S(1)}, bf16[16,64,768]{2,1,0:T(8,128)(2,1)}, u32[]{:S(2)}) copy-start(bf16[16,64,768]{2,1,0:T(8,128)(2,1)} %all-gather.3.cloned.1.call-done.x_ref) | copy-start | bytes 4718596
  95.9 18.9 %copy-start.2 = (bf16[1,8,8,768]{3,2,1,0:T(8,128)(2,1)S(1)}, bf16[1,8,8,768]{3,2,1,0:T(8,128)(2,1)}, u32[]{:S(2)}) copy-start(bf16[1,8,8,768]{3,2,1,0:T(8,128)(2,1)} %param.16) | copy-start | bytes 294916
  95.9 18.9 %copy-start.4 = (f32[768]{0:T(1024)S(1)}, f32[768]{0:T(1024)}, u32[]{:S(2)}) copy-start(f32[768]{0:T(1024)} %gain_ref.7) | copy-start | bytes 9220
  99.6 15.2 %collective-permute-start.11 = (bf16[16,48,384]{2,1,0:T(8,128)(2,1)S(1)}, bf16[16,48,384]{2,1,0:T(8,128)(2,1)S(1)}, u32[]{:S(2)}, u32[]{:S(2)}) collective-permute-start(bf16[16,48,384]{2,1,0:T(8,128)(2,1)S(1)} %slice.47.w_ref), channel_id=1, source_target_pairs={{0,1},{1,0},{2,3},{3,2},{4,5},{5,4},{6,7},{7,6},{8,9},{9,8},{10,11... | collective-permute-start | bytes 1769480 | tf_op jit(solution)/shard_map/ppermute | solution.py:51
Sparse Core Ops, SparseCore 0:
  9.4 71.0 all-gather.2

commit v10 on v7

--- a/solution.py
+++ b/solution.py
@@ -305,26 +305,24 @@
     split = 5 * feats
     attn_w = jnp.broadcast_to(early[None, :, :split], (grp_count, pb_count * w_rows, split))
     late = early[:, split:]
-    attn_w, late = lax.optimization_barrier((attn_w, late))
     attn_w = exchange(attn_w, "grp")
 
     late = [late, swap(late, "ka", TP)]
     late = jnp.concatenate([w[:, i * hid : (i + 1) * hid] for i in range(3) for w in late], axis=1)
     late = jnp.broadcast_to(late[None], (grp_count,) + late.shape)
-    late, attn_w, two = lax.optimization_barrier((late, attn_w, two))
-    late = exchange(late, "grp")
     four = swap(call(third_kernel, half)(keep, one, two), "ka", 4)
     bias = call(
         place_kernel, jax.ShapeDtypeStruct((ka_count, keys_held, lanes), f32)
     )(keep, one, two, four)
+    late, attn_w, bias = lax.optimization_barrier((late, attn_w, bias))
+    late = exchange(late, "grp")
 
     out_w = attn_w[:, :, 4 * feats :]
     for flip in (4, 2):
         out_w = jnp.concatenate([out_w, swap(out_w, "ka", flip)], axis=2)
-    x, bias, out_w = lax.optimization_barrier((x, bias, out_w))
+    x, late, out_w = lax.optimization_barrier((x, late, out_w))
     other = swap(x, "ka", 1)
     other_w = swap(out_w, "ka", 1)
-    attn_w, late = lax.optimization_barrier((attn_w, late))
 
     line_rows = pb_count * chips * row_count
     kv_shape = (samples, line_rows, 2 * feats)

time: 158 us -> 146 us (0.924)
  starting transfers between devices: 67.8 us -> 54.9 us
  waiting for transfers between devices: 34.4 us -> 38.9 us
    ppermute x8, waiting for transfers between devices: 13.3 us -> 32.3 us  [swap(): return lax.ppermute(block, axis, [(i, i ^ flip) for i in range(count)])]
    all_to_all x4, waiting for transfers between devices: 20.4 us -> 5.85 us  [exchange(): lax.all_to_all(blocks, axes, split_axis=0, concat_axis=0, tiled=True, axi...]
    ppermute x8, starting transfers between devices: 28.7 us -> 21.5 us  [swap(): return lax.ppermute(block, axis, [(i, i ^ flip) for i in range(count)])]
    all_to_all x4, starting transfers between devices: 39.1 us -> 33.3 us  [exchange(): lax.all_to_all(blocks, axes, split_axis=0, concat_axis=0, tiled=True, axi...]
    unnamed x16 -> x12, local copies, waits for them, and re-layouts: 3.6 us -> 3.12 us
  transfers between devices with their start and end apart: 13 -> 13, of which waited for: 7 -> 6; matrix products, arithmetic and copies ran while one was open for 5% -> 5% of each run, Pallas kernels for 6% -> 5%
where the time goes in v10:
time: 146 us; the launch traced here: 145 us
  starting transfers between devices  54.9 us (38%)
  waiting for transfers between devices  38.9 us (27%)
  blocking collectives  15.9 us (11%)
  between operations  14.3 us (10%)
  Pallas kernels  10.8 us (7%)
  local copies, waits for them, and re-layouts  9.72 us (7%)
    all_to_all x4, starting transfers between devices, exchange(): lax.all_to_all(blocks, axes, split_axis=0, concat_axis=0, tiled=True, axi...  33.3 us
    ppermute x8, waiting for transfers between devices, swap(): return lax.ppermute(block, axis, [(i, i ^ flip) for i in range(count)])  32.3 us
    ppermute x8, starting transfers between devices, swap(): return lax.ppermute(block, axis, [(i, i ^ flip) for i in range(count)])  21.5 us
    pallas_call x9, Pallas kernels, run(): pl.pallas_call(kernel, out_shape=out_shape, in_specs=[pl.BlockSpec(memory...  10.8 us
    all_to_all x1, blocking collectives, exchange(): lax.all_to_all(blocks, axes, split_axis=0, concat_axis=0, tiled=True, axi...  8.96 us
    all_gather x1, blocking collectives, on_device(): lax.all_gather(normed_t, 'ka', axis=0, tiled=False, axis_index_groups=gro...  6.96 us
    all_to_all x4, waiting for transfers between devices, exchange(): lax.all_to_all(blocks, axes, split_axis=0, concat_axis=0, tiled=True, axi...  5.85 us
    unnamed x12, local copies, waits for them, and re-layouts  3.12 us
  transfers between devices with their start and end apart: 13, of which 6 were waited for; matrix products, arithmetic and copies ran while one was open for 5% of the time, Pallas kernels for 5%

profile of v10, /device:TPU:1, one launch (start us, length us, event | category | flops | bytes accessed | tf_op | source)
XLA Modules:
  0.0 145.0 jit_solution(11139564309665089729)
XLA Ops:
  7.3 0.8 constant_dynamic-slice_fusion.2
  8.1 0.8 constant_dynamic-slice_fusion
  8.8 0.8 concatenate.13
  10.4 15.6 %all-to-all-start = ((bf16[4,12,1056]{2,1,0:T(8,128)(2,1)}), bf16[4,12,1056]{2,1,0:T(8,128)(2,1)S(1)}, u32[]{:S(2)}, u32[]{:S(2)}) async-start(bf16[4,12,1056]{2,1,0:T(8,128)(2,1)} %broadcast_in_dim.6), calls=%async_computation | async-start | bytes 294912 | tf_op jit(solution)/shard_map/all_to_all | solution.py:36
  26.7 1.0 copy-done.1
  28.4 1.8 %shard_map.145 = (f32[4,32,128]{2,1,0:T(8,128)S(1)}, f32[4,32,128]{2,1,0:T(8,128)S(1)}) custom-call(bf16[64,32,128]{2,1,0:T(8,128)(2,1)S(1)} %bitcast.13, f32[128]{0:T(128)S(1)} %copy-done.5, f32[16,128]{1,0:T(8,128)S(1)} %bitcast.16), custom_call_target="tpu_custom_call" | custom-call | flops 50331648 | bytes 655360 | tf_op jit(solution)/shard_map/pallas_call | solution.py:227
  30.2 2.9 %collective-permute-start = (f32[4,32,128]{2,1,0:T(8,128)S(1)}, f32[4,32,128]{2,1,0:T(8,128)S(1)}, u32[]{:S(2)}, u32[]{:S(2)}) collective-permute-start(f32[4,32,128]{2,1,0:T(8,128)S(1)} %get-tuple-element.24), channel_id=1, source_target_pairs={{0,1},{1,0},{2,3},{3,2},{4,5},{5,4},{6,7},{7,6},{8,9},{9,8},{10,11... | collective-permute-start | bytes 196616 | tf_op jit(solution)/shard_map/ppermute | solution.py:51
  33.0 0.9 collective-permute-done.one_ref
  33.9 2.6 %collective-permute-start.1 = (f32[4,32,128]{2,1,0:T(8,128)S(1)}, f32[4,32,128]{2,1,0:T(8,128)S(1)}, u32[]{:S(2)}, u32[]{:S(2)}) collective-permute-start(f32[4,32,128]{2,1,0:T(8,128)S(1)} %shard_map.146), channel_id=1, source_target_pairs={{0,2},{1,3},{2,0},{3,1},{4,6},{5,7},{6,4},{7,5},{8,10},{9,11},{10,... | collective-permute-start | bytes 196616 | tf_op jit(solution)/shard_map/ppermute | solution.py:51
  36.6 2.8 %collective-permute-done.1.two_ref = f32[4,32,128]{2,1,0:T(8,128)S(1)} collective-permute-done((f32[4,32,128]{2,1,0:T(8,128)S(1)}, f32[4,32,128]{2,1,0:T(8,128)S(1)}, u32[]{:S(2)}, u32[]{:S(2)}) %collective-permute-start.1) | collective-permute-done | bytes 65568 | tf_op jit(solution)/shard_map/ppermute | solution.py:51
  39.4 1.0 broadcast_in_dim.8
  40.4 6.8 %all-to-all-start.1 = ((bf16[16,48,480]{2,1,0:T(8,128)(2,1)}), bf16[16,48,480]{2,1,0:T(8,128)(2,1)S(1)}, u32[]{:S(2)}, u32[]{:S(2)}) async-start(bf16[16,48,480]{2,1,0:T(8,128)(2,1)} %broadcast_in_dim.8), calls=%async_computation.1 | async-start | bytes 1572864 | tf_op jit(solution)/shard_map/all_to_all | solution.py:36
  47.2 4.5 %collective-permute-start.2 = (bf16[48,576]{1,0:T(8,128)(2,1)S(1)}, bf16[48,576]{1,0:T(8,128)(2,1)S(1)}, u32[]{:S(2)}, u32[]{:S(2)}) collective-permute-start(bf16[48,576]{1,0:T(8,128)(2,1)S(1)} %slice.40), channel_id=1, source_target_pairs={{0,4},{1,5},{2,6},{3,7},{4,0},{5,1},{6,2},{7,3},{8,12},{9,13},{10,... | collective-permute-start | bytes 165896 | tf_op jit(solution)/shard_map/ppermute | solution.py:51
  51.8 1.9 %collective-permute-start.3 = (f32[4,32,128]{2,1,0:T(8,128)S(1)}, f32[4,32,128]{2,1,0:T(8,128)S(1)}, u32[]{:S(2)}, u32[]{:S(2)}) collective-permute-start(f32[4,32,128]{2,1,0:T(8,128)S(1)} %shard_map.147), channel_id=1, source_target_pairs={{0,4},{1,5},{2,6},{3,7},{4,0},{5,1},{6,2},{7,3},{8,12},{9,13},{10,... | collective-permute-start | bytes 196616 | tf_op jit(solution)/shard_map/ppermute | solution.py:51
  53.9 5.5 %collective-permute-done.3.four_ref = f32[4,32,128]{2,1,0:T(8,128)S(1)} collective-permute-done((f32[4,32,128]{2,1,0:T(8,128)S(1)}, f32[4,32,128]{2,1,0:T(8,128)S(1)}, u32[]{:S(2)}, u32[]{:S(2)}) %collective-permute-start.3) | collective-permute-done | bytes 65568 | tf_op jit(solution)/shard_map/ppermute | solution.py:51
  59.4 1.4 broadcast_in_dim.7
  60.8 7.2 %all-to-all-start.2 = ((bf16[16,48,1152]{2,1,0:T(8,128)(2,1)}), bf16[16,48,1152]{2,1,0:T(8,128)(2,1)S(1)}, u32[]{:S(2)}, u32[]{:S(2)}) async-start(bf16[16,48,1152]{2,1,0:T(8,128)(2,1)} %broadcast_in_dim.7), calls=%async_computation.2 | async-start | bytes 3538944 | tf_op jit(solution)/shard_map/all_to_all | solution.py:36
  68.0 1.9 %collective-permute-start.4 = (bf16[16,48,96]{2,1,0:T(8,128)(2,1)S(1)}, bf16[16,48,96]{2,1,0:T(8,128)(2,1)S(1)}, u32[]{:S(2)}, u32[]{:S(2)}) collective-permute-start(bf16[16,48,96]{2,1,0:T(8,128)(2,1)S(1)} %slice.38), channel_id=1, source_target_pairs={{0,4},{1,5},{2,6},{3,7},{4,0},{5,1},{6,2},{7,3},{8,12},{9,13},{10,... | collective-permute-start | bytes 442376 | tf_op jit(solution)/shard_map/ppermute | solution.py:51
  69.9 13.5 %collective-permute-done.4 = bf16[16,48,96]{2,1,0:T(8,128)(2,1)S(1)} collective-permute-done((bf16[16,48,96]{2,1,0:T(8,128)(2,1)S(1)}, bf16[16,48,96]{2,1,0:T(8,128)(2,1)S(1)}, u32[]{:S(2)}, u32[]{:S(2)}) %collective-permute-start.4) | collective-permute-done | bytes 147488 | tf_op jit(solution)/shard_map/ppermute | solution.py:51
  83.6 1.9 %collective-permute-start.5 = (bf16[16,48,192]{2,1,0:T(8,128)(2,1)S(1)}, bf16[16,48,192]{2,1,0:T(8,128)(2,1)S(1)}, u32[]{:S(2)}, u32[]{:S(2)}) collective-permute-start(bf16[16,48,192]{2,1,0:T(8,128)(2,1)S(1)} %pad_maximum_fusion.1), channel_id=1, source_target_pairs={{0,2},{1,3},{2,0},{3,1},{4,6},{5,7},{6,4},{7,5},{8,10},{9,11},{10,... | collective-permute-start | bytes 884744 | tf_op jit(solution)/shard_map/ppermute | solution.py:51
  85.5 9.8 %collective-permute-done.5 = bf16[16,48,192]{2,1,0:T(8,128)(2,1)S(1)} collective-permute-done((bf16[16,48,192]{2,1,0:T(8,128)(2,1)S(1)}, bf16[16,48,192]{2,1,0:T(8,128)(2,1)S(1)}, u32[]{:S(2)}, u32[]{:S(2)}) %collective-permute-start.5) | collective-permute-done | bytes 294944 | tf_op jit(solution)/shard_map/ppermute | solution.py:51
  95.7 3.9 %collective-permute-start.6 = (bf16[16,64,768]{2,1,0:T(8,128)(2,1)}, bf16[16,64,768]{2,1,0:T(8,128)(2,1)S(1)}, u32[]{:S(2)}, u32[]{:S(2)}) collective-permute-start(bf16[16,64,768]{2,1,0:T(8,128)(2,1)} %all-gather.3.cloned.1.call-done.x_ref), channel_id=1, source_target_pairs={{0,1},{1,0},{2,3},{3,2},{4,5},{5,4},{6,7},{7,6},{8,9},{9,8},{10,11... | collective-permute-start | bytes 4718600 | tf_op jit(solution)/shard_map/ppermute | solution.py:51
  99.6 1.9 %collective-permute-start.7 = (bf16[16,48,384]{2,1,0:T(8,128)(2,1)S(1)}, bf16[16,48,384]{2,1,0:T(8,128)(2,1)}, u32[]{:S(2)}, u32[]{:S(2)}) collective-permute-start(bf16[16,48,384]{2,1,0:T(8,128)(2,1)S(1)} %pad_maximum_fusion.w_ref), channel_id=1, source_target_pairs={{0,1},{1,0},{2,3},{3,2},{4,5},{5,4},{6,7},{7,6},{8,9},{9,8},{10,11... | collective-permute-start | bytes 1769480 | tf_op jit(solution)/shard_map/ppermute | solution.py:51
  102.2 1.4 copy-done
  103.6 1.4 shard_map.149
  105.1 4.2 %shard_map.150 = bf16[8,64,96]{2,1,0:T(8,128)(2,1)} custom-call(s32[1]{0:T(128)S(6)} %copy.21.length_ref, bf16[16,64,768]{2,1,0:T(8,128)(2,1)S(1)} %collective-permute-done.6.x_ref, f32[768]{0:T(1024)S(1)} %copy-done.3, bf16[16,48,480]{2,1,0:T(8,128)(2,1)S(1)} %all-to-all-done.1.w_ref, bf16[8,128,192]{2,1,0:T(8,128)(2,1)S(1)} %get-tuple-element.30.kv_ref, ...), custom_call_target="tpu_custom_call" | custom-call | flops 452984832 | bytes 2310144 | tf_op jit(solution)/shard_map/pallas_call | solution.py:227
  109.3 3.8 %all-to-all-start.3 = ((bf16[8,64,96]{2,1,0:T(8,128)(2,1)}), bf16[8,64,96]{2,1,0:T(8,128)(2,1)S(1)}, u32[]{:S(2)}, u32[]{:S(2)}) async-start(bf16[8,64,96]{2,1,0:T(8,128)(2,1)} %shard_map.150), calls=%async_computation.3 | async-start | bytes 262144 | tf_op jit(solution)/shard_map/all_to_all | solution.py:36
  113.1 5.8 %all-to-all-done.3.gated_ref = bf16[8,64,96]{2,1,0:T(8,128)(2,1)S(1)} async-done(((bf16[8,64,96]{2,1,0:T(8,128)(2,1)}), bf16[8,64,96]{2,1,0:T(8,128)(2,1)S(1)}, u32[]{:S(2)}, u32[]{:S(2)}) %all-to-all-start.3) | async-done | bytes 98336 | tf_op jit(solution)/shard_map/all_to_all | solution.py:36
  118.9 1.8 %shard_map.151 = (bf16[64,768]{1,0:T(8,128)(2,1)S(1)}, bf16[64,768]{1,0:T(8,128)(2,1)S(1)}) custom-call(bf16[8,64,96]{2,1,0:T(8,128)(2,1)S(1)} %all-to-all-done.3.gated_ref, bf16[16,48,384]{2,1,0:T(8,128)(2,1)S(1)} %pad_maximum_fusion.w_ref, bf16[16,48,384]{2,1,0:T(8,128)(2,1)} %collective-permute-done.7.other_ref, bf16[64,768]{1,0:T(8,128)(2,1)S(1)} %bitcast.15, ...), custom_call_target="tpu_custom_call" | custom-call | flops 75497472 | bytes 1179648 | tf_op jit(solution)/shard_map/pallas_call | solution.py:227
  120.7 7.0 %all-gather = bf16[256,768]{1,0:T(8,128)(2,1)S(1)} all-gather(bf16[64,768]{1,0:T(8,128)(2,1)S(1)} %get-tuple-element.35), channel_id=2, replica_groups={{0,1,2,3},{4,5,6,7},{8,9,10,11},{12,13,14,15},{16,17,18,19},{20,21,22,2..., dimensions={0}, use_global_device_ids=true | all-gather | bytes 491520 | tf_op jit(solution)/shard_map/all_gather | solution.py:364
  127.7 0.8 shard_map.152
  128.5 9.0 %all_to_all.25.part_ref = bf16[4,64,768]{2,1,0:T(8,128)(2,1)S(1)} all-to-all(bf16[4,64,768]{2,1,0:T(8,128)(2,1)S(1)} %shard_map.152), channel_id=1, replica_groups={{0,1,2,3},{4,5,6,7},{8,9,10,11},{12,13,14,15},{16,17,18,19},{20,21,22,2..., dimensions={0} | all-to-all | bytes 786432 | tf_op jit(solution)/shard_map/all_to_all | solution.py:36
  (34 shorter events, 4.5 us)
Async XLA Ops:
  6.5 89.1 %all-gather.3.cloned.1.call-start = ((), (), s32[]{:S(2)}) async-start(), calls=%async_computation.5 | async-start | bytes 1671168 | tf_op jit(solution)/shard_map/all_gather | solution.py:275
  10.4 28.9 %all-to-all-start = ((bf16[4,12,1056]{2,1,0:T(8,128)(2,1)}), bf16[4,12,1056]{2,1,0:T(8,128)(2,1)S(1)}, u32[]{:S(2)}, u32[]{:S(2)}) async-start(bf16[4,12,1056]{2,1,0:T(8,128)(2,1)} %broadcast_in_dim.6), calls=%async_computation | async-start | bytes 294912 | tf_op jit(solution)/shard_map/all_to_all | solution.py:36
  26.7 1.0 copy-start.1
  27.8 0.7 copy-start.5
  30.2 3.8 %collective-permute-start = (f32[4,32,128]{2,1,0:T(8,128)S(1)}, f32[4,32,128]{2,1,0:T(8,128)S(1)}, u32[]{:S(2)}, u32[]{:S(2)}) collective-permute-start(f32[4,32,128]{2,1,0:T(8,128)S(1)} %get-tuple-element.24), channel_id=1, source_target_pairs={{0,1},{1,0},{2,3},{3,2},{4,5},{5,4},{6,7},{7,6},{8,9},{9,8},{10,11... | collective-permute-start | bytes 196616 | tf_op jit(solution)/shard_map/ppermute | solution.py:51
  33.9 5.4 %collective-permute-start.1 = (f32[4,32,128]{2,1,0:T(8,128)S(1)}, f32[4,32,128]{2,1,0:T(8,128)S(1)}, u32[]{:S(2)}, u32[]{:S(2)}) collective-permute-start(f32[4,32,128]{2,1,0:T(8,128)S(1)} %shard_map.146), channel_id=1, source_target_pairs={{0,2},{1,3},{2,0},{3,1},{4,6},{5,7},{6,4},{7,5},{8,10},{9,11},{10,... | collective-permute-start | bytes 196616 | tf_op jit(solution)/shard_map/ppermute | solution.py:51
  40.4 19.0 %all-to-all-start.1 = ((bf16[16,48,480]{2,1,0:T(8,128)(2,1)}), bf16[16,48,480]{2,1,0:T(8,128)(2,1)S(1)}, u32[]{:S(2)}, u32[]{:S(2)}) async-start(bf16[16,48,480]{2,1,0:T(8,128)(2,1)} %broadcast_in_dim.8), calls=%async_computation.1 | async-start | bytes 1572864 | tf_op jit(solution)/shard_map/all_to_all | solution.py:36
  47.2 6.5 %collective-permute-start.2 = (bf16[48,576]{1,0:T(8,128)(2,1)S(1)}, bf16[48,576]{1,0:T(8,128)(2,1)S(1)}, u32[]{:S(2)}, u32[]{:S(2)}) collective-permute-start(bf16[48,576]{1,0:T(8,128)(2,1)S(1)} %slice.40), channel_id=1, source_target_pairs={{0,4},{1,5},{2,6},{3,7},{4,0},{5,1},{6,2},{7,3},{8,12},{9,13},{10,... | collective-permute-start | bytes 165896 | tf_op jit(solution)/shard_map/ppermute | solution.py:51
  51.8 7.6 %collective-permute-start.3 = (f32[4,32,128]{2,1,0:T(8,128)S(1)}, f32[4,32,128]{2,1,0:T(8,128)S(1)}, u32[]{:S(2)}, u32[]{:S(2)}) collective-permute-start(f32[4,32,128]{2,1,0:T(8,128)S(1)} %shard_map.147), channel_id=1, source_target_pairs={{0,4},{1,5},{2,6},{3,7},{4,0},{5,1},{6,2},{7,3},{8,12},{9,13},{10,... | collective-permute-start | bytes 196616 | tf_op jit(solution)/shard_map/ppermute | solution.py:51
  60.8 34.9 %all-to-all-start.2 = ((bf16[16,48,1152]{2,1,0:T(8,128)(2,1)}), bf16[16,48,1152]{2,1,0:T(8,128)(2,1)S(1)}, u32[]{:S(2)}, u32[]{:S(2)}) async-start(bf16[16,48,1152]{2,1,0:T(8,128)(2,1)} %broadcast_in_dim.7), calls=%async_computation.2 | async-start | bytes 3538944 | tf_op jit(solution)/shard_map/all_to_all | solution.py:36
  68.0 34.2 %copy-start.3 = (f32[768]{0:T(1024)S(1)}, f32[768]{0:T(1024)}, u32[]{:S(2)}) copy-start(f32[768]{0:T(1024)} %gain_ref.6) | copy-start | bytes 9220
  68.0 15.4 %collective-permute-start.4 = (bf16[16,48,96]{2,1,0:T(8,128)(2,1)S(1)}, bf16[16,48,96]{2,1,0:T(8,128)(2,1)S(1)}, u32[]{:S(2)}, u32[]{:S(2)}) collective-permute-start(bf16[16,48,96]{2,1,0:T(8,128)(2,1)S(1)} %slice.38), channel_id=1, source_target_pairs={{0,4},{1,5},{2,6},{3,7},{4,0},{5,1},{6,2},{7,3},{8,12},{9,13},{10,... | collective-permute-start | bytes 442376 | tf_op jit(solution)/shard_map/ppermute | solution.py:51
  83.6 11.7 %collective-permute-start.5 = (bf16[16,48,192]{2,1,0:T(8,128)(2,1)S(1)}, bf16[16,48,192]{2,1,0:T(8,128)(2,1)S(1)}, u32[]{:S(2)}, u32[]{:S(2)}) collective-permute-start(bf16[16,48,192]{2,1,0:T(8,128)(2,1)S(1)} %pad_maximum_fusion.1), channel_id=1, source_target_pairs={{0,2},{1,3},{2,0},{3,1},{4,6},{5,7},{6,4},{7,5},{8,10},{9,11},{10,... | collective-permute-start | bytes 884744 | tf_op jit(solution)/shard_map/ppermute | solution.py:51
  95.7 9.3 %collective-permute-start.6 = (bf16[16,64,768]{2,1,0:T(8,128)(2,1)}, bf16[16,64,768]{2,1,0:T(8,128)(2,1)S(1)}, u32[]{:S(2)}, u32[]{:S(2)}) collective-permute-start(bf16[16,64,768]{2,1,0:T(8,128)(2,1)} %all-gather.3.cloned.1.call-done.x_ref), channel_id=1, source_target_pairs={{0,1},{1,0},{2,3},{3,2},{4,5},{5,4},{6,7},{7,6},{8,9},{9,8},{10,11... | collective-permute-start | bytes 4718600 | tf_op jit(solution)/shard_map/ppermute | solution.py:51
  99.6 13.5 %collective-permute-start.7 = (bf16[16,48,384]{2,1,0:T(8,128)(2,1)S(1)}, bf16[16,48,384]{2,1,0:T(8,128)(2,1)}, u32[]{:S(2)}, u32[]{:S(2)}) collective-permute-start(bf16[16,48,384]{2,1,0:T(8,128)(2,1)S(1)} %pad_maximum_fusion.w_ref), channel_id=1, source_target_pairs={{0,1},{1,0},{2,3},{3,2},{4,5},{5,4},{6,7},{7,6},{8,9},{9,8},{10,11... | collective-permute-start | bytes 1769480 | tf_op jit(solution)/shard_map/ppermute | solution.py:51
  102.2 1.4 copy-start
  105.0 13.9 %copy-start.2 = (bf16[1,8,8,768]{3,2,1,0:T(8,128)(2,1)S(1)}, bf16[1,8,8,768]{3,2,1,0:T(8,128)(2,1)}, u32[]{:S(2)}) copy-start(bf16[1,8,8,768]{3,2,1,0:T(8,128)(2,1)} %param.16) | copy-start | bytes 294916
  105.0 13.9 %copy-start.4 = (f32[768]{0:T(1024)S(1)}, f32[768]{0:T(1024)}, u32[]{:S(2)}) copy-start(f32[768]{0:T(1024)} %gain_ref.7) | copy-start | bytes 9220
  109.3 9.6 %all-to-all-start.3 = ((bf16[8,64,96]{2,1,0:T(8,128)(2,1)}), bf16[8,64,96]{2,1,0:T(8,128)(2,1)S(1)}, u32[]{:S(2)}, u32[]{:S(2)}) async-start(bf16[8,64,96]{2,1,0:T(8,128)(2,1)} %shard_map.150), calls=%async_computation.3 | async-start | bytes 262144 | tf_op jit(solution)/shard_map/all_to_all | solution.py:36
Sparse Core Ops, SparseCore 0:
  9.4 74.3 all-gather.2
